TPU v7x, 32 devices: a whole 2x2x4 slice. The times are simulated.
32 devices in a mesh: groups: 2 (over y), aux: 16 (over z, x, core).
Axes of the slice: x: 2, y: 2, z: 4, core: 2. Of those that a mesh axis runs over, the one named last changes fastest.
Arguments:
- integrals: bfloat16 [8192, 5, 4096], P(('groups', 'aux')), parts along dimension 0, may hold values from -8 to 8
- block_list: int32 [32, 5], P(('groups', 'aux')), parts along dimension 0, may hold values from 0 to 255
- slot_counts: int32 [32], P(('groups', 'aux')), parts along dimension 0, may hold values from 1 to 5, as said below
- coefficients: bfloat16 [32768, 16], P(('groups', 'aux')), parts along dimension 0, may hold values from -0.3125 to 0.3125
- batch_index: int32 [32], P('groups'), parts along dimension 0, may hold values from 0 to 1023
- occ_energy: float32 [2048], P('groups'), parts along dimension 0, may hold values from -2 to -0.3
- vir_energy: float32 [128], P('groups'), parts along dimension 0, may hold values from 0.2 to 3
- owner_map: int32 [32], P('groups'), parts along dimension 0, may hold values from 0 to 15, as said below
Outputs:
- grad_coef: float32 [32768, 16], P(('groups', 'aux')), parts along dimension 0
- pair_energy: float32 [64], P(('groups', 'aux')), parts along dimension 0
There are 2 independent parts, one for each index of `groups`. A program takes and returns all parts, laid end to end along the dimension named above; each array names one. Nothing has to cross between parts.
Inputs may be any that keep to these rules, and one draw needn't show every extreme that they name: `slot_counts`: some shard uses all 5 slots. `owner_map`: each device owns at most 2 batch orbitals, and some device owns 2.
All inputs are finite; a program needn't handle non-finite values.
Results may differ from a plain program's by a relative error of at most 0.0007.
Values may be sent and summed in bfloat16 or wider, within the bound.
No kernel may reach another device: no remote copies, remote signals or barrier semaphores. Data moves between devices by JAX's collectives and lax.ppermute only.
A program may use at most 128 MiB of HBM per device.

v0:
```python
import jax
import jax.numpy as jnp
from jax import lax
from jax.sharding import PartitionSpec as P

BW = 64
S = 5
CAP = 2


def slot_table(owner_map, cap_slots):
    orbitals = owner_map.shape[0]
    same_owner = owner_map[:, None] == owner_map[None, :]
    earlier = jnp.arange(orbitals)[None, :] < jnp.arange(orbitals)[:, None]
    owner_rank = jnp.sum((same_owner & earlier).astype(jnp.int32), axis=1)
    return owner_map * cap_slots + owner_rank


def body(
    integrals, block_list, slot_counts, coefficients, batch_index, occ_energy, vir_energy, owner_map
):
    shard_count = lax.axis_size("aux")
    own_index = lax.axis_index("aux")
    local_q = integrals.shape[0]
    orbitals = owner_map.shape[0]
    fit_scale = 0.125 / (local_q * shard_count)
    slabs = integrals.reshape(local_q, S, BW, BW)
    whole_coef = lax.all_gather(coefficients, "aux", axis=0, tiled=True)
    usable = (jnp.arange(S) < slot_counts[0]).astype(jnp.bfloat16)
    row_ids = block_list[0][:, None] * BW + jnp.arange(BW)[None, :]
    picked = (
        jnp.take(whole_coef, row_ids.reshape(-1), axis=0).reshape(S, BW, orbitals)
        * usable[:, None, None]
    )
    halfway = jnp.einsum("qsma,smi->qia", slabs, picked, preferred_element_type=jnp.float32).astype(
        jnp.bfloat16
    )
    occ_levels = jnp.take(occ_energy, batch_index)
    denominators = (
        2.0 * occ_levels[:, None, None] - vir_energy[None, :, None] - vir_energy[None, None, :]
    )
    slot_ids = slot_table(owner_map, CAP)
    flat_slots = shard_count * CAP
    matches = slot_ids[None, :] == jnp.arange(flat_slots)[:, None]
    slot_orbital = jnp.sum(jnp.where(matches, jnp.arange(orbitals)[None, :], 0), axis=1)
    slot_filled = jnp.any(matches, axis=1)
    my_orbitals = lax.dynamic_slice_in_dim(slot_orbital, own_index * CAP, CAP)
    my_filled = lax.dynamic_slice_in_dim(slot_filled, own_index * CAP, CAP).astype(jnp.float32)
    outgoing = (
        jnp.take(halfway, slot_orbital, axis=1) * slot_filled.astype(jnp.bfloat16)[None, :, None]
    )
    outgoing = outgoing.reshape(local_q, flat_slots * BW)
    incoming = lax.all_to_all(outgoing, "aux", split_axis=1, concat_axis=0, tiled=True)
    incoming = incoming.reshape(local_q * shard_count, CAP, BW)
    pair_ints = fit_scale * jnp.einsum(
        "qca,qcb->cab", incoming, incoming, preferred_element_type=jnp.float32
    )
    my_denoms = jnp.take(denominators, my_orbitals, axis=0)
    my_amps = pair_ints / my_denoms
    pair_energy = jnp.sum(pair_ints * my_amps, axis=(1, 2)) * my_filled
    sent_amps = my_amps.astype(jnp.bfloat16).reshape(CAP, BW * BW)
    every_amp = lax.all_gather(sent_amps, "aux", axis=0, tiled=True)
    amps_half = jnp.take(every_amp, slot_ids, axis=0).reshape(orbitals, BW, BW)
    weights = (
        0.5
        / BW
        * jnp.einsum("qia,iab->qib", halfway, amps_half, preferred_element_type=jnp.float32)
    )
    weights = weights.astype(jnp.bfloat16)
    slot_terms = jnp.einsum("qsmn,qin->smi", slabs, weights, preferred_element_type=jnp.float32)
    slot_terms = slot_terms * usable.astype(jnp.float32)[:, None, None]
    local_rows = coefficients.shape[0]
    block_ids = jnp.arange(local_rows * lax.axis_size("aux") // BW)
    block_hits = (block_ids[:, None] == block_list[0][None, :]).astype(jnp.float32)
    placed = jnp.einsum("rs,smi->rmi", block_hits, slot_terms, precision=lax.Precision.HIGHEST)
    grad_coef = lax.psum_scatter(
        placed.reshape(local_rows * lax.axis_size("aux"), orbitals),
        "aux",
        scatter_dimension=0,
        tiled=True,
    )
    return (grad_coef, pair_energy)


def solution(mesh):
    return jax.shard_map(
        body,
        mesh=mesh,
        in_specs=(
            P(("groups", "aux"), None, None),
            P(("groups", "aux"), None),
            P(("groups", "aux")),
            P(("groups", "aux"), None),
            P("groups"),
            P("groups"),
            P("groups"),
            P("groups"),
        ),
        out_specs=(P(("groups", "aux"), None), P(("groups", "aux"))),
        check_vma=False,
    )
```

profile of v0, /device:TPU:0, one launch (start us, length us, event | category | flops | bytes accessed | tf_op | source)
XLA Modules:
  0.0 229.6 jit_solution(596828440116151364)
XLA Ops:
  7.2 0.9 convert_reduce_fusion
  8.1 0.7 compare_and_fusion.3
  8.9 0.7 broadcast_multiply_fusion
  10.7 0.1 mul.77
  11.1 0.9 copy.46
  12.0 53.9 %all_gather.6 = bf16[16384,16]{1,0:T(8,128)(2,1)} all-gather(bf16[1024,16]{1,0:T(8,128)(2,1)S(1)} %copy.46), channel_id=1, replica_groups=mesh['groups'=2,'aux'=16] {'aux'}, dimensions={0}, use_global_device_ids=true | all-gather | bytes 557056 | tf_op jit(solution)/shard_map/all_gather | solution.py:28
  65.9 3.9 %gather_fusion = bf16[320,16]{1,0:T(8,128)(2,1)S(1)} fusion(bf16[16384,16]{1,0:T(8,128)(2,1)} %all_gather.6, s32[1024]{0:T(1024)S(1)} %pad_clamp_fusion.4), kind=kCustom, calls=%fused_computation | custom fusion | bytes 21760 | tf_op jit(solution)/shard_map/jit(_take)/gather | solution.py:32
  69.9 14.2 %copy.48 = bf16[256,5,4096]{0,2,1:T(8,128)(2,1)} copy(bf16[256,5,4096]{2,0,1:T(8,128)(2,1)} %param.8) | data formatting | bytes 20971520 | tf_op args[0]
  84.1 9.5 %fusion.12 = bf16[256,16,64]{0,1,2:T(8,128)(2,1)S(1)} fusion(bf16[256,5,64,64]{0,3,2,1:T(8,128)(2,1)} %bitcast.49, bf16[5,64,16]{1,2,0:T(8,128)(2,1)S(1)} %copy.47, pred[5,64]{1,0:T(8,128)(4,1)S(1)} %compare_and_fusion.1, bf16[5]{0:T(256)(128)(2,1)S(1)} %get-tuple-element.8), kind=kOutput, calls=%fused_computation.14 | convolution fusion | flops 168059904 | bytes 11020618 | tf_op jit(solution)/shard_map/qsma,smi->qia/dot_general | solution.py:35
  93.7 0.2 copy.50
  93.8 0.6 gather_fusion.1
  94.5 1.5 select_multiply_fusion
  96.0 8.5 %all-to-all-start = ((bf16[256,16,128]{0,2,1:T(8,128)(2,1)}), bf16[256,16,128]{0,2,1:T(8,128)(2,1)S(1)}, u32[]{:S(2)}, u32[]{:S(2)}) async-start(bf16[256,16,128]{0,2,1:T(8,128)(2,1)} %select_multiply_fusion), calls=%async_computation | async-start | bytes 2097152 | tf_op jit(solution)/shard_map/all_to_all | solution.py:53
  104.6 0.6 gather_fusion.2
  105.4 0.2 broadcast_subtract_fusion
  105.6 0.6 gather_fusion.3
  106.2 21.2 %all-to-all-done = bf16[256,16,128]{0,2,1:T(8,128)(2,1)S(1)} async-done(((bf16[256,16,128]{0,2,1:T(8,128)(2,1)}), bf16[256,16,128]{0,2,1:T(8,128)(2,1)S(1)}, u32[]{:S(2)}, u32[]{:S(2)}) %all-to-all-start) | async-done | bytes 1048608 | tf_op jit(solution)/shard_map/all_to_all | solution.py:53
  127.4 0.6 copy.51
  128.0 0.5 reshape.188
  128.6 0.5 multiply_reduce_fusion
  129.1 0.1 reshape.235
  129.2 23.5 %all-gather = bf16[16,2,4096]{2,1,0:T(2,128)(2,1)S(1)} all-gather(bf16[1,2,4096]{2,1,0:T(2,128)(2,1)S(1)} %reshape.235), channel_id=1, replica_groups=mesh['groups'=2,'aux'=16] {'aux'}, dimensions={0}, use_global_device_ids=true | all-gather | bytes 278528 | tf_op jit(solution)/shard_map/all_gather | solution.py:62
  152.7 0.1 reshape.236
  152.8 0.6 gather_fusion.4
  153.4 0.2 gather.33
  153.6 0.2 copy.52
  153.8 0.4 fusion.11
  154.2 10.9 %fusion.21 = f32[5,64,16]{1,2,0:T(8,128)S(1)} fusion(bf16[256,5,64,64]{0,3,2,1:T(8,128)(2,1)} %bitcast.50, bf16[256,16,64]{0,2,1:T(8,128)(2,1)S(1)} %fusion.11, f32[5]{0:T(128)S(1)} %get-tuple-element.9), kind=kOutput, calls=%fused_computation.18 | convolution fusion | flops 167777280 | bytes 11030548 | tf_op jit(solution)/shard_map/qsmn,qin->smi/dot_general | solution.py:70
  165.1 1.1 fusion.29
  166.2 1.6 reshape.190
  167.9 0.6 dynamic-slice_select_fusion
  168.5 54.2 %reduce-scatter.2.cloned.1.call-done = f32[1024,16]{0,1:T(8,128)} async-done(((f32[16384,16]{0,1:T(8,128)}), f32[1024,16]{0,1:T(8,128)}) %reduce-scatter.2.cloned.1.call-update) | async-done | bytes 65552 | tf_op jit(solution)/shard_map/reduce_scatter | solution.py:76
  (36 shorter events, 1.2 us)
Async XLA Ops:
  7.2 97.4 %copy-start = (f32[1024]{0:T(1024)S(1)}, f32[1024]{0:T(1024)}, u32[]{:S(2)}) copy-start(f32[1024]{0:T(1024)} %param.13) | copy-start | bytes 12292
  84.1 20.4 %copy-start.3 = (s32[16]{0:T(128)S(1)}, s32[16]{0:T(128)}, u32[]{:S(2)}) copy-start(s32[16]{0:T(128)} %param.12) | copy-start | bytes 196
  84.1 21.2 %copy-start.1 = (f32[64]{0:T(128)S(1)}, f32[64]{0:T(128)}, u32[]{:S(2)}) copy-start(f32[64]{0:T(128)} %param.14) | copy-start | bytes 772
  96.0 31.4 %all-to-all-start = ((bf16[256,16,128]{0,2,1:T(8,128)(2,1)}), bf16[256,16,128]{0,2,1:T(8,128)(2,1)S(1)}, u32[]{:S(2)}, u32[]{:S(2)}) async-start(bf16[256,16,128]{0,2,1:T(8,128)(2,1)} %select_multiply_fusion), calls=%async_computation | async-start | bytes 2097152 | tf_op jit(solution)/shard_map/all_to_all | solution.py:53
  104.5 118.2 %reduce-scatter.2.cloned.1.call-start = ((), (), s32[]{:S(2)}) async-start(), calls=%async_computation.2 | async-start | bytes 1114112 | tf_op jit(solution)/shard_map/reduce_scatter | solution.py:76
  128.0 37.1 %copy-start.2 = (s32[1,5]{1,0:T(1,128)S(1)}, s32[1,5]{1,0:T(1,128)}, u32[]{:S(2)}) copy-start(s32[1,5]{1,0:T(1,128)} %param.9) | copy-start | bytes 64
Sparse Core Ops, SparseCore 0:
  168.0 54.6 reduce-scatter.1
where the time goes:
time: 230 us
  blocking collectives  77.4 us (34%)
  waiting for transfers between devices  75.4 us (33%)
  local copies, waits for them, and re-layouts  25.7 us (11%)
  matrix products  22.5 us (10%)
  between operations  14.9 us (6%)
  starting transfers between devices  8.53 us (4%)
  other arithmetic  5.11 us (2%)
    reduce_scatter x1, waiting for transfers between devices, body(): lax.psum_scatter(placed.reshape(local_rows * lax.axis_size('aux'), orbita...  54.2 us
    all_gather x1, blocking collectives, body(): whole_coef = lax.all_gather(coefficients, 'aux', axis=0, tiled=True)  53.9 us
    all_gather x1, blocking collectives, body(): every_amp = lax.all_gather(sent_amps, 'aux', axis=0, tiled=True)  23.5 us
    all_to_all x1, waiting for transfers between devices, body(): lax.all_to_all(outgoing, 'aux', split_axis=1, concat_axis=0, tiled=True)  21.2 us
    unnamed x12, local copies, waits for them, and re-layouts  15.4 us
    dot_general x1, matrix products, body(): jnp.einsum('qsmn,qin->smi', slabs, weights, preferred_element_type=jnp.fl...  10.9 us
    dot_general x1, matrix products, body(): jnp.einsum('qsma,smi->qia', slabs, picked, preferred_element_type=jnp.flo...  9.55 us
    all_to_all x1, starting transfers between devices, body(): lax.all_to_all(outgoing, 'aux', split_axis=1, concat_axis=0, tiled=True)  8.49 us
  transfers between devices with their start and end apart: 2, of which 2 were waited for; matrix products, arithmetic and copies ran while one was open for 1% of the time, Pallas kernels for 0%

commit v1 on v0

v1 whole, which is shorter than its diff:
```python
import functools

import jax
import jax.numpy as jnp
from jax import lax
from jax.experimental import pallas as pl
from jax.experimental.pallas import tpu as pltpu
from jax.sharding import PartitionSpec as P

BW = 64
S = 5
CAP = 2
LANES = 128
HALVES = LANES // BW
TILES = BW * BW // LANES
ROWS = S * TILES
PARTS = 4
F32 = jnp.float32
BF16 = jnp.bfloat16
VMEM = pl.BlockSpec(memory_space=pltpu.VMEM)
SMEM = pl.BlockSpec(memory_space=pltpu.SMEM)


def iota(shape, dim):
    return lax.broadcasted_iota(jnp.int32, shape, dim)


def retile_kernel(part, x, out):
    count = out.shape[0]

    def step(g, carry):
        dst = pl.multiple_of(g * 16, 16)
        src = pl.multiple_of(part * count + g * 16, 16)
        for s in range(S):
            rows = x[s, pl.ds(src, 16), :].reshape(16, TILES, LANES)
            out[pl.ds(dst, 16), s * TILES : (s + 1) * TILES, :] = rows
        return carry

    lax.fori_loop(0, count // 16, step, 0)


def retile(x, part):
    q = x.shape[1] // PARTS
    return pl.pallas_call(
        functools.partial(retile_kernel, part),
        in_specs=[VMEM],
        out_specs=VMEM,
        out_shape=jax.ShapeDtypeStruct((q, ROWS, LANES), BF16),
        compiler_params=pltpu.CompilerParams(vmem_limit_bytes=28 * 2**20),
        cost_estimate=pl.CostEstimate(flops=0, bytes_accessed=4 * q * ROWS * LANES, transcendentals=0),
    )(x)


def gather_index(dev, me, masks):
    rel = lax.bitwise_xor(dev, me)
    place = 0
    for k, mask in enumerate(masks):
        place = place + jnp.where(lax.bitwise_and(rel, mask) != 0, 1 << k, 0)
    return place


def half_kernel(masks, blocks, counts, coef_a, coef_b, *refs):
    slabs, (half, keep, send, scr) = refs[:PARTS], refs[PARTS:]
    me = lax.axis_index("aux")
    orbs, width = coef_a.shape[1], coef_a.shape[2]
    per_dev = width // BW
    near = coef_a.shape[0]
    picked, perm = [], [[], []]
    src = iota((LANES, ROWS), 0)
    dst = iota((LANES, ROWS), 1)
    for s in range(S):
        block = blocks[0, s]
        dev = lax.div(block, per_dev)
        inner = lax.rem(block, per_dev)
        place = gather_index(dev, me, masks)
        col = pl.multiple_of(lax.div(inner, HALVES) * LANES, LANES)
        spot = lax.rem(place, near)
        ours = coef_a[spot, :, pl.ds(col, LANES)]
        theirs = coef_b[spot, :, pl.ds(col, LANES)]
        picked.append(jnp.where(place < near, ours, theirs))
        base = lax.rem(inner, HALVES) * BW
        used = jnp.where(s < counts[0], 1, 0)
        for h in range(HALVES):
            tile = dst - s * TILES
            hit = (src == base + HALVES * tile + h) & (tile >= 0) & (tile < TILES) & (used > 0)
            perm[h].append(jnp.where(hit, 1.0, 0.0).astype(BF16))
    picked = jnp.concatenate(picked, axis=1)
    coef = jnp.concatenate(
        [jnp.dot(picked, jnp.concatenate(perm[h], axis=0), preferred_element_type=F32) for h in range(HALVES)],
        axis=0,
    ).astype(BF16)
    low = iota((orbs, LANES), 1) < BW
    pairs = half.shape[1]
    for part in range(PARTS):
        slab = slabs[part]
        for p in range(slab.shape[0] // 2):
            both = jnp.concatenate([slab[2 * p], slab[2 * p + 1]], axis=1)
            r = jnp.dot(coef, both, preferred_element_type=F32)
            straight = jnp.where(low, r[:orbs, :LANES], r[orbs:, LANES:])
            crossed = jnp.where(low, r[:orbs, LANES:], r[orbs:, :LANES])
            row = straight + pltpu.roll(crossed, BW, 1)
            at = part * (slab.shape[0] // 2) + p
            for g in range(orbs // 8):
                scr[pl.ds(g * 8 * pairs + at, 8, stride=pairs), :] = row[g * 8 : g * 8 + 8]
    scale = 0.125 / (2 * pairs * lax.axis_size("aux"))
    lane = iota((BW, LANES), 1)
    left = lane < BW
    upper = iota((BW, LANES), 0) <= lax.rem(lane, BW)
    eye = iota((BW, LANES), 0) == lax.rem(lane, BW)

    def square(i):
        h = scr[i * pairs : (i + 1) * pairs, :].astype(BF16)
        half[i] = h
        t = lax.dot_general(h, h, (((0,), (0,)), ((), ())), preferred_element_type=F32) * scale
        return t[:BW], t[BW:]

    quads = orbs // 8
    cores = []
    for core in range(2):
        tiles, diags = [], []
        for k in range(quads):
            first = core * (orbs // 2) + 4 * k
            t = [square(first + j) for j in range(4)]
            lefts = [t[j][0] + pltpu.roll(t[j][1], BW, 1) for j in (0, 1)]
            rights = [pltpu.roll(t[j][0], BW, 1) + t[j][1] for j in (2, 3)]
            a = jnp.where(left, lefts[0], rights[0])
            b = jnp.where(left, lefts[1], rights[1])
            tiles.append(jnp.where(upper, a, b))
            diags.append(jnp.sum(jnp.where(eye, b, 0.0), axis=0, keepdims=True))
        spare = keep.shape[0] - quads * BW - quads
        if spare:
            diags.append(jnp.zeros((spare, LANES), F32))
        cores.append((tiles, jnp.concatenate(diags, axis=0)))
    own = lax.rem(me, 2) == 0
    for k in range(quads):
        keep[k * BW : (k + 1) * BW, :] = jnp.where(own, cores[0][0][k], cores[1][0][k])
        send[k * BW : (k + 1) * BW, :] = jnp.where(own, cores[1][0][k], cores[0][0][k])
    keep[quads * BW :, :] = jnp.where(own, cores[0][1], cores[1][1])
    send[quads * BW :, :] = jnp.where(own, cores[1][1], cores[0][1])


def half_transform(masks, block_list, slot_counts, coef_a, coef_b, slabs):
    orbs = coef_a.shape[1]
    pairs = sum(s.shape[0] for s in slabs) // 2
    quads = orbs // 8
    rows = quads * BW + -(-quads // 8) * 8
    packed = jax.ShapeDtypeStruct((rows, LANES), F32)
    return pl.pallas_call(
        functools.partial(half_kernel, masks),
        in_specs=[SMEM, SMEM, VMEM, VMEM] + [VMEM] * PARTS,
        out_specs=[VMEM] * 3,
        out_shape=[jax.ShapeDtypeStruct((orbs, pairs, LANES), BF16), packed, packed],
        scratch_shapes=[pltpu.VMEM((orbs * pairs, LANES), F32)],
        compiler_params=pltpu.CompilerParams(vmem_limit_bytes=44 * 2**20),
    )(block_list, slot_counts, coef_a, coef_b, *slabs)


def level_kernel(index, levels, out):
    lane = iota((1, LANES), 1)

    def step(i, carry):
        at = index[i]
        row = levels[pl.ds(lax.div(at, LANES), 1), :]
        value = jnp.sum(jnp.where(lane == lax.rem(at, LANES), row, 0.0), axis=1, keepdims=True)
        out[pl.ds(i, 1), :] = jnp.broadcast_to(2.0 * value, (1, LANES))
        return carry

    lax.fori_loop(0, out.shape[0], step, 0)


def level_rows(batch_index, occ_energy):
    return pl.pallas_call(
        level_kernel,
        in_specs=[SMEM, VMEM],
        out_specs=VMEM,
        out_shape=jax.ShapeDtypeStruct((batch_index.shape[0], LANES), F32),
    )(batch_index, occ_energy.reshape(-1, LANES))


def grad_kernel(blocks, counts, mine, other, levels, vir, half, *refs):
    slabs, (terms, energy, scr) = refs[:PARTS], refs[PARTS:]
    me = lax.axis_index("aux")
    orbs, pairs = half.shape[0], half.shape[1]
    quads = orbs // 8
    lane = iota((BW, LANES), 1)
    row = iota((BW, LANES), 0)
    left = lane < BW
    inner = lax.rem(lane, BW)
    vir_b = jnp.concatenate([vir[...], vir[...]], axis=1)
    vir_a = jnp.sum(jnp.where((row == inner) & left, vir_b, 0.0), axis=1, keepdims=True)
    even = lax.rem(me, 2) == 0
    zero = jnp.zeros((BW, LANES), F32)
    scale = 0.5 / BW
    for core in range(2):
        ours = even if core == 0 else jnp.logical_not(even)

        def packed(start, size, ours=ours):
            return jnp.where(ours, mine[start : start + size, :], other[start : start + size, :])

        for k in range(0, quads, 2):
            squares = [packed((k + j) * BW, BW) for j in range(2)]
            turned = jnp.concatenate(squares, axis=0).T
            top, bottom = turned[:BW], turned[BW:]
            flips = [
                jnp.where(left, top, pltpu.roll(bottom, BW, 1)),
                jnp.where(left, pltpu.roll(top, BW, 1), bottom),
            ]
            for j in range(2):
                first = core * (orbs // 2) + 4 * (k + j)
                diag = packed(quads * BW + k + j, 1)
                ints = [
                    jnp.where(row <= inner, squares[j], flips[j]),
                    jnp.where(row == inner, diag, jnp.where(row > inner, squares[j], flips[j])),
                ]
                for b in range(2):
                    one, two = first + b, first + 2 + b
                    level = jnp.where(left, levels[one : one + 1, :], levels[two : two + 1, :])
                    amps = ints[b] / ((level - vir_a) - vir_b)
                    sums = jnp.sum(ints[b] * amps, axis=0, keepdims=True)
                    energy[one : one + 1, :] = jnp.where(left[:1], sums, 0.0)
                    energy[two : two + 1, :] = jnp.where(left[:1], 0.0, sums)
                    turn = pltpu.roll(amps, BW, 1)
                    for i, lows, highs in ((one, amps, turn), (two, turn, amps)):
                        square = jnp.concatenate([jnp.where(left, lows, zero), jnp.where(left, zero, highs)], axis=0)
                        w = jnp.dot(half[i], square.astype(BF16), preferred_element_type=F32) * scale
                        scr[i * pairs : (i + 1) * pairs, :] = w.astype(BF16).astype(F32)
    low = iota((orbs, LANES), 1) < BW
    blank = jnp.zeros((orbs, LANES), F32)
    total = jnp.zeros((ROWS, HALVES * orbs), F32)
    for part in range(PARTS):
        slab = slabs[part]
        xs, ws = [], []
        for p in range(slab.shape[0] // 2):
            at = part * (slab.shape[0] // 2) + p
            w = jnp.concatenate(
                [scr[pl.ds(g * 8 * pairs + at, 8, stride=pairs), :] for g in range(orbs // 8)], axis=0
            )
            turn = pltpu.roll(w, BW, 1)
            ws.append(jnp.concatenate([jnp.where(low, w, blank), jnp.where(low, blank, turn)], axis=0).astype(BF16))
            ws.append(jnp.concatenate([jnp.where(low, turn, blank), jnp.where(low, blank, w)], axis=0).astype(BF16))
            xs += [slab[2 * p], slab[2 * p + 1]]
        total = total + lax.dot_general(
            jnp.concatenate(xs, axis=1),
            jnp.concatenate(ws, axis=1),
            (((1,), (1,)), ((), ())),
            preferred_element_type=F32,
        )
    flat = total.T
    width = terms.shape[1]
    src = iota((ROWS, width), 0)
    dst = iota((ROWS, width), 1)
    out = jnp.zeros((orbs, width), F32)
    for h in range(HALVES):
        spread = jnp.where(dst == lax.div(src, TILES) * BW + lax.rem(src, TILES) * HALVES + h, 1.0, 0.0)
        out = out + lax.dot_general(
            flat[h * orbs : (h + 1) * orbs],
            spread,
            (((1,), (0,)), ((), ())),
            precision=lax.Precision.HIGHEST,
            preferred_element_type=F32,
        )
    place = iota((orbs, width), 1) - S * BW
    for s in range(S):
        out = jnp.where(place == s, jnp.where(s < counts[0], blocks[0, s], -1).astype(F32), out)
    terms[...] = out


def gradient_terms(block_list, slot_counts, mine, other, levels, vir_energy, half, slabs):
    orbs, pairs = half.shape[0], half.shape[1]
    width = -(-(S * BW + S) // LANES) * LANES
    return pl.pallas_call(
        grad_kernel,
        in_specs=[SMEM, SMEM] + [VMEM] * 5 + [VMEM] * PARTS,
        out_specs=[VMEM] * 2,
        out_shape=[jax.ShapeDtypeStruct((orbs, width), F32), jax.ShapeDtypeStruct((orbs, LANES), F32)],
        scratch_shapes=[pltpu.VMEM((orbs * pairs, LANES), F32)],
        compiler_params=pltpu.CompilerParams(vmem_limit_bytes=44 * 2**20),
    )(block_list, slot_counts, mine, other, levels, vir_energy.reshape(1, -1), half, *slabs)


def place_kernel(near, far, out):
    me = lax.axis_index("aux")
    orbs, width = out.shape
    per_dev = width // BW
    lane = iota((orbs, LANES), 1)
    side = jnp.where(lane < BW, 0, 1)
    tiles = S * BW // LANES + 1
    for t in range(width // LANES):
        out[:, t * LANES : (t + 1) * LANES] = jnp.zeros((orbs, LANES), F32)

    def take(ref, d):
        ids = ref[d, :, (tiles - 1) * LANES : tiles * LANES]
        start = S * BW - (tiles - 1) * LANES
        ids = [ids[:, start + s : start + s + 1].astype(jnp.int32) - me * per_dev for s in range(S)]
        none = jnp.full_like(ids[0], -1)
        ids = ids + [none] * (2 * tiles - S)
        for k in range(tiles):
            value = ref[d, :, k * LANES : (k + 1) * LANES]
            one, two = ids[2 * k], ids[2 * k + 1]
            spot = jnp.where(side == 0, one, two)
            turn = pltpu.roll(value, BW, 1)
            turn_spot = jnp.where(side == 0, two, one)
            for t in range(width // LANES):
                here = HALVES * t + side
                cols = slice(t * LANES, (t + 1) * LANES)
                out[:, cols] += jnp.where(spot == here, value, 0.0) + jnp.where(turn_spot == here, turn, 0.0)

    def step(d, carry):
        take(near, d)
        take(far, d)
        return carry

    lax.fori_loop(0, near.shape[0], step, 0)


def place_terms(near, far, rows):
    return pl.pallas_call(
        place_kernel,
        in_specs=[VMEM, VMEM],
        out_specs=VMEM,
        out_shape=jax.ShapeDtypeStruct((near.shape[1], rows), F32),
        compiler_params=pltpu.CompilerParams(vmem_limit_bytes=44 * 2**20),
    )(near, far)


def swap(x, mask):
    size = lax.axis_size("aux")
    return lax.ppermute(x, "aux", [(i, i ^ mask) for i in range(size)])


def body(
    integrals, block_list, slot_counts, coefficients, batch_index, occ_energy, vir_energy, owner_map
):
    size = lax.axis_size("aux")
    me = lax.axis_index("aux")
    local_rows = coefficients.shape[0]
    masks = []
    while size >> (len(masks) + 1):
        masks.append(size >> (len(masks) + 1))
    x = jnp.transpose(integrals, (1, 0, 2))
    buf = coefficients.T[None]
    slabs = []
    for k, mask in enumerate(masks):
        far = swap(buf, mask)
        if k < PARTS:
            slabs.append(retile(x, k))
            if k == 0:
                levels = level_rows(batch_index, occ_energy)
        near, far = buf, far
        if k + 1 < len(masks):
            buf = jnp.concatenate([near, far], axis=0)
            if k + 1 < PARTS:
                buf, _ = lax.optimization_barrier((buf, slabs[-1]))
                x, _ = lax.optimization_barrier((x, far))
    while len(slabs) < PARTS:
        slabs.append(retile(x, len(slabs)))
    half, keep, send = half_transform(tuple(masks), block_list, slot_counts, near, far, slabs)
    keep = keep + swap(send, 1)
    for mask in reversed(masks[:-1]):
        keep = keep + swap(keep, mask)
    other = swap(keep, 1)
    terms, energy = gradient_terms(
        block_list, slot_counts, keep, other, levels, vir_energy, half, slabs
    )
    buf = terms[None]
    for mask in masks:
        near, far = buf, swap(buf, mask)
        buf = jnp.concatenate([near, far], axis=0)
    grad_coef = place_terms(near, far, local_rows).T
    energies = jnp.sum(energy, axis=1)
    orbs = owner_map.shape[0]
    same = owner_map[:, None] == owner_map[None, :]
    earlier = jnp.arange(orbs)[None, :] < jnp.arange(orbs)[:, None]
    rank = jnp.sum((same & earlier).astype(jnp.int32), axis=1)
    hit = (owner_map == me)[None, :] & (rank[None, :] == jnp.arange(CAP)[:, None])
    pair_energy = jnp.sum(jnp.where(hit, energies[None, :], 0.0), axis=1)
    return (grad_coef, pair_energy)


def solution(mesh):
    return jax.shard_map(
        body,
        mesh=mesh,
        in_specs=(
            P(("groups", "aux"), None, None),
            P(("groups", "aux"), None),
            P(("groups", "aux")),
            P(("groups", "aux"), None),
            P("groups"),
            P("groups"),
            P("groups"),
            P("groups"),
        ),
        out_specs=(P(("groups", "aux"), None), P(("groups", "aux"))),
        check_vma=False,
    )
```

time: 230 us -> 73.6 us (0.32)
  blocking collectives: 77.4 us -> 0 us
  waiting for transfers between devices: 75.4 us -> 26.4 us
  matrix products: 22.5 us -> 0 us
  Pallas kernels: 0 us -> 19.5 us
  local copies, waits for them, and re-layouts: 25.7 us -> 9.67 us
  between operations: 14.9 us -> 1.45 us
  starting transfers between devices: 8.53 us -> 15.1 us
  other arithmetic: 5.11 us -> 1.05 us
    all_gather x2 -> x0, blocking collectives: 77.4 us -> none  [the longest x1 53.9 us: body(): whole_coef = lax.all_gather(coefficients, 'aux', axis=0, tiled=True)]
    reduce_scatter x1 -> x0, waiting for transfers between devices: 54.2 us -> none  [body(): lax.psum_scatter(placed.reshape(local_rows * lax.axis_size('aux'), orbita...]
    ppermute x0 -> x13, waiting for transfers between devices: none -> 26.4 us  [swap(): return lax.ppermute(x, 'aux', [(i, i ^ mask) for i in range(size)])]
    dot_general x5 -> x0, matrix products: 22.5 us -> none  [the longest x1 10.9 us: body(): jnp.einsum('qsmn,qin->smi', slabs, weights, preferred_element_type=jnp.fl...]
    all_to_all x1 -> x0, waiting for transfers between devices: 21.2 us -> none  [body(): lax.all_to_all(outgoing, 'aux', split_axis=1, concat_axis=0, tiled=True)]
    pallas_call x0 -> x8, Pallas kernels: none -> 19.5 us  [the longest x1 6.68 us: gradient_terms(): pl.pallas_call(grad_kernel, in_specs=[SMEM, SMEM] + [VMEM] * 5 + [VMEM] *...]
    ppermute x0 -> x13, starting transfers between devices: none -> 15.1 us  [swap(): return lax.ppermute(x, 'aux', [(i, i ^ mask) for i in range(size)])]
    all_to_all x1 -> x0, starting transfers between devices: 8.49 us -> none  [body(): lax.all_to_all(outgoing, 'aux', split_axis=1, concat_axis=0, tiled=True)]
  transfers between devices with their start and end apart: 2 -> 13, of which waited for: 2 -> 10; matrix products, arithmetic and copies ran while one was open for 1% -> 1% of each run, Pallas kernels for 0% -> 8%
where the time goes in v1:
time: 73.6 us; the launch traced here: 73.2 us
  waiting for transfers between devices  26.4 us (36%)
  Pallas kernels  19.5 us (26%)
  starting transfers between devices  15.1 us (21%)
  local copies, waits for them, and re-layouts  9.67 us (13%)
  between operations  1.45 us (2%)
  other arithmetic  1.05 us (1%)
    ppermute x13, waiting for transfers between devices, swap(): return lax.ppermute(x, 'aux', [(i, i ^ mask) for i in range(size)])  26.4 us
    ppermute x13, starting transfers between devices, swap(): return lax.ppermute(x, 'aux', [(i, i ^ mask) for i in range(size)])  15.1 us
    unnamed x22, local copies, waits for them, and re-layouts  9.67 us
    pallas_call x1, Pallas kernels, gradient_terms(): pl.pallas_call(grad_kernel, in_specs=[SMEM, SMEM] + [VMEM] * 5 + [VMEM] *...  6.68 us
    pallas_call x1, Pallas kernels, half_transform(): pl.pallas_call(functools.partial(half_kernel, masks), in_specs=[SMEM, SME...  4.75 us
    pallas_call x4, Pallas kernels, retile(): pl.pallas_call(functools.partial(retile_kernel, part), in_specs=[VMEM], o...  3.5 us
    pallas_call x1, Pallas kernels, level_rows(): pl.pallas_call(level_kernel, in_specs=[SMEM, VMEM], out_specs=VMEM, out_s...  2.57 us
    pallas_call x1, Pallas kernels, place_terms(): pl.pallas_call(place_kernel, in_specs=[VMEM, VMEM], out_specs=VMEM, out_s...  2.02 us
  transfers between devices with their start and end apart: 13, of which 10 were waited for; matrix products, arithmetic and copies ran while one was open for 1% of the time, Pallas kernels for 8%

profile of v1, /device:TPU:0, one launch (start us, length us, event | category | flops | bytes accessed | tf_op | source)
XLA Modules:
  0.0 73.2 jit_solution(16229433567970980479)
XLA Ops:
  0.6 4.1 %collective-permute-start = (bf16[1,16,1024]{2,1,0:T(8,128)(2,1)}, bf16[1,16,1024]{2,1,0:T(8,128)(2,1)S(1)}, u32[]{:S(2)}, u32[]{:S(2)}) collective-permute-start(bf16[1,16,1024]{2,1,0:T(8,128)(2,1)} %bitcast.18), channel_id=1, source_target_pairs={{0,8},{1,9},{2,10},{3,11},{4,12},{5,13},{6,14},{7,15},{8,0},{9,1},... | collective-permute-start | bytes 98312 | tf_op jit(solution)/shard_map/ppermute | solution.py:328
  4.7 4.0 %copy-done = bf16[256,5,4096]{2,0,1:T(8,128)(2,1)S(1)} copy-done((bf16[256,5,4096]{2,0,1:T(8,128)(2,1)S(1)}, bf16[256,5,4096]{2,0,1:T(8,128)(2,1)}, u32[]{:S(2)}) %copy-start) | copy-done | bytes 10485784
  8.7 0.9 %shard_map.95.refs_0_ = bf16[64,160,128]{2,1,0:T(8,128)(2,1)S(1)} custom-call(bf16[5,256,4096]{2,1,0:T(8,128)(2,1)S(1)} %bitcast.8), custom_call_target="tpu_custom_call" | custom-call | bytes 5242880 | tf_op jit(solution)/shard_map/pallas_call | solution.py:44
  9.6 1.6 %collective-permute-start.1 = (bf16[2,16,1024]{2,1,0:T(8,128)(2,1)S(1)}, bf16[2,16,1024]{2,1,0:T(8,128)(2,1)S(1)}, u32[]{:S(2)}, u32[]{:S(2)}) collective-permute-start(bf16[2,16,1024]{2,1,0:T(8,128)(2,1)S(1)} %pad_maximum_fusion.4), channel_id=1, source_target_pairs={{0,4},{1,5},{2,6},{3,7},{4,0},{5,1},{6,2},{7,3},{8,12},{9,13},{10,... | collective-permute-start | bytes 196616 | tf_op jit(solution)/shard_map/ppermute | solution.py:328
  11.3 0.9 %shard_map.96.refs_1_ = bf16[64,160,128]{2,1,0:T(8,128)(2,1)S(1)} custom-call(bf16[5,256,4096]{2,1,0:T(8,128)(2,1)S(1)} %bitcast.9), custom_call_target="tpu_custom_call" | custom-call | bytes 5242880 | tf_op jit(solution)/shard_map/pallas_call | solution.py:44
  12.2 1.8 %collective-permute-done.1 = bf16[2,16,1024]{2,1,0:T(8,128)(2,1)S(1)} collective-permute-done((bf16[2,16,1024]{2,1,0:T(8,128)(2,1)S(1)}, bf16[2,16,1024]{2,1,0:T(8,128)(2,1)S(1)}, u32[]{:S(2)}, u32[]{:S(2)}) %collective-permute-start.1) | collective-permute-done | bytes 65568 | tf_op jit(solution)/shard_map/ppermute | solution.py:328
  14.0 1.6 %collective-permute-start.2 = (bf16[4,16,1024]{2,1,0:T(8,128)(2,1)S(1)}, bf16[4,16,1024]{2,1,0:T(8,128)(2,1)S(1)}, u32[]{:S(2)}, u32[]{:S(2)}) collective-permute-start(bf16[4,16,1024]{2,1,0:T(8,128)(2,1)S(1)} %pad_maximum_fusion.2), channel_id=1, source_target_pairs={{0,2},{1,3},{2,0},{3,1},{4,6},{5,7},{6,4},{7,5},{8,10},{9,11},{10,... | collective-permute-start | bytes 393224 | tf_op jit(solution)/shard_map/ppermute | solution.py:328
  15.5 0.9 %shard_map.97.refs_2_ = bf16[64,160,128]{2,1,0:T(8,128)(2,1)S(1)} custom-call(bf16[5,256,4096]{2,1,0:T(8,128)(2,1)S(1)} %bitcast.10), custom_call_target="tpu_custom_call" | custom-call | bytes 5242880 | tf_op jit(solution)/shard_map/pallas_call | solution.py:44
  16.4 2.6 %collective-permute-done.2 = bf16[4,16,1024]{2,1,0:T(8,128)(2,1)S(1)} collective-permute-done((bf16[4,16,1024]{2,1,0:T(8,128)(2,1)S(1)}, bf16[4,16,1024]{2,1,0:T(8,128)(2,1)S(1)}, u32[]{:S(2)}, u32[]{:S(2)}) %collective-permute-start.2) | collective-permute-done | bytes 131104 | tf_op jit(solution)/shard_map/ppermute | solution.py:328
  19.8 0.9 %shard_map.98.refs_3_ = bf16[64,160,128]{2,1,0:T(8,128)(2,1)S(1)} custom-call(bf16[5,256,4096]{2,1,0:T(8,128)(2,1)S(1)} %bitcast.11), custom_call_target="tpu_custom_call" | custom-call | bytes 5242880 | tf_op jit(solution)/shard_map/pallas_call | solution.py:44
  20.7 1.5 %copy-done.5 = bf16[64,160,128]{2,1,0:T(8,128)(2,1)} copy-done((bf16[64,160,128]{2,1,0:T(8,128)(2,1)}, bf16[64,160,128]{2,1,0:T(8,128)(2,1)S(1)}, u32[]{:S(2)}) %copy-start.5) | copy-done | bytes 2621464
  22.2 4.7 %shard_map.99 = (bf16[16,128,128]{2,1,0:T(8,128)(2,1)S(1)}, f32[136,128]{1,0:T(8,128)S(1)}, f32[136,128]{1,0:T(8,128)S(1)}) custom-call(s32[1,5]{1,0:T(1,128)S(1)} %copy-done.7, s32[1]{0:T(128)S(6)} %copy.10.counts, bf16[8,16,1024]{2,1,0:T(8,128)(2,1)S(1)} %pad_maximum_fusion.coef_a, bf16[8,16,1024]{2,1,0:T(8,128)(2,1)S(1)} %collective-permute-done.3.coef_b, ...), custom_call_target="tpu_custom_call" | custom-call | tf_op jit(solution)/shard_map/pallas_call | solution.py:148
  26.9 0.6 collective-permute-start.4
  27.5 0.9 %collective-permute-done.4 = f32[136,128]{1,0:T(8,128)S(1)} collective-permute-done((f32[136,128]{1,0:T(8,128)S(1)}, f32[136,128]{1,0:T(8,128)S(1)}, u32[]{:S(2)}, u32[]{:S(2)}) %collective-permute-start.4) | collective-permute-done | bytes 69664 | tf_op jit(solution)/shard_map/ppermute | solution.py:328
  28.4 1.6 %collective-permute-start.5 = (f32[136,128]{1,0:T(8,128)S(1)}, f32[136,128]{1,0:T(8,128)S(1)}, u32[]{:S(2)}, u32[]{:S(2)}) collective-permute-start(f32[136,128]{1,0:T(8,128)S(1)} %add.12), channel_id=1, source_target_pairs={{0,2},{1,3},{2,0},{3,1},{4,6},{5,7},{6,4},{7,5},{8,10},{9,11},{10,... | collective-permute-start | bytes 208904 | tf_op jit(solution)/shard_map/ppermute | solution.py:328
  30.0 2.9 %collective-permute-done.5 = f32[136,128]{1,0:T(8,128)S(1)} collective-permute-done((f32[136,128]{1,0:T(8,128)S(1)}, f32[136,128]{1,0:T(8,128)S(1)}, u32[]{:S(2)}, u32[]{:S(2)}) %collective-permute-start.5) | collective-permute-done | bytes 69664 | tf_op jit(solution)/shard_map/ppermute | solution.py:328
  32.9 1.6 %collective-permute-start.6 = (f32[136,128]{1,0:T(8,128)S(1)}, f32[136,128]{1,0:T(8,128)S(1)}, u32[]{:S(2)}, u32[]{:S(2)}) collective-permute-start(f32[136,128]{1,0:T(8,128)S(1)} %add.13), channel_id=1, source_target_pairs={{0,4},{1,5},{2,6},{3,7},{4,0},{5,1},{6,2},{7,3},{8,12},{9,13},{10,... | collective-permute-start | bytes 208904 | tf_op jit(solution)/shard_map/ppermute | solution.py:328
  34.6 2.7 %collective-permute-done.6 = f32[136,128]{1,0:T(8,128)S(1)} collective-permute-done((f32[136,128]{1,0:T(8,128)S(1)}, f32[136,128]{1,0:T(8,128)S(1)}, u32[]{:S(2)}, u32[]{:S(2)}) %collective-permute-start.6) | collective-permute-done | bytes 69664 | tf_op jit(solution)/shard_map/ppermute | solution.py:328
  37.6 5.0 %collective-permute-done.7 = f32[136,128]{1,0:T(8,128)S(1)} collective-permute-done((f32[136,128]{1,0:T(8,128)S(1)}, f32[136,128]{1,0:T(8,128)S(1)}, u32[]{:S(2)}, u32[]{:S(2)}) %collective-permute-start.7) | collective-permute-done | bytes 69664 | tf_op jit(solution)/shard_map/ppermute | solution.py:328
  42.7 2.6 %shard_map.100.levels = f32[16,128]{1,0:T(8,128)} custom-call(s32[16]{0:T(128)} %index.1, f32[8,128]{1,0:T(8,128)} %bitcast.20), custom_call_target="tpu_custom_call" | custom-call | tf_op jit(solution)/shard_map/pallas_call | solution.py:172
  45.3 1.7 %copy-done.2 = bf16[64,160,128]{2,1,0:T(8,128)(2,1)S(1)} copy-done((bf16[64,160,128]{2,1,0:T(8,128)(2,1)S(1)}, bf16[64,160,128]{2,1,0:T(8,128)(2,1)}, u32[]{:S(2)}) %copy-start.2) | copy-done | bytes 2621464
  47.0 1.7 %copy-done.4 = bf16[64,160,128]{2,1,0:T(8,128)(2,1)S(1)} copy-done((bf16[64,160,128]{2,1,0:T(8,128)(2,1)S(1)}, bf16[64,160,128]{2,1,0:T(8,128)(2,1)}, u32[]{:S(2)}) %copy-start.4) | copy-done | bytes 2621464
  48.8 0.7 copy-done.6
  49.5 6.7 %shard_map.101 = (f32[16,384]{1,0:T(8,128)S(1)}, f32[16,128]{1,0:T(8,128)S(1)}) custom-call(s32[1,5]{1,0:T(1,128)S(1)} %copy-done.7, s32[1]{0:T(128)S(6)} %copy.10.counts, f32[136,128]{1,0:T(8,128)S(1)} %add.15.mine, f32[136,128]{1,0:T(8,128)S(1)} %collective-permute-done.8.other, f32[16,128]{1,0:T(8,128)S(1)} %copy-done.6, f32[1,64]{1,0:T(1,128)S(1)} %bitcast.16, ...), custom_call_target="tpu_custom_call" | custom-call | tf_op jit(solution)/shard_map/pallas_call | solution.py:271
  56.4 4.5 %collective-permute-done.9 = f32[1,16,384]{2,1,0:T(8,128)S(1)} collective-permute-done((f32[1,16,384]{2,1,0:T(8,128)S(1)}, f32[1,16,384]{2,1,0:T(8,128)S(1)}, u32[]{:S(2)}, u32[]{:S(2)}) %collective-permute-start.9) | collective-permute-done | bytes 24608 | tf_op jit(solution)/shard_map/ppermute | solution.py:328
  60.9 1.9 %collective-permute-start.10 = (f32[2,16,384]{2,1,0:T(8,128)S(1)}, f32[2,16,384]{2,1,0:T(8,128)S(1)}, u32[]{:S(2)}, u32[]{:S(2)}) collective-permute-start(f32[2,16,384]{2,1,0:T(8,128)S(1)} %pad_maximum_fusion.5), channel_id=1, source_target_pairs={{0,4},{1,5},{2,6},{3,7},{4,0},{5,1},{6,2},{7,3},{8,12},{9,13},{10,... | collective-permute-start | bytes 147464 | tf_op jit(solution)/shard_map/ppermute | solution.py:328
  62.7 2.2 %collective-permute-done.10 = f32[2,16,384]{2,1,0:T(8,128)S(1)} collective-permute-done((f32[2,16,384]{2,1,0:T(8,128)S(1)}, f32[2,16,384]{2,1,0:T(8,128)S(1)}, u32[]{:S(2)}, u32[]{:S(2)}) %collective-permute-start.10) | collective-permute-done | bytes 49184 | tf_op jit(solution)/shard_map/ppermute | solution.py:328
  65.0 1.6 %collective-permute-start.11 = (f32[4,16,384]{2,1,0:T(8,128)S(1)}, f32[4,16,384]{2,1,0:T(8,128)S(1)}, u32[]{:S(2)}, u32[]{:S(2)}) collective-permute-start(f32[4,16,384]{2,1,0:T(8,128)S(1)} %pad_maximum_fusion.3), channel_id=1, source_target_pairs={{0,2},{1,3},{2,0},{3,1},{4,6},{5,7},{6,4},{7,5},{8,10},{9,11},{10,... | collective-permute-start | bytes 294920 | tf_op jit(solution)/shard_map/ppermute | solution.py:328
  66.5 3.1 %collective-permute-done.11 = f32[4,16,384]{2,1,0:T(8,128)S(1)} collective-permute-done((f32[4,16,384]{2,1,0:T(8,128)S(1)}, f32[4,16,384]{2,1,0:T(8,128)S(1)}, u32[]{:S(2)}, u32[]{:S(2)}) %collective-permute-start.11) | collective-permute-done | bytes 98336 | tf_op jit(solution)/shard_map/ppermute | solution.py:328
  70.0 0.6 fusion.1
  70.7 0.5 collective-permute-done.12.far
  71.2 2.0 %shard_map.102 = f32[16,1024]{1,0:T(8,128)} custom-call(f32[8,16,384]{2,1,0:T(8,128)S(1)} %pad_maximum_fusion.1.near, f32[8,16,384]{2,1,0:T(8,128)S(1)} %collective-permute-done.12.far), custom_call_target="tpu_custom_call" | custom-call | tf_op jit(solution)/shard_map/pallas_call | solution.py:317
  (38 shorter events, 1.1 us)
Async XLA Ops:
  0.6 9.0 %collective-permute-start = (bf16[1,16,1024]{2,1,0:T(8,128)(2,1)}, bf16[1,16,1024]{2,1,0:T(8,128)(2,1)S(1)}, u32[]{:S(2)}, u32[]{:S(2)}) collective-permute-start(bf16[1,16,1024]{2,1,0:T(8,128)(2,1)} %bitcast.18), channel_id=1, source_target_pairs={{0,8},{1,9},{2,10},{3,11},{4,12},{5,13},{6,14},{7,15},{8,0},{9,1},... | collective-permute-start | bytes 98312 | tf_op jit(solution)/shard_map/ppermute | solution.py:328
  4.7 4.0 %copy-start = (bf16[256,5,4096]{2,0,1:T(8,128)(2,1)S(1)}, bf16[256,5,4096]{2,0,1:T(8,128)(2,1)}, u32[]{:S(2)}) copy-start(bf16[256,5,4096]{2,0,1:T(8,128)(2,1)} %param.8) | copy-start | bytes 31457284
  8.7 0.9 %copy-start.9 = (bf16[1024,16]{0,1:T(8,128)(2,1)S(1)}, bf16[1024,16]{0,1:T(8,128)(2,1)}, u32[]{:S(2)}) copy-start(bf16[1024,16]{0,1:T(8,128)(2,1)} %param.11) | copy-start | bytes 98308
  9.6 4.3 %collective-permute-start.1 = (bf16[2,16,1024]{2,1,0:T(8,128)(2,1)S(1)}, bf16[2,16,1024]{2,1,0:T(8,128)(2,1)S(1)}, u32[]{:S(2)}, u32[]{:S(2)}) collective-permute-start(bf16[2,16,1024]{2,1,0:T(8,128)(2,1)S(1)} %pad_maximum_fusion.4), channel_id=1, source_target_pairs={{0,4},{1,5},{2,6},{3,7},{4,0},{5,1},{6,2},{7,3},{8,12},{9,13},{10,... | collective-permute-start | bytes 196616 | tf_op jit(solution)/shard_map/ppermute | solution.py:328
  12.1 10.0 %copy-start.1 = (bf16[64,160,128]{2,1,0:T(8,128)(2,1)}, bf16[64,160,128]{2,1,0:T(8,128)(2,1)S(1)}, u32[]{:S(2)}) copy-start(bf16[64,160,128]{2,1,0:T(8,128)(2,1)S(1)} %shard_map.96.refs_1_) | copy-start | bytes 7864324
  14.0 5.0 %collective-permute-start.2 = (bf16[4,16,1024]{2,1,0:T(8,128)(2,1)S(1)}, bf16[4,16,1024]{2,1,0:T(8,128)(2,1)S(1)}, u32[]{:S(2)}, u32[]{:S(2)}) collective-permute-start(bf16[4,16,1024]{2,1,0:T(8,128)(2,1)S(1)} %pad_maximum_fusion.2), channel_id=1, source_target_pairs={{0,2},{1,3},{2,0},{3,1},{4,6},{5,7},{6,4},{7,5},{8,10},{9,11},{10,... | collective-permute-start | bytes 393224 | tf_op jit(solution)/shard_map/ppermute | solution.py:328
  16.4 5.8 %copy-start.3 = (bf16[64,160,128]{2,1,0:T(8,128)(2,1)}, bf16[64,160,128]{2,1,0:T(8,128)(2,1)S(1)}, u32[]{:S(2)}) copy-start(bf16[64,160,128]{2,1,0:T(8,128)(2,1)S(1)} %shard_map.97.refs_2_) | copy-start | bytes 7864324
  19.0 3.1 %collective-permute-start.3 = (bf16[8,16,1024]{2,1,0:T(8,128)(2,1)S(1)}, bf16[8,16,1024]{2,1,0:T(8,128)(2,1)S(1)}, u32[]{:S(2)}, u32[]{:S(2)}) collective-permute-start(bf16[8,16,1024]{2,1,0:T(8,128)(2,1)S(1)} %pad_maximum_fusion.coef_a), channel_id=1, source_target_pairs={{0,1},{1,0},{2,3},{3,2},{4,5},{5,4},{6,7},{7,6},{8,9},{9,8},{10,11... | collective-permute-start | bytes 786440 | tf_op jit(solution)/shard_map/ppermute | solution.py:328
  19.8 2.4 %copy-start.7 = (s32[1,5]{1,0:T(1,128)S(1)}, s32[1,5]{1,0:T(1,128)}, u32[]{:S(2)}) copy-start(s32[1,5]{1,0:T(1,128)} %blocks.3) | copy-start | bytes 64
  20.7 1.5 %copy-start.5 = (bf16[64,160,128]{2,1,0:T(8,128)(2,1)}, bf16[64,160,128]{2,1,0:T(8,128)(2,1)S(1)}, u32[]{:S(2)}) copy-start(bf16[64,160,128]{2,1,0:T(8,128)(2,1)S(1)} %shard_map.98.refs_3_) | copy-start | bytes 7864324
  22.2 23.1 %copy-start.8 = (f32[64]{0:T(128)S(1)}, f32[64]{0:T(128)}, u32[]{:S(2)}) copy-start(f32[64]{0:T(128)} %param.14) | copy-start | bytes 772
  26.9 1.5 %collective-permute-start.4 = (f32[136,128]{1,0:T(8,128)S(1)}, f32[136,128]{1,0:T(8,128)S(1)}, u32[]{:S(2)}, u32[]{:S(2)}) collective-permute-start(f32[136,128]{1,0:T(8,128)S(1)} %get-tuple-element.20), channel_id=1, source_target_pairs={{0,1},{1,0},{2,3},{3,2},{4,5},{5,4},{6,7},{7,6},{8,9},{9,8},{10,11... | collective-permute-start | bytes 208904 | tf_op jit(solution)/shard_map/ppermute | solution.py:328
  28.4 4.5 %collective-permute-start.5 = (f32[136,128]{1,0:T(8,128)S(1)}, f32[136,128]{1,0:T(8,128)S(1)}, u32[]{:S(2)}, u32[]{:S(2)}) collective-permute-start(f32[136,128]{1,0:T(8,128)S(1)} %add.12), channel_id=1, source_target_pairs={{0,2},{1,3},{2,0},{3,1},{4,6},{5,7},{6,4},{7,5},{8,10},{9,11},{10,... | collective-permute-start | bytes 208904 | tf_op jit(solution)/shard_map/ppermute | solution.py:328
  32.9 4.4 %collective-permute-start.6 = (f32[136,128]{1,0:T(8,128)S(1)}, f32[136,128]{1,0:T(8,128)S(1)}, u32[]{:S(2)}, u32[]{:S(2)}) collective-permute-start(f32[136,128]{1,0:T(8,128)S(1)} %add.13), channel_id=1, source_target_pairs={{0,4},{1,5},{2,6},{3,7},{4,0},{5,1},{6,2},{7,3},{8,12},{9,13},{10,... | collective-permute-start | bytes 208904 | tf_op jit(solution)/shard_map/ppermute | solution.py:328
  37.3 5.3 %collective-permute-start.7 = (f32[136,128]{1,0:T(8,128)S(1)}, f32[136,128]{1,0:T(8,128)S(1)}, u32[]{:S(2)}, u32[]{:S(2)}) collective-permute-start(f32[136,128]{1,0:T(8,128)S(1)} %add.14), channel_id=1, source_target_pairs={{0,8},{1,9},{2,10},{3,11},{4,12},{5,13},{6,14},{7,15},{8,0},{9,1},... | collective-permute-start | bytes 208904 | tf_op jit(solution)/shard_map/ppermute | solution.py:328
  42.6 2.6 %collective-permute-start.8 = (f32[136,128]{1,0:T(8,128)S(1)}, f32[136,128]{1,0:T(8,128)S(1)}, u32[]{:S(2)}, u32[]{:S(2)}) collective-permute-start(f32[136,128]{1,0:T(8,128)S(1)} %add.15.mine), channel_id=1, source_target_pairs={{0,1},{1,0},{2,3},{3,2},{4,5},{5,4},{6,7},{7,6},{8,9},{9,8},{10,11... | collective-permute-start | bytes 208904 | tf_op jit(solution)/shard_map/ppermute | solution.py:328
  45.3 1.7 %copy-start.2 = (bf16[64,160,128]{2,1,0:T(8,128)(2,1)S(1)}, bf16[64,160,128]{2,1,0:T(8,128)(2,1)}, u32[]{:S(2)}) copy-start(bf16[64,160,128]{2,1,0:T(8,128)(2,1)} %copy-done.1) | copy-start | bytes 7864324
  47.0 1.7 %copy-start.4 = (bf16[64,160,128]{2,1,0:T(8,128)(2,1)S(1)}, bf16[64,160,128]{2,1,0:T(8,128)(2,1)}, u32[]{:S(2)}) copy-start(bf16[64,160,128]{2,1,0:T(8,128)(2,1)} %copy-done.3) | copy-start | bytes 7864324
  48.8 0.7 copy-start.6
  49.4 17.1 %copy-start.10 = (s32[16]{0:T(128)S(1)}, s32[16]{0:T(128)}, u32[]{:S(2)}) copy-start(s32[16]{0:T(128)} %param.15) | copy-start | bytes 196
  56.1 4.7 %collective-permute-start.9 = (f32[1,16,384]{2,1,0:T(8,128)S(1)}, f32[1,16,384]{2,1,0:T(8,128)S(1)}, u32[]{:S(2)}, u32[]{:S(2)}) collective-permute-start(f32[1,16,384]{2,1,0:T(8,128)S(1)} %bitcast.12), channel_id=1, source_target_pairs={{0,8},{1,9},{2,10},{3,11},{4,12},{5,13},{6,14},{7,15},{8,0},{9,1},... | collective-permute-start | bytes 73736 | tf_op jit(solution)/shard_map/ppermute | solution.py:328
  60.9 4.1 %collective-permute-start.10 = (f32[2,16,384]{2,1,0:T(8,128)S(1)}, f32[2,16,384]{2,1,0:T(8,128)S(1)}, u32[]{:S(2)}, u32[]{:S(2)}) collective-permute-start(f32[2,16,384]{2,1,0:T(8,128)S(1)} %pad_maximum_fusion.5), channel_id=1, source_target_pairs={{0,4},{1,5},{2,6},{3,7},{4,0},{5,1},{6,2},{7,3},{8,12},{9,13},{10,... | collective-permute-start | bytes 147464 | tf_op jit(solution)/shard_map/ppermute | solution.py:328
  65.0 4.7 %collective-permute-start.11 = (f32[4,16,384]{2,1,0:T(8,128)S(1)}, f32[4,16,384]{2,1,0:T(8,128)S(1)}, u32[]{:S(2)}, u32[]{:S(2)}) collective-permute-start(f32[4,16,384]{2,1,0:T(8,128)S(1)} %pad_maximum_fusion.3), channel_id=1, source_target_pairs={{0,2},{1,3},{2,0},{3,1},{4,6},{5,7},{6,4},{7,5},{8,10},{9,11},{10,... | collective-permute-start | bytes 294920 | tf_op jit(solution)/shard_map/ppermute | solution.py:328
  69.7 1.5 %collective-permute-start.12 = (f32[8,16,384]{2,1,0:T(8,128)S(1)}, f32[8,16,384]{2,1,0:T(8,128)S(1)}, u32[]{:S(2)}, u32[]{:S(2)}) collective-permute-start(f32[8,16,384]{2,1,0:T(8,128)S(1)} %pad_maximum_fusion.1.near), channel_id=1, source_target_pairs={{0,1},{1,0},{2,3},{3,2},{4,5},{5,4},{6,7},{7,6},{8,9},{9,8},{10,11... | collective-permute-start | bytes 589832 | tf_op jit(solution)/shard_map/ppermute | solution.py:328

commit v2 on v0

v2 whole, which is shorter than its diff:
```python
import functools

import jax
import jax.numpy as jnp
from jax import lax
from jax.experimental import pallas as pl
from jax.experimental.pallas import tpu as pltpu
from jax.sharding import PartitionSpec as P

BW = 64
S = 5
CAP = 2
LANES = 128
HALVES = LANES // BW
TILES = BW * BW // LANES
ROWS = S * TILES
PARTS = 3
F32 = jnp.float32
BF16 = jnp.bfloat16
VMEM = pl.BlockSpec(memory_space=pltpu.VMEM)
SMEM = pl.BlockSpec(memory_space=pltpu.SMEM)


def limit(orbs):
    return max(8, orbs // 4) * 2**20


def iota(shape, dim):
    return lax.broadcasted_iota(jnp.int32, shape, dim)


def split_rows(count):
    unit = count // 16
    return (3 * unit, 11 * unit, count - 14 * unit)


def retile_rows(x, out, at):
    for s in range(S):
        out[at : at + 16, s * TILES : (s + 1) * TILES, :] = x[s, at : at + 16, :].reshape(16, TILES, LANES)


def fetch(start, x, slab, sems):
    copies = []
    for c in range(slab.shape[1] // 16):
        src = x.at[:, pl.ds(start + c * 16, 16), :]
        copies.append(pltpu.make_async_copy(src, slab.at[:, pl.ds(c * 16, 16), :], sems.at[c]))
        copies[-1].start()
    return copies


def retile_kernel(start, x, out, slab, sems):
    for c, copy in enumerate(fetch(start, x, slab, sems)):
        copy.wait()
        retile_rows(slab, out, c * 16)


def retile(x, part):
    sizes = split_rows(x.shape[1])
    start, size = sum(sizes[:part]), sizes[part]
    return pl.pallas_call(
        functools.partial(retile_kernel, start),
        in_specs=[pl.BlockSpec(memory_space=pltpu.HBM)],
        out_specs=VMEM,
        out_shape=jax.ShapeDtypeStruct((size, ROWS, LANES), BF16),
        scratch_shapes=[pltpu.VMEM((S, size, TILES * LANES), BF16), pltpu.SemaphoreType.DMA((size // 16,))],
        compiler_params=pltpu.CompilerParams(vmem_limit_bytes=10 * 2**20),
        cost_estimate=pl.CostEstimate(flops=0, bytes_accessed=4 * size * ROWS * LANES, transcendentals=0),
    )(in_hbm(x))


def prepare_kernel(blocks, counts, index, levels, coef, x, *refs):
    rows, ids, held, out = refs[:4]
    sems, own_blocks, own_index, own_levels, slab, slab_sems = refs[4:]
    pairs = (blocks, own_blocks), (index, own_index), (levels, own_levels), (coef, held)
    copies = [pltpu.make_async_copy(src, dst, sems.at[k]) for k, (src, dst) in enumerate(pairs)]
    for copy in copies:
        copy.start()
    for c, copy in enumerate(fetch(0, x, slab, slab_sems)):
        copy.wait()
        retile_rows(slab, out, c * 16)
    for copy in copies:
        copy.wait()
    lane = iota((1, LANES), 1)

    def step(i, carry):
        at = own_index[i]
        row = own_levels[pl.ds(lax.div(at, LANES), 1), :]
        rows[pl.ds(i, 1), :] = jnp.where(lane == lax.rem(at, LANES), 2.0 * row, 0.0)
        return carry

    lax.fori_loop(0, rows.shape[0], step, 0)
    rows[...] = jnp.broadcast_to(jnp.sum(rows[...], axis=1, keepdims=True), rows.shape)
    total = jnp.full(ids.shape, -1, jnp.int32)
    for s in range(S):
        total = jnp.where((lane == s) & (s < counts[...]), own_blocks[0, s], total)
    ids[...] = total


def in_hbm(x):
    return pltpu.with_memory_space_constraint(x, pltpu.HBM)


def prepare(blocks, counts, index, levels, coef, x):
    far = pl.BlockSpec(memory_space=pltpu.HBM)
    size = split_rows(x.shape[1])[0]
    return pl.pallas_call(
        prepare_kernel,
        in_specs=[far, VMEM, far, far, far, far],
        out_specs=[VMEM] * 4,
        out_shape=[
            jax.ShapeDtypeStruct((index.shape[0], LANES), F32),
            jax.ShapeDtypeStruct((1, LANES), jnp.int32),
            jax.ShapeDtypeStruct(coef.shape, coef.dtype),
            jax.ShapeDtypeStruct((size, ROWS, LANES), BF16),
        ],
        scratch_shapes=[
            pltpu.SemaphoreType.DMA((4,)),
            pltpu.SMEM(blocks.shape, blocks.dtype),
            pltpu.SMEM(index.shape, index.dtype),
            pltpu.VMEM(levels.shape, levels.dtype),
            pltpu.VMEM((S, size, TILES * LANES), BF16),
            pltpu.SemaphoreType.DMA((size // 16,)),
        ],
        compiler_params=pltpu.CompilerParams(vmem_limit_bytes=8 * 2**20),
        cost_estimate=pl.CostEstimate(flops=0, bytes_accessed=4 * size * ROWS * LANES, transcendentals=0),
    )(in_hbm(blocks), counts, in_hbm(index), in_hbm(levels), in_hbm(coef), in_hbm(x))


def stages(size):
    bits = []
    while size > 2:
        size //= 2
        bits.append(size)
    steps = [(bits.pop(0),)] if len(bits) % 2 else []
    for high, low in zip(bits[::2], bits[1::2]):
        steps.append((low, high ^ low, high))
    return tuple(steps)


def gather_index(dev, me, steps):
    rel = lax.bitwise_xor(dev, me)
    place, count = 0, 1
    for step in steps:
        low = lax.bitwise_and(rel, step[0]) != 0
        if len(step) == 1:
            place = place + jnp.where(low, count, 0)
        else:
            high = lax.bitwise_and(rel, step[2]) != 0
            place = place + jnp.where(high, jnp.where(low, 2, 3), jnp.where(low, 1, 0)) * count
        count *= len(step) + 1
    return place


def half_kernel(steps, ids, coef_a, coef_b, *refs):
    slabs, (half, send, scr) = refs[:PARTS], refs[PARTS:]
    me = lax.axis_index("aux")
    orbs, width = coef_a.shape[1], coef_a.shape[2]
    per_dev = width // BW
    near = coef_a.shape[0]
    src = iota((LANES, LANES), 0)
    dst = iota((LANES, LANES), 1)
    wanted = (dst & BW) // BW + (dst & (TILES - 1)) * 2 + (dst & TILES) // TILES * BW
    spread = jnp.where(src == wanted, 1.0, 0.0).astype(BF16)
    picked = []
    for s in range(S):
        block = jnp.maximum(ids[0, s], 0)
        dev = lax.div(block, per_dev)
        inner = lax.rem(block, per_dev)
        place = gather_index(dev, me, steps)
        col = pl.multiple_of(lax.div(inner, HALVES) * LANES, LANES)
        spot = lax.rem(place, near)
        ours = coef_a[spot, :, pl.ds(col, LANES)]
        theirs = coef_b[spot, :, pl.ds(col, LANES)]
        picked.append(jnp.where(place < near, ours, theirs))
    apart = jnp.dot(jnp.concatenate(picked, axis=0), spread, preferred_element_type=F32)
    group = iota((orbs, LANES), 1) // TILES
    coef = [[jnp.zeros((orbs, LANES), F32) for _ in range(2)] for _ in range(HALVES)]
    for s in range(S):
        second = lax.rem(ids[0, s], HALVES) == 1
        value = apart[s * orbs : (s + 1) * orbs]
        value = jnp.where(second, pltpu.roll(value, LANES - TILES, 1), value)
        for h in range(HALVES):
            shift = (s * TILES - h * BW) % LANES
            there = pltpu.roll(value, shift, 1) if shift else value
            tile = s * TILES // LANES
            hit = (group == s % (LANES // TILES)) & (ids[0, s] >= 0)
            coef[h][tile] = jnp.where(hit, there, coef[h][tile])
    coef = jnp.concatenate([jnp.concatenate(coef[h], axis=1)[:, :ROWS] for h in range(HALVES)], axis=0).astype(BF16)
    low = iota((orbs, LANES), 1) < BW
    pairs = half.shape[1]
    base = 0
    for slab in slabs:
        for p in range(slab.shape[0] // 2):
            both = jnp.concatenate([slab[2 * p], slab[2 * p + 1]], axis=1)
            r = jnp.dot(coef, both, preferred_element_type=F32)
            straight = jnp.where(low, r[:orbs, :LANES], r[orbs:, LANES:])
            crossed = jnp.where(low, r[:orbs, LANES:], r[orbs:, :LANES])
            row = straight + pltpu.roll(crossed, BW, 1)
            for g in range(orbs // 8):
                scr[pl.ds(g * 8 * pairs + base + p, 8, stride=pairs), :] = row[g * 8 : g * 8 + 8]
        base += slab.shape[0] // 2
    for i in range(orbs):
        half[i] = scr[i * pairs : (i + 1) * pairs, :].astype(BF16)
    pair_squares(half, 1 - lax.rem(me, 2), send)


def pair_squares(half, core, out):
    orbs, pairs = half.shape[0], half.shape[1]
    scale = 0.125 / (2 * pairs * lax.axis_size("aux"))
    lane = iota((BW, LANES), 1)
    left = lane < BW
    upper = iota((BW, LANES), 0) <= lax.rem(lane, BW)
    eye = iota((BW, LANES), 0) == lax.rem(lane, BW)
    quads = orbs // 8
    diags = []
    for k in range(quads):
        t = []
        for j in range(4):
            h = half[core * (orbs // 2) + 4 * k + j]
            t.append(lax.dot_general(h, h, (((0,), (0,)), ((), ())), preferred_element_type=F32) * scale)
        lefts = [t[j][:BW] + pltpu.roll(t[j][BW:], BW, 1) for j in (0, 1)]
        rights = [pltpu.roll(t[j][:BW], BW, 1) + t[j][BW:] for j in (2, 3)]
        a = jnp.where(left, lefts[0], rights[0])
        b = jnp.where(left, lefts[1], rights[1])
        out[k * BW : (k + 1) * BW, :] = jnp.where(upper, a, b)
        diags.append(jnp.sum(jnp.where(eye, b, 0.0), axis=0, keepdims=True))
    spare = out.shape[0] - quads * BW - quads
    if spare:
        diags.append(jnp.zeros((spare, LANES), F32))
    out[quads * BW :, :] = jnp.concatenate(diags, axis=0)


def own_kernel(half, out):
    pair_squares(half, lax.rem(lax.axis_index("aux"), 2), out)


def own_squares(half, like):
    return pl.pallas_call(
        own_kernel,
        in_specs=[VMEM],
        out_specs=VMEM,
        out_shape=jax.ShapeDtypeStruct(like.shape, F32),
        compiler_params=pltpu.CompilerParams(vmem_limit_bytes=4 * 2**20),
        cost_estimate=pl.CostEstimate(flops=0, bytes_accessed=2 * 2**20, transcendentals=0),
    )(half)


def half_transform(steps, ids, coef_a, coef_b, slabs):
    orbs = coef_a.shape[1]
    pairs = sum(s.shape[0] for s in slabs) // 2
    quads = orbs // 8
    rows = quads * BW + -(-quads // 8) * 8
    packed = jax.ShapeDtypeStruct((rows, LANES), F32)
    return pl.pallas_call(
        functools.partial(half_kernel, steps),
        in_specs=[SMEM, VMEM, VMEM] + [VMEM] * PARTS,
        out_specs=[VMEM] * 2,
        out_shape=[jax.ShapeDtypeStruct((orbs, pairs, LANES), BF16), packed],
        scratch_shapes=[pltpu.VMEM((orbs * pairs, LANES), F32)],
        compiler_params=pltpu.CompilerParams(vmem_limit_bytes=limit(orbs)),
    )(ids, coef_a, coef_b, *slabs)


def weight_rows(packed, core, levels, vir, half, energy, weights):
    orbs, pairs = half.shape[0], half.shape[1]
    quads = orbs // 8
    lane = iota((BW, LANES), 1)
    row = iota((BW, LANES), 0)
    left = lane < BW
    inner = lax.rem(lane, BW)
    vir_b = jnp.concatenate([vir[...], vir[...]], axis=1)
    vir_a = jnp.sum(jnp.where((row == inner) & left, vir_b, 0.0), axis=1, keepdims=True)
    zero = jnp.zeros((BW, LANES), F32)
    scale = 0.5 / BW
    start = core * (orbs // 2)
    for k in range(0, quads, 2):
        squares = [packed[(k + j) * BW : (k + j + 1) * BW, :] for j in range(2)]
        turned = jnp.concatenate(squares, axis=0).T
        top, bottom = turned[:BW], turned[BW:]
        flips = [
            jnp.where(left, top, pltpu.roll(bottom, BW, 1)),
            jnp.where(left, pltpu.roll(top, BW, 1), bottom),
        ]
        for j in range(2):
            first = 4 * (k + j)
            diag = packed[quads * BW + k + j : quads * BW + k + j + 1, :]
            ints = [
                jnp.where(row <= inner, squares[j], flips[j]),
                jnp.where(row == inner, diag, jnp.where(row > inner, squares[j], flips[j])),
            ]
            for b in range(2):
                one, two = first + b, first + 2 + b
                level = jnp.where(left[:1], levels[pl.ds(start + one, 1), :], levels[pl.ds(start + two, 1), :])
                amps = ints[b] / ((level - vir_a) - vir_b)
                sums = jnp.sum(ints[b] * amps, axis=0, keepdims=True)
                energy[one : one + 1, :] = jnp.where(left[:1], sums, 0.0)
                energy[two : two + 1, :] = jnp.where(left[:1], 0.0, sums)
                turn = pltpu.roll(amps, BW, 1)
                for i, lows, highs in ((one, amps, turn), (two, turn, amps)):
                    square = jnp.concatenate([jnp.where(left, lows, zero), jnp.where(left, zero, highs)], axis=0)
                    w = jnp.dot(half[start + i], square.astype(BF16), preferred_element_type=F32) * scale
                    weights[i * pairs : (i + 1) * pairs, :] = w.astype(BF16).astype(F32)


def weight_kernel(packed, levels, vir, half, energy, weights):
    weight_rows(packed, lax.rem(lax.axis_index("aux"), 2), levels, vir, half, energy, weights)


def own_weights(packed, levels, vir, half):
    orbs, pairs = half.shape[0], half.shape[1]
    return pl.pallas_call(
        weight_kernel,
        in_specs=[VMEM] * 4,
        out_specs=[VMEM] * 2,
        out_shape=[
            jax.ShapeDtypeStruct((orbs // 2, LANES), F32),
            jax.ShapeDtypeStruct((orbs // 2 * pairs, LANES), F32),
        ],
        compiler_params=pltpu.CompilerParams(vmem_limit_bytes=4 * 2**20),
        cost_estimate=pl.CostEstimate(flops=0, bytes_accessed=3 * 2**20, transcendentals=0),
    )(packed, levels, vir, half)


def grad_kernel(ids, packed, levels, vir, half, own_energy, own, *refs):
    slabs, (terms, energy, other_energy, other, mixed) = refs[:PARTS], refs[PARTS:]
    core = lax.rem(lax.axis_index("aux"), 2)
    orbs, pairs = half.shape[0], half.shape[1]
    mid = orbs // 2
    weight_rows(packed, 1 - core, levels, vir, half, other_energy, other)

    def ordered(ours, theirs):
        return jnp.concatenate([jnp.where(core == 0, ours, theirs), jnp.where(core == 0, theirs, ours)], axis=0)

    energy[...] = ordered(own_energy[...], other_energy[...])
    low = iota((orbs, LANES), 1) < BW
    blank = jnp.zeros((orbs, LANES), F32)
    total = jnp.zeros((ROWS, HALVES * orbs), F32)
    base = 0
    for slab in slabs:
        for start in range(0, slab.shape[0] // 2, 32):
            xs, ws = [], []
            for p in range(start, min(start + 32, slab.shape[0] // 2)):
                w = jnp.concatenate(
                    [
                        ref[pl.ds(g * 8 * pairs + base + p, 8, stride=pairs), :]
                        for ref in (own, other)
                        for g in range(mid // 8)
                    ],
                    axis=0,
                )
                turn = pltpu.roll(w, BW, 1)
                ws.append(jnp.concatenate([jnp.where(low, w, blank), jnp.where(low, blank, turn)], axis=0).astype(BF16))
                ws.append(jnp.concatenate([jnp.where(low, turn, blank), jnp.where(low, blank, w)], axis=0).astype(BF16))
                xs += [slab[2 * p], slab[2 * p + 1]]
            total = total + lax.dot_general(
                jnp.concatenate(xs, axis=1),
                jnp.concatenate(ws, axis=1),
                (((1,), (1,)), ((), ())),
                preferred_element_type=F32,
            )
        base += slab.shape[0] // 2
    width = terms.shape[1]
    turn = total if HALVES * orbs > LANES else jnp.pad(total, ((0, 0), (0, LANES - HALVES * orbs)))
    for h in range(HALVES):
        rows = turn[:, h * orbs : h * orbs + LANES]
        if rows.shape[1] < LANES:
            rows = pltpu.roll(turn, LANES - h * orbs, 1)
        mixed[pl.ds(h, ROWS, stride=HALVES), :] = rows
    mixed[HALVES * ROWS :, :] = jnp.zeros((width - HALVES * ROWS, LANES), F32)
    for t in range(width // LANES):
        out = mixed[t * LANES : (t + 1) * LANES, :].T[:orbs]
        out = ordered(out[:mid], out[mid:])
        place = iota((orbs, LANES), 1) + (t * LANES - S * BW)
        for s in range(S):
            if t * LANES <= S * BW + s < (t + 1) * LANES:
                out = jnp.where(place == s, ids[0, s].astype(F32), out)
        terms[:, t * LANES : (t + 1) * LANES] = out


def gradient_terms(ids, packed, levels, vir, half, own_energy, own, slabs):
    orbs, pairs = half.shape[0], half.shape[1]
    width = -(-(S * BW + S) // LANES) * LANES
    return pl.pallas_call(
        grad_kernel,
        in_specs=[SMEM] + [VMEM] * 6 + [VMEM] * PARTS,
        out_specs=[VMEM] * 2,
        out_shape=[jax.ShapeDtypeStruct((orbs, width), F32), jax.ShapeDtypeStruct((orbs, LANES), F32)],
        scratch_shapes=[
            pltpu.VMEM(own_energy.shape, F32),
            pltpu.VMEM(own.shape, F32),
            pltpu.VMEM((width, LANES), F32),
        ],
        compiler_params=pltpu.CompilerParams(vmem_limit_bytes=limit(orbs)),
    )(ids, packed, levels, vir, half, own_energy, own, *slabs)


def place_kernel(*refs):
    piece, out = refs[0], refs[-1]
    me = lax.axis_index("aux")
    orbs, width = out.shape
    per_dev = width // BW
    step_tiles = range(width // LANES)
    lane = iota((8, LANES), 1)
    side = jnp.where(lane < BW, 0, 1)
    tiles = S * BW // LANES + 1
    start = S * BW - (tiles - 1) * LANES
    groups = [slice(g, min(g + 16, orbs)) for g in range(0, orbs, 16)]
    for rows in groups:
        parts = [slice(r, r + 8) for r in range(rows.start, rows.stop, 8)]
        if len(refs) == 3:
            total = [[refs[1][r, t * LANES : (t + 1) * LANES] for t in step_tiles] for r in parts]
        else:
            total = [[jnp.zeros((8, LANES), F32) for _ in step_tiles] for _ in parts]

        def step(d, total, parts=parts):
            total = [list(row) for row in total]
            tail = piece[d, 0:8, (tiles - 1) * LANES : tiles * LANES]
            ids = [jnp.broadcast_to(tail[:, start + s : start + s + 1], (8, LANES)) for s in range(S)]
            ids = [i.astype(jnp.int32) - me * per_dev for i in ids]
            ids = ids + [jnp.full((8, LANES), -1, jnp.int32)] * (2 * tiles - S)
            for k in range(tiles):
                spot = jnp.where(side == 0, ids[2 * k], ids[2 * k + 1]) - side
                turn_spot = jnp.where(side == 0, ids[2 * k + 1], ids[2 * k]) - side
                values = [piece[d, r, k * LANES : (k + 1) * LANES] for r in parts]
                turns = [pltpu.roll(v, BW, 1) for v in values]
                for t in step_tiles:
                    here, there = spot == HALVES * t, turn_spot == HALVES * t
                    for r in range(len(parts)):
                        added = jnp.where(here, values[r], 0.0) + jnp.where(there, turns[r], 0.0)
                        total[r][t] = total[r][t] + added
            return total

        if piece.shape[0] <= 8:
            for d in range(piece.shape[0]):
                total = step(d, total)
        else:
            total = lax.fori_loop(0, piece.shape[0], step, total)
        for r, part in enumerate(parts):
            for t in step_tiles:
                out[part, t * LANES : (t + 1) * LANES] = total[r][t]


def place_terms(piece, total, rows):
    args = (piece,) if total is None else (piece, total)
    return pl.pallas_call(
        place_kernel,
        in_specs=[VMEM] * len(args),
        out_specs=VMEM,
        out_shape=jax.ShapeDtypeStruct((piece.shape[1], rows), F32),
        compiler_params=pltpu.CompilerParams(vmem_limit_bytes=8 * 2**20),
        cost_estimate=pl.CostEstimate(flops=0, bytes_accessed=4 * piece.size, transcendentals=0),
    )(*args)


def pair_kernel(owner, energy, out, held, sem):
    copy = pltpu.make_async_copy(owner, held, sem)
    copy.start()
    copy.wait()
    me = lax.axis_index("aux")

    def step(i, carry):
        rank, rows = carry
        mine = held[i] == me
        row = energy[pl.ds(i, 1), :]
        rows = [jnp.where(mine & (rank == k), row, rows[k]) for k in range(CAP)]
        return rank + jnp.where(mine, 1, 0), rows

    blank = jnp.zeros((1, LANES), F32)
    _, rows = lax.fori_loop(0, energy.shape[0], step, (jnp.int32(0), [blank] * CAP))
    for k in range(CAP):
        out[k] = jnp.sum(rows[k])


def pair_slots(owner_map, energy):
    return pl.pallas_call(
        pair_kernel,
        in_specs=[pl.BlockSpec(memory_space=pltpu.HBM), VMEM],
        out_specs=SMEM,
        out_shape=jax.ShapeDtypeStruct((CAP,), F32),
        scratch_shapes=[pltpu.SMEM(owner_map.shape, owner_map.dtype), pltpu.SemaphoreType.DMA],
        compiler_params=pltpu.CompilerParams(vmem_limit_bytes=2**20),
        cost_estimate=pl.CostEstimate(flops=0, bytes_accessed=2**20, transcendentals=0),
    )(in_hbm(owner_map), energy)


def swap(x, mask):
    size = lax.axis_size("aux")
    return lax.ppermute(x, "aux", [(i, i ^ mask) for i in range(size)])


def body(
    integrals, block_list, slot_counts, coefficients, batch_index, occ_energy, vir_energy, owner_map
):
    local_rows = coefficients.shape[0]
    steps = stages(lax.axis_size("aux"))
    x = jnp.transpose(integrals, (1, 0, 2))
    buf = coefficients.T[None]
    slabs = []
    for k, step in enumerate(steps):
        far = [swap(buf, mask) for mask in step]
        if k == 0:
            levels, ids, buf, slab = prepare(
                block_list, slot_counts.reshape(1, 1), batch_index, occ_energy.reshape(-1, LANES), buf, x
            )
            slabs.append(slab)
        if k + 1 == len(steps):
            slabs.append(retile(x, 1))
        buf = jnp.concatenate([buf] + far, axis=0)
        buf, _ = lax.optimization_barrier((buf, slabs[-1]))
        x, _ = lax.optimization_barrier((x, far[0]))
    far = swap(buf, 1)
    slabs.append(retile(x, 2))
    half, send = half_transform(steps + ((1,),), ids, buf, far, slabs)
    keep = own_squares(half, send) + swap(send, 1)
    for step in reversed(steps):
        keep = sum([swap(keep, mask) for mask in step], keep)
    other = swap(keep, 1)
    vir = vir_energy.reshape(1, -1)
    own_energy, own = own_weights(keep, levels, vir, half)
    terms, energy = gradient_terms(ids, other, levels, vir, half, own_energy, own, slabs)
    buf, total, done = terms[None], None, 0
    for k, step in enumerate(steps):
        far = [swap(buf, mask) for mask in step]
        if k == 0:
            pair_energy = pair_slots(owner_map, energy)
        total = place_terms(buf[done:], total, local_rows)
        done = buf.shape[0]
        buf = jnp.concatenate([buf] + far, axis=0)
        buf, total, pair_energy = lax.optimization_barrier((buf, total, pair_energy))
    far = swap(buf, 1)
    total = place_terms(buf[done:], total, local_rows)
    grad_coef = place_terms(far, total, local_rows).T
    return (grad_coef, pair_energy)


def solution(mesh):
    return jax.shard_map(
        body,
        mesh=mesh,
        in_specs=(
            P(("groups", "aux"), None, None),
            P(("groups", "aux"), None),
            P(("groups", "aux")),
            P(("groups", "aux"), None),
            P("groups"),
            P("groups"),
            P("groups"),
            P("groups"),
        ),
        out_specs=(P(("groups", "aux"), None), P(("groups", "aux"))),
        check_vma=False,
    )
```

time: 230 us -> 55.8 us (0.24)
  blocking collectives: 77.4 us -> 0 us
  waiting for transfers between devices: 75.4 us -> 15.8 us
  local copies, waits for them, and re-layouts: 25.7 us -> 0.02 us
  matrix products: 22.5 us -> 0 us
  Pallas kernels: 0 us -> 19 us
  between operations: 14.9 us -> 1.47 us
  starting transfers between devices: 8.53 us -> 19.3 us
  other arithmetic: 5.11 us -> 0.11 us
    all_gather x2 -> x0, blocking collectives: 77.4 us -> none  [the longest x1 53.9 us: body(): whole_coef = lax.all_gather(coefficients, 'aux', axis=0, tiled=True)]
    reduce_scatter x1 -> x0, waiting for transfers between devices: 54.2 us -> none  [body(): lax.psum_scatter(placed.reshape(local_rows * lax.axis_size('aux'), orbita...]
    dot_general x5 -> x0, matrix products: 22.5 us -> none  [the longest x1 10.9 us: body(): jnp.einsum('qsmn,qin->smi', slabs, weights, preferred_element_type=jnp.fl...]
    all_to_all x1 -> x0, waiting for transfers between devices: 21.2 us -> none  [body(): lax.all_to_all(outgoing, 'aux', split_axis=1, concat_axis=0, tiled=True)]
    ppermute x0 -> x16, starting transfers between devices: none -> 19.3 us  [swap(): return lax.ppermute(x, 'aux', [(i, i ^ mask) for i in range(size)])]
    pallas_call x0 -> x12, Pallas kernels: none -> 19 us  [the longest x2 5.11 us: retile(): pl.pallas_call(functools.partial(retile_kernel, start), in_specs=[pl.Bloc...]
    ppermute x0 -> x16, waiting for transfers between devices: none -> 15.8 us  [swap(): return lax.ppermute(x, 'aux', [(i, i ^ mask) for i in range(size)])]
    unnamed x12 -> x2, local copies, waits for them, and re-layouts: 15.4 us -> 0.01 us
  transfers between devices with their start and end apart: 2 -> 16, of which waited for: 2 -> 12; matrix products, arithmetic and copies ran while one was open for 1% -> 0% of each run, Pallas kernels for 0% -> 18%
where the time goes in v2:
time: 55.8 us; the launch traced here: 55.7 us
  starting transfers between devices  19.3 us (35%)
  Pallas kernels  19 us (34%)
  waiting for transfers between devices  15.8 us (28%)
  between operations  1.47 us (3%)
    ppermute x16, starting transfers between devices, swap(): return lax.ppermute(x, 'aux', [(i, i ^ mask) for i in range(size)])  19.3 us
    ppermute x16, waiting for transfers between devices, swap(): return lax.ppermute(x, 'aux', [(i, i ^ mask) for i in range(size)])  15.8 us
    pallas_call x2, Pallas kernels, retile(): pl.pallas_call(functools.partial(retile_kernel, start), in_specs=[pl.Bloc...  5.11 us
    pallas_call x1, Pallas kernels, gradient_terms(): pl.pallas_call(grad_kernel, in_specs=[SMEM] + [VMEM] * 6 + [VMEM] * PARTS...  4.53 us
    pallas_call x1, Pallas kernels, half_transform(): pl.pallas_call(functools.partial(half_kernel, steps), in_specs=[SMEM, VME...  3.42 us
    pallas_call x1, Pallas kernels, prepare(): pl.pallas_call(prepare_kernel, in_specs=[far, VMEM, far, far, far, far],...  2.08 us
    pallas_call x4, Pallas kernels, place_terms(): pl.pallas_call(place_kernel, in_specs=[VMEM] * len(args), out_specs=VMEM,...  1.54 us
    pallas_call x1, Pallas kernels, pair_slots(): pl.pallas_call(pair_kernel, in_specs=[pl.BlockSpec(memory_space=pltpu.HBM...  1.46 us
  transfers between devices with their start and end apart: 16, of which 12 were waited for; matrix products, arithmetic and copies ran while one was open for 0% of the time, Pallas kernels for 18%

profile of v2, /device:TPU:0, one launch (start us, length us, event | category | flops | bytes accessed | tf_op | source)
XLA Modules:
  0.0 55.7 jit_solution(14023255005027938696)
XLA Ops:
  0.6 4.1 %collective-permute-start = (bf16[1,16,1024]{2,1,0:T(8,128)(2,1)}, bf16[1,16,1024]{2,1,0:T(8,128)(2,1)S(1)}, u32[]{:S(2)}, u32[]{:S(2)}) collective-permute-start(bf16[1,16,1024]{2,1,0:T(8,128)(2,1)} %bitcast.19), channel_id=1, source_target_pairs={{0,8},{1,9},{2,10},{3,11},{4,12},{5,13},{6,14},{7,15},{8,0},{9,1},... | collective-permute-start | bytes 98312 | tf_op jit(solution)/shard_map/ppermute | solution.py:488
  5.4 2.1 %shard_map.95 = (f32[16,128]{1,0:T(8,128)S(1)}, s32[1,128]{1,0:T(1,128)S(1)}, bf16[1,16,1024]{2,1,0:T(8,128)(2,1)S(1)}, bf16[48,160,128]{2,1,0:T(8,128)(2,1)S(1)}) custom-call(s32[1,5]{1,0:T(1,128)} %blocks.1, s32[1,1]{1,0:T(1,128)} %bitcast.9.counts, s32[16]{0:T(128)} %index.1, f32[8,128]{1,0:T(8,128)} %bitcast.21, bf16[1,16,1024]{2,1,0:T(8,128)(2,1)} %bitcast.20, ...), custom_call_target="tpu_custom_call" | custom-call | bytes 3932160 | tf_op jit(solution)/shard_map/pallas_call | solution.py:106
  7.5 1.6 %collective-permute-start.3 = (bf16[2,16,1024]{2,1,0:T(8,128)(2,1)S(1)}, bf16[2,16,1024]{2,1,0:T(8,128)(2,1)S(1)}, u32[]{:S(2)}, u32[]{:S(2)}) collective-permute-start(bf16[2,16,1024]{2,1,0:T(8,128)(2,1)S(1)} %pad_maximum_fusion.2), channel_id=1, source_target_pairs={{0,4},{1,5},{2,6},{3,7},{4,0},{5,1},{6,2},{7,3},{8,12},{9,13},{10,... | collective-permute-start | bytes 196616 | tf_op jit(solution)/shard_map/ppermute | solution.py:488
  9.1 1.4 %collective-permute-start.2 = (bf16[2,16,1024]{2,1,0:T(8,128)(2,1)S(1)}, bf16[2,16,1024]{2,1,0:T(8,128)(2,1)S(1)}, u32[]{:S(2)}, u32[]{:S(2)}) collective-permute-start(bf16[2,16,1024]{2,1,0:T(8,128)(2,1)S(1)} %pad_maximum_fusion.2), channel_id=1, source_target_pairs={{0,6},{1,7},{2,4},{3,5},{4,2},{5,3},{6,0},{7,1},{8,14},{9,15},{10,... | collective-permute-start | bytes 196616 | tf_op jit(solution)/shard_map/ppermute | solution.py:488
  10.5 0.5 collective-permute-start.1
  11.1 3.6 %shard_map.96.refs_1_ = bf16[176,160,128]{2,1,0:T(8,128)(2,1)S(1)} custom-call(bf16[5,256,4096]{2,1,0:T(8,128)(2,1)} %bitcast.16), custom_call_target="tpu_custom_call" | custom-call | bytes 14417920 | tf_op jit(solution)/shard_map/pallas_call | solution.py:60
  15.1 1.5 %shard_map.97.refs_2_ = bf16[32,160,128]{2,1,0:T(8,128)(2,1)S(1)} custom-call(bf16[5,256,4096]{2,1,0:T(8,128)(2,1)} %bitcast.17), custom_call_target="tpu_custom_call" | custom-call | bytes 2621440 | tf_op jit(solution)/shard_map/pallas_call | solution.py:60
  16.7 3.4 %shard_map.98 = (bf16[16,128,128]{2,1,0:T(8,128)(2,1)S(1)}, f32[136,128]{1,0:T(8,128)S(1)}) custom-call(s32[1,128]{1,0:T(1,128)S(1)} %get-tuple-element.22.ids, bf16[8,16,1024]{2,1,0:T(8,128)(2,1)S(1)} %pad_maximum_fusion.coef_a, bf16[8,16,1024]{2,1,0:T(8,128)(2,1)S(1)} %collective-permute-done.4.coef_b, ...), custom_call_target="tpu_custom_call" | custom-call | tf_op jit(solution)/shard_map/pallas_call | solution.py:254
  20.1 0.6 collective-permute-start.5
  21.0 0.6 %collective-permute-done.5 = f32[136,128]{1,0:T(8,128)S(1)} collective-permute-done((f32[136,128]{1,0:T(8,128)S(1)}, f32[136,128]{1,0:T(8,128)S(1)}, u32[]{:S(2)}, u32[]{:S(2)}) %collective-permute-start.5) | collective-permute-done | bytes 69664 | tf_op jit(solution)/shard_map/ppermute | solution.py:488
  21.6 1.4 %collective-permute-start.8 = (f32[136,128]{1,0:T(8,128)S(1)}, f32[136,128]{1,0:T(8,128)S(1)}, u32[]{:S(2)}, u32[]{:S(2)}) collective-permute-start(f32[136,128]{1,0:T(8,128)S(1)} %add.15), channel_id=1, source_target_pairs={{0,4},{1,5},{2,6},{3,7},{4,0},{5,1},{6,2},{7,3},{8,12},{9,13},{10,... | collective-permute-start | bytes 208904 | tf_op jit(solution)/shard_map/ppermute | solution.py:488
  23.0 1.3 %collective-permute-start.7 = (f32[136,128]{1,0:T(8,128)S(1)}, f32[136,128]{1,0:T(8,128)S(1)}, u32[]{:S(2)}, u32[]{:S(2)}) collective-permute-start(f32[136,128]{1,0:T(8,128)S(1)} %add.15), channel_id=1, source_target_pairs={{0,6},{1,7},{2,4},{3,5},{4,2},{5,3},{6,0},{7,1},{8,14},{9,15},{10,... | collective-permute-start | bytes 208904 | tf_op jit(solution)/shard_map/ppermute | solution.py:488
  24.3 0.9 %collective-permute-start.6 = (f32[136,128]{1,0:T(8,128)S(1)}, f32[136,128]{1,0:T(8,128)S(1)}, u32[]{:S(2)}, u32[]{:S(2)}) collective-permute-start(f32[136,128]{1,0:T(8,128)S(1)} %add.15), channel_id=1, source_target_pairs={{0,2},{1,3},{2,0},{3,1},{4,6},{5,7},{6,4},{7,5},{8,10},{9,11},{10,... | collective-permute-start | bytes 208904 | tf_op jit(solution)/shard_map/ppermute | solution.py:488
  25.2 0.9 %collective-permute-done.8 = f32[136,128]{1,0:T(8,128)S(1)} collective-permute-done((f32[136,128]{1,0:T(8,128)S(1)}, f32[136,128]{1,0:T(8,128)S(1)}, u32[]{:S(2)}, u32[]{:S(2)}) %collective-permute-start.8) | collective-permute-done | bytes 69664 | tf_op jit(solution)/shard_map/ppermute | solution.py:488
  26.1 2.2 %collective-permute-done.7 = f32[136,128]{1,0:T(8,128)S(1)} collective-permute-done((f32[136,128]{1,0:T(8,128)S(1)}, f32[136,128]{1,0:T(8,128)S(1)}, u32[]{:S(2)}, u32[]{:S(2)}) %collective-permute-start.7) | collective-permute-done | bytes 69664 | tf_op jit(solution)/shard_map/ppermute | solution.py:488
  28.3 1.3 %collective-permute-done.6 = f32[136,128]{1,0:T(8,128)S(1)} collective-permute-done((f32[136,128]{1,0:T(8,128)S(1)}, f32[136,128]{1,0:T(8,128)S(1)}, u32[]{:S(2)}, u32[]{:S(2)}) %collective-permute-start.6) | collective-permute-done | bytes 69664 | tf_op jit(solution)/shard_map/ppermute | solution.py:488
  29.6 2.5 %collective-permute-start.9 = (f32[136,128]{1,0:T(8,128)S(1)}, f32[136,128]{1,0:T(8,128)S(1)}, u32[]{:S(2)}, u32[]{:S(2)}) collective-permute-start(f32[136,128]{1,0:T(8,128)S(1)} %add_add_fusion), channel_id=1, source_target_pairs={{0,8},{1,9},{2,10},{3,11},{4,12},{5,13},{6,14},{7,15},{8,0},{9,1},... | collective-permute-start | bytes 208904 | tf_op jit(solution)/shard_map/ppermute | solution.py:488
  32.2 3.9 %collective-permute-done.9 = f32[136,128]{1,0:T(8,128)S(1)} collective-permute-done((f32[136,128]{1,0:T(8,128)S(1)}, f32[136,128]{1,0:T(8,128)S(1)}, u32[]{:S(2)}, u32[]{:S(2)}) %collective-permute-start.9) | collective-permute-done | bytes 69664 | tf_op jit(solution)/shard_map/ppermute | solution.py:488
  36.2 0.5 shard_map.100
  36.7 0.8 %collective-permute-done.10.packed = f32[136,128]{1,0:T(8,128)S(1)} collective-permute-done((f32[136,128]{1,0:T(8,128)S(1)}, f32[136,128]{1,0:T(8,128)S(1)}, u32[]{:S(2)}, u32[]{:S(2)}) %collective-permute-start.10) | collective-permute-done | bytes 69664 | tf_op jit(solution)/shard_map/ppermute | solution.py:488
  37.4 4.5 %shard_map.101 = (f32[16,384]{1,0:T(8,128)S(1)}, f32[16,128]{1,0:T(8,128)S(1)}) custom-call(s32[1,128]{1,0:T(1,128)S(1)} %get-tuple-element.22.ids, f32[136,128]{1,0:T(8,128)S(1)} %collective-permute-done.10.packed, f32[16,128]{1,0:T(8,128)S(1)} %get-tuple-element.31.levels, f32[1,64]{1,0:T(1,128)S(1)} %bitcast.14, ...), custom_call_target="tpu_custom_call" | custom-call | tf_op jit(solution)/shard_map/pallas_call | solution.py:383
  42.0 1.3 %collective-permute-start.11 = (f32[1,16,384]{2,1,0:T(8,128)S(1)}, f32[1,16,384]{2,1,0:T(8,128)S(1)}, u32[]{:S(2)}, u32[]{:S(2)}) collective-permute-start(f32[1,16,384]{2,1,0:T(8,128)S(1)} %bitcast.10), channel_id=1, source_target_pairs={{0,8},{1,9},{2,10},{3,11},{4,12},{5,13},{6,14},{7,15},{8,0},{9,1},... | collective-permute-start | bytes 73736 | tf_op jit(solution)/shard_map/ppermute | solution.py:488
  43.4 1.5 %shard_map.103 = f32[2]{0:T(128)} custom-call(s32[16]{0:T(128)} %owner.1, f32[16,128]{1,0:T(8,128)S(1)} %get-tuple-element.35.energy), custom_call_target="tpu_custom_call" | custom-call | bytes 1048576 | tf_op jit(solution)/shard_map/pallas_call | solution.py:475
  44.9 1.9 %collective-permute-done.11 = f32[1,16,384]{2,1,0:T(8,128)S(1)} collective-permute-done((f32[1,16,384]{2,1,0:T(8,128)S(1)}, f32[1,16,384]{2,1,0:T(8,128)S(1)}, u32[]{:S(2)}, u32[]{:S(2)}) %collective-permute-start.11) | collective-permute-done | bytes 24608 | tf_op jit(solution)/shard_map/ppermute | solution.py:488
  46.8 0.8 %collective-permute-start.14 = (f32[2,16,384]{2,1,0:T(8,128)S(1)}, f32[2,16,384]{2,1,0:T(8,128)S(1)}, u32[]{:S(2)}, u32[]{:S(2)}) collective-permute-start(f32[2,16,384]{2,1,0:T(8,128)S(1)} %pad_maximum_fusion.3), channel_id=1, source_target_pairs={{0,4},{1,5},{2,6},{3,7},{4,0},{5,1},{6,2},{7,3},{8,12},{9,13},{10,... | collective-permute-start | bytes 147464 | tf_op jit(solution)/shard_map/ppermute | solution.py:488
  47.6 1.2 %collective-permute-start.13 = (f32[2,16,384]{2,1,0:T(8,128)S(1)}, f32[2,16,384]{2,1,0:T(8,128)S(1)}, u32[]{:S(2)}, u32[]{:S(2)}) collective-permute-start(f32[2,16,384]{2,1,0:T(8,128)S(1)} %pad_maximum_fusion.3), channel_id=1, source_target_pairs={{0,6},{1,7},{2,4},{3,5},{4,2},{5,3},{6,0},{7,1},{8,14},{9,15},{10,... | collective-permute-start | bytes 147464 | tf_op jit(solution)/shard_map/ppermute | solution.py:488
  48.8 1.5 %collective-permute-start.12 = (f32[2,16,384]{2,1,0:T(8,128)S(1)}, f32[2,16,384]{2,1,0:T(8,128)S(1)}, u32[]{:S(2)}, u32[]{:S(2)}) collective-permute-start(f32[2,16,384]{2,1,0:T(8,128)S(1)} %pad_maximum_fusion.3), channel_id=1, source_target_pairs={{0,2},{1,3},{2,0},{3,1},{4,6},{5,7},{6,4},{7,5},{8,10},{9,11},{10,... | collective-permute-start | bytes 147464 | tf_op jit(solution)/shard_map/ppermute | solution.py:488
  50.4 0.5 collective-permute-done.14
  50.9 1.7 %collective-permute-done.13 = f32[2,16,384]{2,1,0:T(8,128)S(1)} collective-permute-done((f32[2,16,384]{2,1,0:T(8,128)S(1)}, f32[2,16,384]{2,1,0:T(8,128)S(1)}, u32[]{:S(2)}, u32[]{:S(2)}) %collective-permute-start.13) | collective-permute-done | bytes 49184 | tf_op jit(solution)/shard_map/ppermute | solution.py:488
  52.6 0.5 collective-permute-done.12
  53.5 1.1 %collective-permute-done.15.refs_0_ = f32[8,16,384]{2,1,0:T(8,128)S(1)} collective-permute-done((f32[8,16,384]{2,1,0:T(8,128)S(1)}, f32[8,16,384]{2,1,0:T(8,128)S(1)}, u32[]{:S(2)}, u32[]{:S(2)}) %collective-permute-start.15) | collective-permute-done | bytes 196640 | tf_op jit(solution)/shard_map/ppermute | solution.py:488
  54.6 1.0 %shard_map.106 = f32[16,1024]{1,0:T(8,128)} custom-call(f32[8,16,384]{2,1,0:T(8,128)S(1)} %collective-permute-done.15.refs_0_, f32[16,1024]{1,0:T(8,128)S(1)} %shard_map.105.refs_1_), custom_call_target="tpu_custom_call" | custom-call | bytes 196608 | tf_op jit(solution)/shard_map/pallas_call | solution.py:445
  (23 shorter events, 1.6 us)
Async XLA Ops:
  0.6 6.8 %collective-permute-start = (bf16[1,16,1024]{2,1,0:T(8,128)(2,1)}, bf16[1,16,1024]{2,1,0:T(8,128)(2,1)S(1)}, u32[]{:S(2)}, u32[]{:S(2)}) collective-permute-start(bf16[1,16,1024]{2,1,0:T(8,128)(2,1)} %bitcast.19), channel_id=1, source_target_pairs={{0,8},{1,9},{2,10},{3,11},{4,12},{5,13},{6,14},{7,15},{8,0},{9,1},... | collective-permute-start | bytes 98312 | tf_op jit(solution)/shard_map/ppermute | solution.py:488
  7.5 7.1 %collective-permute-start.3 = (bf16[2,16,1024]{2,1,0:T(8,128)(2,1)S(1)}, bf16[2,16,1024]{2,1,0:T(8,128)(2,1)S(1)}, u32[]{:S(2)}, u32[]{:S(2)}) collective-permute-start(bf16[2,16,1024]{2,1,0:T(8,128)(2,1)S(1)} %pad_maximum_fusion.2), channel_id=1, source_target_pairs={{0,4},{1,5},{2,6},{3,7},{4,0},{5,1},{6,2},{7,3},{8,12},{9,13},{10,... | collective-permute-start | bytes 196616 | tf_op jit(solution)/shard_map/ppermute | solution.py:488
  9.1 5.5 %collective-permute-start.2 = (bf16[2,16,1024]{2,1,0:T(8,128)(2,1)S(1)}, bf16[2,16,1024]{2,1,0:T(8,128)(2,1)S(1)}, u32[]{:S(2)}, u32[]{:S(2)}) collective-permute-start(bf16[2,16,1024]{2,1,0:T(8,128)(2,1)S(1)} %pad_maximum_fusion.2), channel_id=1, source_target_pairs={{0,6},{1,7},{2,4},{3,5},{4,2},{5,3},{6,0},{7,1},{8,14},{9,15},{10,... | collective-permute-start | bytes 196616 | tf_op jit(solution)/shard_map/ppermute | solution.py:488
  10.5 4.5 %collective-permute-start.1 = (bf16[2,16,1024]{2,1,0:T(8,128)(2,1)S(1)}, bf16[2,16,1024]{2,1,0:T(8,128)(2,1)S(1)}, u32[]{:S(2)}, u32[]{:S(2)}) collective-permute-start(bf16[2,16,1024]{2,1,0:T(8,128)(2,1)S(1)} %pad_maximum_fusion.2), channel_id=1, source_target_pairs={{0,2},{1,3},{2,0},{3,1},{4,6},{5,7},{6,4},{7,5},{8,10},{9,11},{10,... | collective-permute-start | bytes 196616 | tf_op jit(solution)/shard_map/ppermute | solution.py:488
  15.0 1.6 %collective-permute-start.4 = (bf16[8,16,1024]{2,1,0:T(8,128)(2,1)S(1)}, bf16[8,16,1024]{2,1,0:T(8,128)(2,1)S(1)}, u32[]{:S(2)}, u32[]{:S(2)}) collective-permute-start(bf16[8,16,1024]{2,1,0:T(8,128)(2,1)S(1)} %pad_maximum_fusion.coef_a), channel_id=1, source_target_pairs={{0,1},{1,0},{2,3},{3,2},{4,5},{5,4},{6,7},{7,6},{8,9},{9,8},{10,11... | collective-permute-start | bytes 786440 | tf_op jit(solution)/shard_map/ppermute | solution.py:488
  16.7 19.5 %copy-start = (f32[64]{0:T(128)S(1)}, f32[64]{0:T(128)}, u32[]{:S(2)}) copy-start(f32[64]{0:T(128)} %param.14) | copy-start | bytes 772
  20.1 1.5 %collective-permute-start.5 = (f32[136,128]{1,0:T(8,128)S(1)}, f32[136,128]{1,0:T(8,128)S(1)}, u32[]{:S(2)}, u32[]{:S(2)}) collective-permute-start(f32[136,128]{1,0:T(8,128)S(1)} %get-tuple-element.30), channel_id=1, source_target_pairs={{0,1},{1,0},{2,3},{3,2},{4,5},{5,4},{6,7},{7,6},{8,9},{9,8},{10,11... | collective-permute-start | bytes 208904 | tf_op jit(solution)/shard_map/ppermute | solution.py:488
  21.6 4.5 %collective-permute-start.8 = (f32[136,128]{1,0:T(8,128)S(1)}, f32[136,128]{1,0:T(8,128)S(1)}, u32[]{:S(2)}, u32[]{:S(2)}) collective-permute-start(f32[136,128]{1,0:T(8,128)S(1)} %add.15), channel_id=1, source_target_pairs={{0,4},{1,5},{2,6},{3,7},{4,0},{5,1},{6,2},{7,3},{8,12},{9,13},{10,... | collective-permute-start | bytes 208904 | tf_op jit(solution)/shard_map/ppermute | solution.py:488
  23.0 5.3 %collective-permute-start.7 = (f32[136,128]{1,0:T(8,128)S(1)}, f32[136,128]{1,0:T(8,128)S(1)}, u32[]{:S(2)}, u32[]{:S(2)}) collective-permute-start(f32[136,128]{1,0:T(8,128)S(1)} %add.15), channel_id=1, source_target_pairs={{0,6},{1,7},{2,4},{3,5},{4,2},{5,3},{6,0},{7,1},{8,14},{9,15},{10,... | collective-permute-start | bytes 208904 | tf_op jit(solution)/shard_map/ppermute | solution.py:488
  24.3 5.3 %collective-permute-start.6 = (f32[136,128]{1,0:T(8,128)S(1)}, f32[136,128]{1,0:T(8,128)S(1)}, u32[]{:S(2)}, u32[]{:S(2)}) collective-permute-start(f32[136,128]{1,0:T(8,128)S(1)} %add.15), channel_id=1, source_target_pairs={{0,2},{1,3},{2,0},{3,1},{4,6},{5,7},{6,4},{7,5},{8,10},{9,11},{10,... | collective-permute-start | bytes 208904 | tf_op jit(solution)/shard_map/ppermute | solution.py:488
  29.6 6.5 %collective-permute-start.9 = (f32[136,128]{1,0:T(8,128)S(1)}, f32[136,128]{1,0:T(8,128)S(1)}, u32[]{:S(2)}, u32[]{:S(2)}) collective-permute-start(f32[136,128]{1,0:T(8,128)S(1)} %add_add_fusion), channel_id=1, source_target_pairs={{0,8},{1,9},{2,10},{3,11},{4,12},{5,13},{6,14},{7,15},{8,0},{9,1},... | collective-permute-start | bytes 208904 | tf_op jit(solution)/shard_map/ppermute | solution.py:488
  36.1 1.3 %collective-permute-start.10 = (f32[136,128]{1,0:T(8,128)S(1)}, f32[136,128]{1,0:T(8,128)S(1)}, u32[]{:S(2)}, u32[]{:S(2)}) collective-permute-start(f32[136,128]{1,0:T(8,128)S(1)} %add.19.packed), channel_id=1, source_target_pairs={{0,1},{1,0},{2,3},{3,2},{4,5},{5,4},{6,7},{7,6},{8,9},{9,8},{10,11... | collective-permute-start | bytes 208904 | tf_op jit(solution)/shard_map/ppermute | solution.py:488
  42.0 4.8 %collective-permute-start.11 = (f32[1,16,384]{2,1,0:T(8,128)S(1)}, f32[1,16,384]{2,1,0:T(8,128)S(1)}, u32[]{:S(2)}, u32[]{:S(2)}) collective-permute-start(f32[1,16,384]{2,1,0:T(8,128)S(1)} %bitcast.10), channel_id=1, source_target_pairs={{0,8},{1,9},{2,10},{3,11},{4,12},{5,13},{6,14},{7,15},{8,0},{9,1},... | collective-permute-start | bytes 73736 | tf_op jit(solution)/shard_map/ppermute | solution.py:488
  46.8 4.1 %collective-permute-start.14 = (f32[2,16,384]{2,1,0:T(8,128)S(1)}, f32[2,16,384]{2,1,0:T(8,128)S(1)}, u32[]{:S(2)}, u32[]{:S(2)}) collective-permute-start(f32[2,16,384]{2,1,0:T(8,128)S(1)} %pad_maximum_fusion.3), channel_id=1, source_target_pairs={{0,4},{1,5},{2,6},{3,7},{4,0},{5,1},{6,2},{7,3},{8,12},{9,13},{10,... | collective-permute-start | bytes 147464 | tf_op jit(solution)/shard_map/ppermute | solution.py:488
  47.6 5.0 %collective-permute-start.13 = (f32[2,16,384]{2,1,0:T(8,128)S(1)}, f32[2,16,384]{2,1,0:T(8,128)S(1)}, u32[]{:S(2)}, u32[]{:S(2)}) collective-permute-start(f32[2,16,384]{2,1,0:T(8,128)S(1)} %pad_maximum_fusion.3), channel_id=1, source_target_pairs={{0,6},{1,7},{2,4},{3,5},{4,2},{5,3},{6,0},{7,1},{8,14},{9,15},{10,... | collective-permute-start | bytes 147464 | tf_op jit(solution)/shard_map/ppermute | solution.py:488
  48.8 4.3 %collective-permute-start.12 = (f32[2,16,384]{2,1,0:T(8,128)S(1)}, f32[2,16,384]{2,1,0:T(8,128)S(1)}, u32[]{:S(2)}, u32[]{:S(2)}) collective-permute-start(f32[2,16,384]{2,1,0:T(8,128)S(1)} %pad_maximum_fusion.3), channel_id=1, source_target_pairs={{0,2},{1,3},{2,0},{3,1},{4,6},{5,7},{6,4},{7,5},{8,10},{9,11},{10,... | collective-permute-start | bytes 147464 | tf_op jit(solution)/shard_map/ppermute | solution.py:488
  53.1 1.5 %collective-permute-start.15 = (f32[8,16,384]{2,1,0:T(8,128)S(1)}, f32[8,16,384]{2,1,0:T(8,128)S(1)}, u32[]{:S(2)}, u32[]{:S(2)}) collective-permute-start(f32[8,16,384]{2,1,0:T(8,128)S(1)} %pad_maximum_fusion.1), channel_id=1, source_target_pairs={{0,1},{1,0},{2,3},{3,2},{4,5},{5,4},{6,7},{7,6},{8,9},{9,8},{10,11... | collective-permute-start | bytes 589832 | tf_op jit(solution)/shard_map/ppermute | solution.py:488

commit v3 on v2

--- a/solution.py
+++ b/solution.py
@@ -15,6 +15,9 @@
 TILES = BW * BW // LANES
 ROWS = S * TILES
 PARTS = 3
+SEAT = 8
+SEATS = LANES // SEAT
+TERM_TILES = -(-S * BW // LANES)
 F32 = jnp.float32
 BF16 = jnp.bfloat16
 VMEM = pl.BlockSpec(memory_space=pltpu.VMEM)
@@ -31,7 +34,7 @@
 
 def split_rows(count):
     unit = count // 16
-    return (3 * unit, 11 * unit, count - 14 * unit)
+    return (unit, 13 * unit, count - 14 * unit)
 
 
 def retile_rows(x, out, at):
@@ -151,8 +154,8 @@
     return place
 
 
-def half_kernel(steps, ids, coef_a, coef_b, *refs):
-    slabs, (half, send, scr) = refs[:PARTS], refs[PARTS:]
+def half_kernel(steps, ids, id_row, coef_a, coef_b, *refs):
+    slabs, (half, send) = refs[:PARTS], refs[PARTS:]
     me = lax.axis_index("aux")
     orbs, width = coef_a.shape[1], coef_a.shape[2]
     per_dev = width // BW
@@ -187,24 +190,22 @@
             coef[h][tile] = jnp.where(hit, there, coef[h][tile])
     coef = jnp.concatenate([jnp.concatenate(coef[h], axis=1)[:, :ROWS] for h in range(HALVES)], axis=0).astype(BF16)
     low = iota((orbs, LANES), 1) < BW
-    pairs = half.shape[1]
     base = 0
+    rows = []
     for slab in slabs:
         for p in range(slab.shape[0] // 2):
             both = jnp.concatenate([slab[2 * p], slab[2 * p + 1]], axis=1)
             r = jnp.dot(coef, both, preferred_element_type=F32)
             straight = jnp.where(low, r[:orbs, :LANES], r[orbs:, LANES:])
             crossed = jnp.where(low, r[:orbs, LANES:], r[orbs:, :LANES])
-            row = straight + pltpu.roll(crossed, BW, 1)
-            for g in range(orbs // 8):
-                scr[pl.ds(g * 8 * pairs + base + p, 8, stride=pairs), :] = row[g * 8 : g * 8 + 8]
-        base += slab.shape[0] // 2
-    for i in range(orbs):
-        half[i] = scr[i * pairs : (i + 1) * pairs, :].astype(BF16)
-    pair_squares(half, 1 - lax.rem(me, 2), send)
-
-
-def pair_squares(half, core, out):
+            rows.append(straight + pltpu.roll(crossed, BW, 1))
+            if len(rows) == 16:
+                half[:, base : base + 16, :] = jnp.swapaxes(jnp.stack(rows), 0, 1).astype(BF16)
+                base, rows = base + 16, []
+    pair_squares(half, 1 - lax.rem(me, 2), id_row, send)
+
+
+def pair_squares(half, core, id_row, out):
     orbs, pairs = half.shape[0], half.shape[1]
     scale = 0.125 / (2 * pairs * lax.axis_size("aux"))
     lane = iota((BW, LANES), 1)
@@ -224,41 +225,41 @@
         b = jnp.where(left, lefts[1], rights[1])
         out[k * BW : (k + 1) * BW, :] = jnp.where(upper, a, b)
         diags.append(jnp.sum(jnp.where(eye, b, 0.0), axis=0, keepdims=True))
+    me = lax.axis_index("aux")
     spare = out.shape[0] - quads * BW - quads
-    if spare:
-        diags.append(jnp.zeros((spare, LANES), F32))
+    own = pltpu.roll((id_row[...] + 1).astype(F32), lax.rem(me, SEATS) * SEAT, 1)
+    diags.append(jnp.where(iota((spare, LANES), 0) == lax.div(me, SEATS), own, 0.0))
     out[quads * BW :, :] = jnp.concatenate(diags, axis=0)
 
 
-def own_kernel(half, out):
-    pair_squares(half, lax.rem(lax.axis_index("aux"), 2), out)
-
-
-def own_squares(half, like):
+def own_kernel(half, id_row, out):
+    pair_squares(half, lax.rem(lax.axis_index("aux"), 2), id_row, out)
+
+
+def own_squares(half, ids, like):
     return pl.pallas_call(
         own_kernel,
-        in_specs=[VMEM],
+        in_specs=[VMEM] * 2,
         out_specs=VMEM,
         out_shape=jax.ShapeDtypeStruct(like.shape, F32),
         compiler_params=pltpu.CompilerParams(vmem_limit_bytes=4 * 2**20),
         cost_estimate=pl.CostEstimate(flops=0, bytes_accessed=2 * 2**20, transcendentals=0),
-    )(half)
+    )(half, ids)
 
 
 def half_transform(steps, ids, coef_a, coef_b, slabs):
     orbs = coef_a.shape[1]
     pairs = sum(s.shape[0] for s in slabs) // 2
     quads = orbs // 8
-    rows = quads * BW + -(-quads // 8) * 8
+    rows = quads * BW + -(-(quads + -(-lax.axis_size("aux") // SEATS)) // 8) * 8
     packed = jax.ShapeDtypeStruct((rows, LANES), F32)
     return pl.pallas_call(
         functools.partial(half_kernel, steps),
-        in_specs=[SMEM, VMEM, VMEM] + [VMEM] * PARTS,
+        in_specs=[SMEM] + [VMEM] * (3 + PARTS),
         out_specs=[VMEM] * 2,
         out_shape=[jax.ShapeDtypeStruct((orbs, pairs, LANES), BF16), packed],
-        scratch_shapes=[pltpu.VMEM((orbs * pairs, LANES), F32)],
         compiler_params=pltpu.CompilerParams(vmem_limit_bytes=limit(orbs)),
-    )(ids, coef_a, coef_b, *slabs)
+    )(ids, ids, coef_a, coef_b, *slabs)
 
 
 def weight_rows(packed, core, levels, vir, half, energy, weights):
@@ -321,7 +322,7 @@
     )(packed, levels, vir, half)
 
 
-def grad_kernel(ids, packed, levels, vir, half, own_energy, own, *refs):
+def grad_kernel(packed, levels, vir, half, own_energy, own, *refs):
     slabs, (terms, energy, other_energy, other, mixed) = refs[:PARTS], refs[PARTS:]
     core = lax.rem(lax.axis_index("aux"), 2)
     orbs, pairs = half.shape[0], half.shape[1]
@@ -359,7 +360,7 @@
                 preferred_element_type=F32,
             )
         base += slab.shape[0] // 2
-    width = terms.shape[1]
+    width = mixed.shape[0]
     turn = total if HALVES * orbs > LANES else jnp.pad(total, ((0, 0), (0, LANES - HALVES * orbs)))
     for h in range(HALVES):
         rows = turn[:, h * orbs : h * orbs + LANES]
@@ -370,59 +371,82 @@
     for t in range(width // LANES):
         out = mixed[t * LANES : (t + 1) * LANES, :].T[:orbs]
         out = ordered(out[:mid], out[mid:])
-        place = iota((orbs, LANES), 1) + (t * LANES - S * BW)
-        for s in range(S):
-            if t * LANES <= S * BW + s < (t + 1) * LANES:
-                out = jnp.where(place == s, ids[0, s].astype(F32), out)
-        terms[:, t * LANES : (t + 1) * LANES] = out
-
-
-def gradient_terms(ids, packed, levels, vir, half, own_energy, own, slabs):
+        if (t + 1) * LANES > S * BW:
+            out = jnp.where(low[:mid], out[:mid], pltpu.roll(out[mid:], BW, 1))
+        terms[t * orbs : t * orbs + out.shape[0], :] = out
+
+
+def gradient_terms(packed, levels, vir, half, own_energy, own, slabs):
     orbs, pairs = half.shape[0], half.shape[1]
-    width = -(-(S * BW + S) // LANES) * LANES
+    width = -(-S * BW // LANES) * LANES
     return pl.pallas_call(
         grad_kernel,
-        in_specs=[SMEM] + [VMEM] * 6 + [VMEM] * PARTS,
+        in_specs=[VMEM] * (6 + PARTS),
         out_specs=[VMEM] * 2,
-        out_shape=[jax.ShapeDtypeStruct((orbs, width), F32), jax.ShapeDtypeStruct((orbs, LANES), F32)],
+        out_shape=[jax.ShapeDtypeStruct((orbs * S * BW // LANES, LANES), F32), jax.ShapeDtypeStruct((orbs, LANES), F32)],
         scratch_shapes=[
             pltpu.VMEM(own_energy.shape, F32),
             pltpu.VMEM(own.shape, F32),
             pltpu.VMEM((width, LANES), F32),
         ],
         compiler_params=pltpu.CompilerParams(vmem_limit_bytes=limit(orbs)),
-    )(ids, packed, levels, vir, half, own_energy, own, *slabs)
-
-
-def place_kernel(*refs):
-    piece, out = refs[0], refs[-1]
+    )(packed, levels, vir, half, own_energy, own, *slabs)
+
+
+def seat_kernel(start, per_dev, rels, packed, out):
     me = lax.axis_index("aux")
+    side = jnp.where(iota((1, LANES), 1) < BW, 0, 1)
+    for d, rel in enumerate(rels):
+        dev = lax.bitwise_xor(me, rel)
+        row = packed[pl.ds(start + lax.div(dev, SEATS), 1), :]
+        row = pltpu.roll(row, lax.rem(SEATS - lax.rem(dev, SEATS), SEATS) * SEAT, 1)
+        row = row.astype(jnp.int32) - (1 + me * per_dev)
+        ids = [jnp.broadcast_to(row[:, s : s + 1], (1, LANES)) for s in range(2 * TERM_TILES)]
+        for k in range(TERM_TILES):
+            one, two = ids[2 * k], ids[2 * k + 1]
+            out[d * SEAT + 2 * k : d * SEAT + 2 * k + 1, :] = jnp.where(side == 0, one, two) - side
+            out[d * SEAT + 2 * k + 1 : d * SEAT + 2 * k + 2, :] = jnp.where(side == 0, two, one) - side
+
+
+def seats(packed, orbs, rows, rels):
+    start = orbs // 8 * (BW + 1)
+    return pl.pallas_call(
+        functools.partial(seat_kernel, start, rows // BW, rels),
+        in_specs=[VMEM],
+        out_specs=VMEM,
+        out_shape=jax.ShapeDtypeStruct((len(rels) * SEAT, LANES), jnp.int32),
+        compiler_params=pltpu.CompilerParams(vmem_limit_bytes=2 * 2**20),
+        cost_estimate=pl.CostEstimate(flops=0, bytes_accessed=2**20, transcendentals=0),
+    )(packed)
+
+
+def place_kernel(base, piece, spots, *refs):
+    out = refs[-1]
     orbs, width = out.shape
-    per_dev = width // BW
+    mid = orbs // 2
     step_tiles = range(width // LANES)
-    lane = iota((8, LANES), 1)
-    side = jnp.where(lane < BW, 0, 1)
-    tiles = S * BW // LANES + 1
-    start = S * BW - (tiles - 1) * LANES
-    groups = [slice(g, min(g + 16, orbs)) for g in range(0, orbs, 16)]
-    for rows in groups:
-        parts = [slice(r, r + 8) for r in range(rows.start, rows.stop, 8)]
-        if len(refs) == 3:
-            total = [[refs[1][r, t * LANES : (t + 1) * LANES] for t in step_tiles] for r in parts]
+    for first in range(0, orbs, 16):
+        parts = [slice(r, r + 8) for r in range(first, min(first + 16, orbs), 8)]
+        if len(refs) == 2:
+            total = [[refs[0][r, t * LANES : (t + 1) * LANES] for t in step_tiles] for r in parts]
         else:
             total = [[jnp.zeros((8, LANES), F32) for _ in step_tiles] for _ in parts]
 
         def step(d, total, parts=parts):
             total = [list(row) for row in total]
-            tail = piece[d, 0:8, (tiles - 1) * LANES : tiles * LANES]
-            ids = [jnp.broadcast_to(tail[:, start + s : start + s + 1], (8, LANES)) for s in range(S)]
-            ids = [i.astype(jnp.int32) - me * per_dev for i in ids]
-            ids = ids + [jnp.full((8, LANES), -1, jnp.int32)] * (2 * tiles - S)
-            for k in range(tiles):
-                spot = jnp.where(side == 0, ids[2 * k], ids[2 * k + 1]) - side
-                turn_spot = jnp.where(side == 0, ids[2 * k + 1], ids[2 * k]) - side
-                values = [piece[d, r, k * LANES : (k + 1) * LANES] for r in parts]
-                turns = [pltpu.roll(v, BW, 1) for v in values]
+            for k in range(TERM_TILES):
+                at = (base + d) * SEAT + 2 * k
+                spot = jnp.broadcast_to(spots[pl.ds(at, 1), :], (8, LANES))
+                turn_spot = jnp.broadcast_to(spots[pl.ds(at + 1, 1), :], (8, LANES))
+                values, turns = [], []
+                for r in parts:
+                    half = (k + 1) * LANES > S * BW
+                    swapped = half and r.start >= mid
+                    start = k * orbs + r.start - (mid if swapped else 0)
+                    value = piece[d, start : start + 8, :]
+                    turn = pltpu.roll(value, BW, 1)
+                    values.append(turn if swapped else value)
+                    turns.append(value if swapped else turn)
                 for t in step_tiles:
                     here, there = spot == HALVES * t, turn_spot == HALVES * t
                     for r in range(len(parts)):
@@ -440,13 +464,13 @@
                 out[part, t * LANES : (t + 1) * LANES] = total[r][t]
 
 
-def place_terms(piece, total, rows):
-    args = (piece,) if total is None else (piece, total)
-    return pl.pallas_call(
-        place_kernel,
+def place_terms(base, piece, spots, total, orbs, rows):
+    args = (piece, spots) if total is None else (piece, spots, total)
+    return pl.pallas_call(
+        functools.partial(place_kernel, base),
         in_specs=[VMEM] * len(args),
         out_specs=VMEM,
-        out_shape=jax.ShapeDtypeStruct((piece.shape[1], rows), F32),
+        out_shape=jax.ShapeDtypeStruct((orbs, rows), F32),
         compiler_params=pltpu.CompilerParams(vmem_limit_bytes=8 * 2**20),
         cost_estimate=pl.CostEstimate(flops=0, bytes_accessed=4 * piece.size, transcendentals=0),
     )(*args)
@@ -511,25 +535,32 @@
     far = swap(buf, 1)
     slabs.append(retile(x, 2))
     half, send = half_transform(steps + ((1,),), ids, buf, far, slabs)
-    keep = own_squares(half, send) + swap(send, 1)
+    keep = own_squares(half, ids, send) + swap(send, 1)
     for step in reversed(steps):
         keep = sum([swap(keep, mask) for mask in step], keep)
     other = swap(keep, 1)
     vir = vir_energy.reshape(1, -1)
     own_energy, own = own_weights(keep, levels, vir, half)
-    terms, energy = gradient_terms(ids, other, levels, vir, half, own_energy, own, slabs)
+    rels = [0]
+    for step in steps + ((1,),):
+        rels = rels + [rel ^ mask for mask in step for rel in rels]
+    orbs = owner_map.shape[0]
+    spots = seats(keep, orbs, local_rows, tuple(rels))
+    other, spots = lax.optimization_barrier((other, spots))
+    terms, energy = gradient_terms(other, levels, vir, half, own_energy, own, slabs)
     buf, total, done = terms[None], None, 0
     for k, step in enumerate(steps):
         far = [swap(buf, mask) for mask in step]
-        if k == 0:
+        total = place_terms(done, buf[done:], spots, total, orbs, local_rows)
+        if k + 1 == len(steps):
             pair_energy = pair_slots(owner_map, energy)
-        total = place_terms(buf[done:], total, local_rows)
+            total, pair_energy = lax.optimization_barrier((total, pair_energy))
         done = buf.shape[0]
         buf = jnp.concatenate([buf] + far, axis=0)
-        buf, total, pair_energy = lax.optimization_barrier((buf, total, pair_energy))
+        buf, total = lax.optimization_barrier((buf, total))
     far = swap(buf, 1)
-    total = place_terms(buf[done:], total, local_rows)
-    grad_coef = place_terms(far, total, local_rows).T
+    total = place_terms(done, buf[done:], spots, total, orbs, local_rows)
+    grad_coef = place_terms(buf.shape[0], far, spots, total, orbs, local_rows).T
     return (grad_coef, pair_energy)
 
 

time: 55.8 us -> 53.7 us (0.962)
  waiting for transfers between devices: 15.8 us -> 13.9 us
  Pallas kernels: 19 us -> 18.1 us
  starting transfers between devices: 19.3 us -> 19.9 us
    ppermute x16, waiting for transfers between devices: 15.8 us -> 13.9 us  [swap(): return lax.ppermute(x, 'aux', [(i, i ^ mask) for i in range(size)])]
    pallas_call x7 -> x8, Pallas kernels: 9.82 us -> 8.99 us  [the longest x1 3.95 us: gradient_terms(): pl.pallas_call(grad_kernel, in_specs=[VMEM] * (6 + PARTS), out_specs=[VME...]
  transfers between devices with their start and end apart: 16 -> 16, of which waited for: 12 -> 10; matrix products, arithmetic and copies ran while one was open for 0% -> 0% of each run, Pallas kernels for 18% -> 19%
where the time goes in v3:
time: 53.7 us; the launch traced here: 53.6 us
  starting transfers between devices  19.9 us (37%)
  Pallas kernels  18.1 us (34%)
  waiting for transfers between devices  13.9 us (26%)
  between operations  1.49 us (3%)
    ppermute x16, starting transfers between devices, swap(): return lax.ppermute(x, 'aux', [(i, i ^ mask) for i in range(size)])  19.9 us
    ppermute x16, waiting for transfers between devices, swap(): return lax.ppermute(x, 'aux', [(i, i ^ mask) for i in range(size)])  13.9 us
    pallas_call x2, Pallas kernels, retile(): pl.pallas_call(functools.partial(retile_kernel, start), in_specs=[pl.Bloc...  5.56 us
    pallas_call x1, Pallas kernels, gradient_terms(): pl.pallas_call(grad_kernel, in_specs=[VMEM] * (6 + PARTS), out_specs=[VME...  3.95 us
    pallas_call x1, Pallas kernels, half_transform(): pl.pallas_call(functools.partial(half_kernel, steps), in_specs=[SMEM] + [...  2.95 us
    pallas_call x1, Pallas kernels, prepare(): pl.pallas_call(prepare_kernel, in_specs=[far, VMEM, far, far, far, far],...  1.66 us
    pallas_call x1, Pallas kernels, pair_slots(): pl.pallas_call(pair_kernel, in_specs=[pl.BlockSpec(memory_space=pltpu.HBM...  1.46 us
    pallas_call x4, Pallas kernels, place_terms(): pl.pallas_call(functools.partial(place_kernel, base), in_specs=[VMEM] * l...  1.36 us
  transfers between devices with their start and end apart: 16, of which 10 were waited for; matrix products, arithmetic and copies ran while one was open for 0% of the time, Pallas kernels for 19%

profile of v3, /device:TPU:0, one launch (start us, length us, event | category | flops | bytes accessed | tf_op | source)
XLA Modules:
  0.0 53.6 jit_solution(16819327956315322593)
XLA Ops:
  0.6 4.1 %collective-permute-start = (bf16[1,16,1024]{2,1,0:T(8,128)(2,1)}, bf16[1,16,1024]{2,1,0:T(8,128)(2,1)S(1)}, u32[]{:S(2)}, u32[]{:S(2)}) collective-permute-start(bf16[1,16,1024]{2,1,0:T(8,128)(2,1)} %bitcast.19), channel_id=1, source_target_pairs={{0,8},{1,9},{2,10},{3,11},{4,12},{5,13},{6,14},{7,15},{8,0},{9,1},... | collective-permute-start | bytes 98312 | tf_op jit(solution)/shard_map/ppermute | solution.py:512
  5.4 1.7 %shard_map.95 = (f32[16,128]{1,0:T(8,128)S(1)}, s32[1,128]{1,0:T(1,128)S(1)}, bf16[1,16,1024]{2,1,0:T(8,128)(2,1)S(1)}, bf16[16,160,128]{2,1,0:T(8,128)(2,1)S(1)}) custom-call(s32[1,5]{1,0:T(1,128)} %blocks.1, s32[1,1]{1,0:T(1,128)} %bitcast.9.counts, s32[16]{0:T(128)} %index.1, f32[8,128]{1,0:T(8,128)} %bitcast.21, bf16[1,16,1024]{2,1,0:T(8,128)(2,1)} %bitcast.20, ...), custom_call_target="tpu_custom_call" | custom-call | bytes 1310720 | tf_op jit(solution)/shard_map/pallas_call | solution.py:109
  7.2 1.8 %collective-permute-start.1 = (bf16[2,16,1024]{2,1,0:T(8,128)(2,1)S(1)}, bf16[2,16,1024]{2,1,0:T(8,128)(2,1)S(1)}, u32[]{:S(2)}, u32[]{:S(2)}) collective-permute-start(bf16[2,16,1024]{2,1,0:T(8,128)(2,1)S(1)} %pad_maximum_fusion.2), channel_id=1, source_target_pairs={{0,2},{1,3},{2,0},{3,1},{4,6},{5,7},{6,4},{7,5},{8,10},{9,11},{10,... | collective-permute-start | bytes 196616 | tf_op jit(solution)/shard_map/ppermute | solution.py:512
  9.0 1.3 %collective-permute-start.2 = (bf16[2,16,1024]{2,1,0:T(8,128)(2,1)S(1)}, bf16[2,16,1024]{2,1,0:T(8,128)(2,1)S(1)}, u32[]{:S(2)}, u32[]{:S(2)}) collective-permute-start(bf16[2,16,1024]{2,1,0:T(8,128)(2,1)S(1)} %pad_maximum_fusion.2), channel_id=1, source_target_pairs={{0,6},{1,7},{2,4},{3,5},{4,2},{5,3},{6,0},{7,1},{8,14},{9,15},{10,... | collective-permute-start | bytes 196616 | tf_op jit(solution)/shard_map/ppermute | solution.py:512
  10.3 0.5 collective-permute-start.3
  10.8 4.0 %shard_map.96.refs_1_ = bf16[208,160,128]{2,1,0:T(8,128)(2,1)S(1)} custom-call(bf16[5,256,4096]{2,1,0:T(8,128)(2,1)} %bitcast.16), custom_call_target="tpu_custom_call" | custom-call | bytes 17039360 | tf_op jit(solution)/shard_map/pallas_call | solution.py:63
  14.9 1.5 %shard_map.97.refs_2_ = bf16[32,160,128]{2,1,0:T(8,128)(2,1)S(1)} custom-call(bf16[5,256,4096]{2,1,0:T(8,128)(2,1)} %bitcast.17), custom_call_target="tpu_custom_call" | custom-call | bytes 2621440 | tf_op jit(solution)/shard_map/pallas_call | solution.py:63
  16.5 3.0 %shard_map.98 = (bf16[16,128,128]{2,1,0:T(8,128)(2,1)S(1)}, f32[136,128]{1,0:T(8,128)S(1)}) custom-call(s32[1,128]{1,0:T(1,128)S(1)} %get-tuple-element.24.ids.id_row, s32[1,128]{1,0:T(1,128)S(1)} %get-tuple-element.24.ids.id_row, bf16[8,16,1024]{2,1,0:T(8,128)(2,1)S(1)} %pad_maximum_fusion.coef_a, bf16[8,16,1024]{2,1,0:T(8,128)(2,1)S(1)} %collective-permute-done.4.coef_b, ...), custom_call_target="tpu_custom_call" | custom-call | tf_op jit(solution)/shard_map/pallas_call | solution.py:256
  19.5 0.6 %collective-permute-start.5 = (f32[136,128]{1,0:T(8,128)S(1)}, f32[136,128]{1,0:T(8,128)S(1)}, u32[]{:S(2)}, u32[]{:S(2)}) collective-permute-start(f32[136,128]{1,0:T(8,128)S(1)} %get-tuple-element.32), channel_id=1, source_target_pairs={{0,1},{1,0},{2,3},{3,2},{4,5},{5,4},{6,7},{7,6},{8,9},{9,8},{10,11... | collective-permute-start | bytes 208904 | tf_op jit(solution)/shard_map/ppermute | solution.py:512
  20.0 0.3 shard_map.99
  20.4 0.6 %collective-permute-done.5 = f32[136,128]{1,0:T(8,128)S(1)} collective-permute-done((f32[136,128]{1,0:T(8,128)S(1)}, f32[136,128]{1,0:T(8,128)S(1)}, u32[]{:S(2)}, u32[]{:S(2)}) %collective-permute-start.5) | collective-permute-done | bytes 69664 | tf_op jit(solution)/shard_map/ppermute | solution.py:512
  20.9 1.8 %collective-permute-start.6 = (f32[136,128]{1,0:T(8,128)S(1)}, f32[136,128]{1,0:T(8,128)S(1)}, u32[]{:S(2)}, u32[]{:S(2)}) collective-permute-start(f32[136,128]{1,0:T(8,128)S(1)} %add.15), channel_id=1, source_target_pairs={{0,2},{1,3},{2,0},{3,1},{4,6},{5,7},{6,4},{7,5},{8,10},{9,11},{10,... | collective-permute-start | bytes 208904 | tf_op jit(solution)/shard_map/ppermute | solution.py:512
  22.7 1.3 %collective-permute-start.7 = (f32[136,128]{1,0:T(8,128)S(1)}, f32[136,128]{1,0:T(8,128)S(1)}, u32[]{:S(2)}, u32[]{:S(2)}) collective-permute-start(f32[136,128]{1,0:T(8,128)S(1)} %add.15), channel_id=1, source_target_pairs={{0,6},{1,7},{2,4},{3,5},{4,2},{5,3},{6,0},{7,1},{8,14},{9,15},{10,... | collective-permute-start | bytes 208904 | tf_op jit(solution)/shard_map/ppermute | solution.py:512
  24.0 0.5 collective-permute-start.8
  24.5 1.4 %collective-permute-done.6 = f32[136,128]{1,0:T(8,128)S(1)} collective-permute-done((f32[136,128]{1,0:T(8,128)S(1)}, f32[136,128]{1,0:T(8,128)S(1)}, u32[]{:S(2)}, u32[]{:S(2)}) %collective-permute-start.6) | collective-permute-done | bytes 69664 | tf_op jit(solution)/shard_map/ppermute | solution.py:512
  25.9 2.7 %collective-permute-done.7 = f32[136,128]{1,0:T(8,128)S(1)} collective-permute-done((f32[136,128]{1,0:T(8,128)S(1)}, f32[136,128]{1,0:T(8,128)S(1)}, u32[]{:S(2)}, u32[]{:S(2)}) %collective-permute-start.7) | collective-permute-done | bytes 69664 | tf_op jit(solution)/shard_map/ppermute | solution.py:512
  28.6 2.6 %collective-permute-start.9 = (f32[136,128]{1,0:T(8,128)S(1)}, f32[136,128]{1,0:T(8,128)S(1)}, u32[]{:S(2)}, u32[]{:S(2)}) collective-permute-start(f32[136,128]{1,0:T(8,128)S(1)} %add_add_fusion), channel_id=1, source_target_pairs={{0,8},{1,9},{2,10},{3,11},{4,12},{5,13},{6,14},{7,15},{8,0},{9,1},... | collective-permute-start | bytes 208904 | tf_op jit(solution)/shard_map/ppermute | solution.py:512
  31.2 3.5 %collective-permute-done.9 = f32[136,128]{1,0:T(8,128)S(1)} collective-permute-done((f32[136,128]{1,0:T(8,128)S(1)}, f32[136,128]{1,0:T(8,128)S(1)}, u32[]{:S(2)}, u32[]{:S(2)}) %collective-permute-start.9) | collective-permute-done | bytes 69664 | tf_op jit(solution)/shard_map/ppermute | solution.py:512
  34.7 0.4 shard_map.100.spots
  35.2 0.5 shard_map.101
  35.6 0.4 collective-permute-done.10.packed
  36.0 3.9 %shard_map.102 = (f32[40,128]{1,0:T(8,128)S(1)}, f32[16,128]{1,0:T(8,128)S(1)}) custom-call(f32[136,128]{1,0:T(8,128)S(1)} %collective-permute-done.10.packed, f32[16,128]{1,0:T(8,128)S(1)} %get-tuple-element.34.levels, f32[1,64]{1,0:T(1,128)S(1)} %bitcast.14, bf16[16,128,128]{2,1,0:T(8,128)(2,1)S(1)} %get-tuple-element.31.half, ...), custom_call_target="tpu_custom_call" | custom-call | tf_op jit(solution)/shard_map/pallas_call | solution.py:382
  39.9 1.8 %collective-permute-start.11 = (f32[1,40,128]{2,1,0:T(8,128)S(1)}, f32[1,40,128]{2,1,0:T(8,128)S(1)}, u32[]{:S(2)}, u32[]{:S(2)}) collective-permute-start(f32[1,40,128]{2,1,0:T(8,128)S(1)} %bitcast.10), channel_id=1, source_target_pairs={{0,8},{1,9},{2,10},{3,11},{4,12},{5,13},{6,14},{7,15},{8,0},{9,1},... | collective-permute-start | bytes 61448 | tf_op jit(solution)/shard_map/ppermute | solution.py:512
  41.9 2.9 %collective-permute-done.11 = f32[1,40,128]{2,1,0:T(8,128)S(1)} collective-permute-done((f32[1,40,128]{2,1,0:T(8,128)S(1)}, f32[1,40,128]{2,1,0:T(8,128)S(1)}, u32[]{:S(2)}, u32[]{:S(2)}) %collective-permute-start.11) | collective-permute-done | bytes 20512 | tf_op jit(solution)/shard_map/ppermute | solution.py:512
  44.8 1.4 %collective-permute-start.12 = (f32[2,40,128]{2,1,0:T(8,128)S(1)}, f32[2,40,128]{2,1,0:T(8,128)S(1)}, u32[]{:S(2)}, u32[]{:S(2)}) collective-permute-start(f32[2,40,128]{2,1,0:T(8,128)S(1)} %pad_maximum_fusion.3), channel_id=1, source_target_pairs={{0,2},{1,3},{2,0},{3,1},{4,6},{5,7},{6,4},{7,5},{8,10},{9,11},{10,... | collective-permute-start | bytes 122888 | tf_op jit(solution)/shard_map/ppermute | solution.py:512
  46.2 1.0 %collective-permute-start.13 = (f32[2,40,128]{2,1,0:T(8,128)S(1)}, f32[2,40,128]{2,1,0:T(8,128)S(1)}, u32[]{:S(2)}, u32[]{:S(2)}) collective-permute-start(f32[2,40,128]{2,1,0:T(8,128)S(1)} %pad_maximum_fusion.3), channel_id=1, source_target_pairs={{0,6},{1,7},{2,4},{3,5},{4,2},{5,3},{6,0},{7,1},{8,14},{9,15},{10,... | collective-permute-start | bytes 122888 | tf_op jit(solution)/shard_map/ppermute | solution.py:512
  47.1 1.1 %collective-permute-start.14 = (f32[2,40,128]{2,1,0:T(8,128)S(1)}, f32[2,40,128]{2,1,0:T(8,128)S(1)}, u32[]{:S(2)}, u32[]{:S(2)}) collective-permute-start(f32[2,40,128]{2,1,0:T(8,128)S(1)} %pad_maximum_fusion.3), channel_id=1, source_target_pairs={{0,4},{1,5},{2,6},{3,7},{4,0},{5,1},{6,2},{7,3},{8,12},{9,13},{10,... | collective-permute-start | bytes 122888 | tf_op jit(solution)/shard_map/ppermute | solution.py:512
  48.3 1.5 %shard_map.105 = f32[2]{0:T(128)} custom-call(s32[16]{0:T(128)} %owner.1, f32[16,128]{1,0:T(8,128)S(1)} %get-tuple-element.41.energy), custom_call_target="tpu_custom_call" | custom-call | bytes 1048576 | tf_op jit(solution)/shard_map/pallas_call | solution.py:499
  49.9 1.2 %collective-permute-done.13 = f32[2,40,128]{2,1,0:T(8,128)S(1)} collective-permute-done((f32[2,40,128]{2,1,0:T(8,128)S(1)}, f32[2,40,128]{2,1,0:T(8,128)S(1)}, u32[]{:S(2)}, u32[]{:S(2)}) %collective-permute-start.13) | collective-permute-done | bytes 40992 | tf_op jit(solution)/shard_map/ppermute | solution.py:512
  51.3 0.2 shard_map.106.refs_0_
  51.5 1.1 %collective-permute-done.15.piece = f32[8,40,128]{2,1,0:T(8,128)S(1)} collective-permute-done((f32[8,40,128]{2,1,0:T(8,128)S(1)}, f32[8,40,128]{2,1,0:T(8,128)S(1)}, u32[]{:S(2)}, u32[]{:S(2)}) %collective-permute-start.15) | collective-permute-done | bytes 163872 | tf_op jit(solution)/shard_map/ppermute | solution.py:512
  52.6 0.9 %shard_map.107 = f32[16,1024]{1,0:T(8,128)} custom-call(f32[8,40,128]{2,1,0:T(8,128)S(1)} %collective-permute-done.15.piece, s32[128,128]{1,0:T(8,128)S(1)} %shard_map.100.spots, f32[16,1024]{1,0:T(8,128)S(1)} %shard_map.106.refs_0_), custom_call_target="tpu_custom_call" | custom-call | bytes 163840 | tf_op jit(solution)/shard_map/pallas_call | solution.py:469
  (24 shorter events, 0.8 us)
Async XLA Ops:
  0.6 6.6 %collective-permute-start = (bf16[1,16,1024]{2,1,0:T(8,128)(2,1)}, bf16[1,16,1024]{2,1,0:T(8,128)(2,1)S(1)}, u32[]{:S(2)}, u32[]{:S(2)}) collective-permute-start(bf16[1,16,1024]{2,1,0:T(8,128)(2,1)} %bitcast.19), channel_id=1, source_target_pairs={{0,8},{1,9},{2,10},{3,11},{4,12},{5,13},{6,14},{7,15},{8,0},{9,1},... | collective-permute-start | bytes 98312 | tf_op jit(solution)/shard_map/ppermute | solution.py:512
  7.2 7.6 %collective-permute-start.1 = (bf16[2,16,1024]{2,1,0:T(8,128)(2,1)S(1)}, bf16[2,16,1024]{2,1,0:T(8,128)(2,1)S(1)}, u32[]{:S(2)}, u32[]{:S(2)}) collective-permute-start(bf16[2,16,1024]{2,1,0:T(8,128)(2,1)S(1)} %pad_maximum_fusion.2), channel_id=1, source_target_pairs={{0,2},{1,3},{2,0},{3,1},{4,6},{5,7},{6,4},{7,5},{8,10},{9,11},{10,... | collective-permute-start | bytes 196616 | tf_op jit(solution)/shard_map/ppermute | solution.py:512
  9.0 5.8 %collective-permute-start.2 = (bf16[2,16,1024]{2,1,0:T(8,128)(2,1)S(1)}, bf16[2,16,1024]{2,1,0:T(8,128)(2,1)S(1)}, u32[]{:S(2)}, u32[]{:S(2)}) collective-permute-start(bf16[2,16,1024]{2,1,0:T(8,128)(2,1)S(1)} %pad_maximum_fusion.2), channel_id=1, source_target_pairs={{0,6},{1,7},{2,4},{3,5},{4,2},{5,3},{6,0},{7,1},{8,14},{9,15},{10,... | collective-permute-start | bytes 196616 | tf_op jit(solution)/shard_map/ppermute | solution.py:512
  10.3 4.5 %collective-permute-start.3 = (bf16[2,16,1024]{2,1,0:T(8,128)(2,1)S(1)}, bf16[2,16,1024]{2,1,0:T(8,128)(2,1)S(1)}, u32[]{:S(2)}, u32[]{:S(2)}) collective-permute-start(bf16[2,16,1024]{2,1,0:T(8,128)(2,1)S(1)} %pad_maximum_fusion.2), channel_id=1, source_target_pairs={{0,4},{1,5},{2,6},{3,7},{4,0},{5,1},{6,2},{7,3},{8,12},{9,13},{10,... | collective-permute-start | bytes 196616 | tf_op jit(solution)/shard_map/ppermute | solution.py:512
  14.9 1.6 %collective-permute-start.4 = (bf16[8,16,1024]{2,1,0:T(8,128)(2,1)S(1)}, bf16[8,16,1024]{2,1,0:T(8,128)(2,1)S(1)}, u32[]{:S(2)}, u32[]{:S(2)}) collective-permute-start(bf16[8,16,1024]{2,1,0:T(8,128)(2,1)S(1)} %pad_maximum_fusion.coef_a), channel_id=1, source_target_pairs={{0,1},{1,0},{2,3},{3,2},{4,5},{5,4},{6,7},{7,6},{8,9},{9,8},{10,11... | collective-permute-start | bytes 786440 | tf_op jit(solution)/shard_map/ppermute | solution.py:512
  16.5 18.7 %copy-start = (f32[64]{0:T(128)S(1)}, f32[64]{0:T(128)}, u32[]{:S(2)}) copy-start(f32[64]{0:T(128)} %param.14) | copy-start | bytes 772
  19.5 1.5 %collective-permute-start.5 = (f32[136,128]{1,0:T(8,128)S(1)}, f32[136,128]{1,0:T(8,128)S(1)}, u32[]{:S(2)}, u32[]{:S(2)}) collective-permute-start(f32[136,128]{1,0:T(8,128)S(1)} %get-tuple-element.32), channel_id=1, source_target_pairs={{0,1},{1,0},{2,3},{3,2},{4,5},{5,4},{6,7},{7,6},{8,9},{9,8},{10,11... | collective-permute-start | bytes 208904 | tf_op jit(solution)/shard_map/ppermute | solution.py:512
  20.9 5.0 %collective-permute-start.6 = (f32[136,128]{1,0:T(8,128)S(1)}, f32[136,128]{1,0:T(8,128)S(1)}, u32[]{:S(2)}, u32[]{:S(2)}) collective-permute-start(f32[136,128]{1,0:T(8,128)S(1)} %add.15), channel_id=1, source_target_pairs={{0,2},{1,3},{2,0},{3,1},{4,6},{5,7},{6,4},{7,5},{8,10},{9,11},{10,... | collective-permute-start | bytes 208904 | tf_op jit(solution)/shard_map/ppermute | solution.py:512
  22.7 5.9 %collective-permute-start.7 = (f32[136,128]{1,0:T(8,128)S(1)}, f32[136,128]{1,0:T(8,128)S(1)}, u32[]{:S(2)}, u32[]{:S(2)}) collective-permute-start(f32[136,128]{1,0:T(8,128)S(1)} %add.15), channel_id=1, source_target_pairs={{0,6},{1,7},{2,4},{3,5},{4,2},{5,3},{6,0},{7,1},{8,14},{9,15},{10,... | collective-permute-start | bytes 208904 | tf_op jit(solution)/shard_map/ppermute | solution.py:512
  24.0 4.6 %collective-permute-start.8 = (f32[136,128]{1,0:T(8,128)S(1)}, f32[136,128]{1,0:T(8,128)S(1)}, u32[]{:S(2)}, u32[]{:S(2)}) collective-permute-start(f32[136,128]{1,0:T(8,128)S(1)} %add.15), channel_id=1, source_target_pairs={{0,4},{1,5},{2,6},{3,7},{4,0},{5,1},{6,2},{7,3},{8,12},{9,13},{10,... | collective-permute-start | bytes 208904 | tf_op jit(solution)/shard_map/ppermute | solution.py:512
  28.6 6.0 %collective-permute-start.9 = (f32[136,128]{1,0:T(8,128)S(1)}, f32[136,128]{1,0:T(8,128)S(1)}, u32[]{:S(2)}, u32[]{:S(2)}) collective-permute-start(f32[136,128]{1,0:T(8,128)S(1)} %add_add_fusion), channel_id=1, source_target_pairs={{0,8},{1,9},{2,10},{3,11},{4,12},{5,13},{6,14},{7,15},{8,0},{9,1},... | collective-permute-start | bytes 208904 | tf_op jit(solution)/shard_map/ppermute | solution.py:512
  34.7 1.3 %collective-permute-start.10 = (f32[136,128]{1,0:T(8,128)S(1)}, f32[136,128]{1,0:T(8,128)S(1)}, u32[]{:S(2)}, u32[]{:S(2)}) collective-permute-start(f32[136,128]{1,0:T(8,128)S(1)} %add.19.packed), channel_id=1, source_target_pairs={{0,1},{1,0},{2,3},{3,2},{4,5},{5,4},{6,7},{7,6},{8,9},{9,8},{10,11... | collective-permute-start | bytes 208904 | tf_op jit(solution)/shard_map/ppermute | solution.py:512
  39.9 4.9 %collective-permute-start.11 = (f32[1,40,128]{2,1,0:T(8,128)S(1)}, f32[1,40,128]{2,1,0:T(8,128)S(1)}, u32[]{:S(2)}, u32[]{:S(2)}) collective-permute-start(f32[1,40,128]{2,1,0:T(8,128)S(1)} %bitcast.10), channel_id=1, source_target_pairs={{0,8},{1,9},{2,10},{3,11},{4,12},{5,13},{6,14},{7,15},{8,0},{9,1},... | collective-permute-start | bytes 61448 | tf_op jit(solution)/shard_map/ppermute | solution.py:512
  44.8 5.1 %collective-permute-start.12 = (f32[2,40,128]{2,1,0:T(8,128)S(1)}, f32[2,40,128]{2,1,0:T(8,128)S(1)}, u32[]{:S(2)}, u32[]{:S(2)}) collective-permute-start(f32[2,40,128]{2,1,0:T(8,128)S(1)} %pad_maximum_fusion.3), channel_id=1, source_target_pairs={{0,2},{1,3},{2,0},{3,1},{4,6},{5,7},{6,4},{7,5},{8,10},{9,11},{10,... | collective-permute-start | bytes 122888 | tf_op jit(solution)/shard_map/ppermute | solution.py:512
  46.2 4.9 %collective-permute-start.13 = (f32[2,40,128]{2,1,0:T(8,128)S(1)}, f32[2,40,128]{2,1,0:T(8,128)S(1)}, u32[]{:S(2)}, u32[]{:S(2)}) collective-permute-start(f32[2,40,128]{2,1,0:T(8,128)S(1)} %pad_maximum_fusion.3), channel_id=1, source_target_pairs={{0,6},{1,7},{2,4},{3,5},{4,2},{5,3},{6,0},{7,1},{8,14},{9,15},{10,... | collective-permute-start | bytes 122888 | tf_op jit(solution)/shard_map/ppermute | solution.py:512
  47.1 4.0 %collective-permute-start.14 = (f32[2,40,128]{2,1,0:T(8,128)S(1)}, f32[2,40,128]{2,1,0:T(8,128)S(1)}, u32[]{:S(2)}, u32[]{:S(2)}) collective-permute-start(f32[2,40,128]{2,1,0:T(8,128)S(1)} %pad_maximum_fusion.3), channel_id=1, source_target_pairs={{0,4},{1,5},{2,6},{3,7},{4,0},{5,1},{6,2},{7,3},{8,12},{9,13},{10,... | collective-permute-start | bytes 122888 | tf_op jit(solution)/shard_map/ppermute | solution.py:512
  51.2 1.5 %collective-permute-start.15 = (f32[8,40,128]{2,1,0:T(8,128)S(1)}, f32[8,40,128]{2,1,0:T(8,128)S(1)}, u32[]{:S(2)}, u32[]{:S(2)}) collective-permute-start(f32[8,40,128]{2,1,0:T(8,128)S(1)} %pad_maximum_fusion.1), channel_id=1, source_target_pairs={{0,1},{1,0},{2,3},{3,2},{4,5},{5,4},{6,7},{7,6},{8,9},{9,8},{10,11... | collective-permute-start | bytes 491528 | tf_op jit(solution)/shard_map/ppermute | solution.py:512

commit v4 on v3

--- a/solution.py
+++ b/solution.py
@@ -15,6 +15,9 @@
 TILES = BW * BW // LANES
 ROWS = S * TILES
 PARTS = 3
+GATHER_COEF = (1, 2, 0)
+SUM_INTS = (2, 0, 1)
+GATHER_TERMS = (0, 2, 1)
 SEAT = 8
 SEATS = LANES // SEAT
 TERM_TILES = -(-S * BW // LANES)
@@ -34,53 +37,113 @@
 
 def split_rows(count):
     unit = count // 16
-    return (unit, 13 * unit, count - 14 * unit)
-
-
-def retile_rows(x, out, at):
+    return (unit, 13 * unit, count - 14 * unit), (2 * unit, unit, 0)
+
+
+def retile_rows(x, at, out, to):
     for s in range(S):
-        out[at : at + 16, s * TILES : (s + 1) * TILES, :] = x[s, at : at + 16, :].reshape(16, TILES, LANES)
-
-
-def fetch(start, x, slab, sems):
+        out[to : to + 16, s * TILES : (s + 1) * TILES, :] = x[s, at : at + 16, :].reshape(16, TILES, LANES)
+
+
+def fetch(start, x, slab, sems, first):
     copies = []
     for c in range(slab.shape[1] // 16):
         src = x.at[:, pl.ds(start + c * 16, 16), :]
-        copies.append(pltpu.make_async_copy(src, slab.at[:, pl.ds(c * 16, 16), :], sems.at[c]))
+        copies.append(pltpu.make_async_copy(src, slab.at[:, pl.ds(c * 16, 16), :], sems.at[first + c]))
         copies[-1].start()
     return copies
 
 
-def retile_kernel(start, x, out, slab, sems):
-    for c, copy in enumerate(fetch(start, x, slab, sems)):
+def retile_part(start, x, raw, out, ahead, slab, sems):
+    have = 0 if raw is None else raw.shape[1]
+    copies = fetch(start + have, x, slab, sems, 0)
+    later = [] if ahead is None else fetch(start + out.shape[0], x, ahead, sems, len(copies))
+    for c in range(have // 16):
+        retile_rows(raw, c * 16, out, c * 16)
+    for c, copy in enumerate(copies):
         copy.wait()
-        retile_rows(slab, out, c * 16)
-
-
-def retile(x, part):
-    sizes = split_rows(x.shape[1])
-    start, size = sum(sizes[:part]), sizes[part]
+        retile_rows(slab, c * 16, out, have + c * 16)
+    return later
+
+
+def retile_kernel(start, x, raw, out, *refs):
+    ahead = refs[0] if len(refs) == 3 else None
+    slab, sems = refs[-2:]
+    for copy in retile_part(start, x, raw, out, ahead, slab, sems):
+        copy.wait()
+
+
+def retile_shapes(count, part):
+    sizes, ahead = split_rows(count)
+    width = TILES * LANES
+    have = ahead[part - 1] if part else 0
+    out = [jax.ShapeDtypeStruct((sizes[part], ROWS, LANES), BF16)]
+    if ahead[part]:
+        out.append(jax.ShapeDtypeStruct((S, ahead[part], width), BF16))
+    scratch = [
+        pltpu.VMEM((S, sizes[part] - have, width), BF16),
+        pltpu.SemaphoreType.DMA(((sizes[part] - have + ahead[part]) // 16,)),
+    ]
+    return sum(sizes[:part]), out, scratch
+
+
+def retile(x, part, raw):
+    start, out, scratch = retile_shapes(x.shape[1], part)
     return pl.pallas_call(
         functools.partial(retile_kernel, start),
-        in_specs=[pl.BlockSpec(memory_space=pltpu.HBM)],
-        out_specs=VMEM,
-        out_shape=jax.ShapeDtypeStruct((size, ROWS, LANES), BF16),
-        scratch_shapes=[pltpu.VMEM((S, size, TILES * LANES), BF16), pltpu.SemaphoreType.DMA((size // 16,))],
+        in_specs=[pl.BlockSpec(memory_space=pltpu.HBM), VMEM],
+        out_specs=[VMEM] * len(out),
+        out_shape=out,
+        scratch_shapes=scratch,
         compiler_params=pltpu.CompilerParams(vmem_limit_bytes=10 * 2**20),
-        cost_estimate=pl.CostEstimate(flops=0, bytes_accessed=4 * size * ROWS * LANES, transcendentals=0),
-    )(in_hbm(x))
-
-
-def prepare_kernel(blocks, counts, index, levels, coef, x, *refs):
-    rows, ids, held, out = refs[:4]
-    sems, own_blocks, own_index, own_levels, slab, slab_sems = refs[4:]
-    pairs = (blocks, own_blocks), (index, own_index), (levels, own_levels), (coef, held)
+        cost_estimate=pl.CostEstimate(flops=0, bytes_accessed=4 * out[0].size, transcendentals=0),
+    )(in_hbm(x), raw)
+
+
+def prepare_kernel(blocks, counts, coef, x, ids, held, out, ahead, sems, own_blocks, slab, slab_sems):
+    pairs = (blocks, own_blocks), (coef, held)
     copies = [pltpu.make_async_copy(src, dst, sems.at[k]) for k, (src, dst) in enumerate(pairs)]
     for copy in copies:
         copy.start()
-    for c, copy in enumerate(fetch(0, x, slab, slab_sems)):
+    later = retile_part(0, x, None, out, ahead, slab, slab_sems)
+    for copy in copies:
         copy.wait()
-        retile_rows(slab, out, c * 16)
+    lane = iota((1, LANES), 1)
+    total = jnp.full(ids.shape, -1, jnp.int32)
+    for s in range(S):
+        total = jnp.where((lane == s) & (s < counts[...]), own_blocks[0, s], total)
+    ids[...] = total
+    for copy in later:
+        copy.wait()
+
+
+def in_hbm(x):
+    return pltpu.with_memory_space_constraint(x, pltpu.HBM)
+
+
+def prepare(blocks, counts, coef, x):
+    far = pl.BlockSpec(memory_space=pltpu.HBM)
+    _, out, scratch = retile_shapes(x.shape[1], 0)
+    return pl.pallas_call(
+        prepare_kernel,
+        in_specs=[far, VMEM, far, far],
+        out_specs=[VMEM] * 4,
+        out_shape=[
+            jax.ShapeDtypeStruct((1, LANES), jnp.int32),
+            jax.ShapeDtypeStruct(coef.shape, coef.dtype),
+        ]
+        + out,
+        scratch_shapes=[pltpu.SemaphoreType.DMA((2,)), pltpu.SMEM(blocks.shape, blocks.dtype)] + scratch,
+        compiler_params=pltpu.CompilerParams(vmem_limit_bytes=8 * 2**20),
+        cost_estimate=pl.CostEstimate(flops=0, bytes_accessed=4 * out[0].size, transcendentals=0),
+    )(in_hbm(blocks), counts, in_hbm(coef), in_hbm(x))
+
+
+def level_kernel(index, levels, rows, own_index, own_levels, sems):
+    pairs = (index, own_index), (levels, own_levels)
+    copies = [pltpu.make_async_copy(src, dst, sems.at[k]) for k, (src, dst) in enumerate(pairs)]
+    for copy in copies:
+        copy.start()
     for copy in copies:
         copy.wait()
     lane = iota((1, LANES), 1)
@@ -93,50 +156,34 @@
 
     lax.fori_loop(0, rows.shape[0], step, 0)
     rows[...] = jnp.broadcast_to(jnp.sum(rows[...], axis=1, keepdims=True), rows.shape)
-    total = jnp.full(ids.shape, -1, jnp.int32)
-    for s in range(S):
-        total = jnp.where((lane == s) & (s < counts[...]), own_blocks[0, s], total)
-    ids[...] = total
-
-
-def in_hbm(x):
-    return pltpu.with_memory_space_constraint(x, pltpu.HBM)
-
-
-def prepare(blocks, counts, index, levels, coef, x):
+
+
+def level_rows(index, levels):
     far = pl.BlockSpec(memory_space=pltpu.HBM)
-    size = split_rows(x.shape[1])[0]
-    return pl.pallas_call(
-        prepare_kernel,
-        in_specs=[far, VMEM, far, far, far, far],
-        out_specs=[VMEM] * 4,
-        out_shape=[
-            jax.ShapeDtypeStruct((index.shape[0], LANES), F32),
-            jax.ShapeDtypeStruct((1, LANES), jnp.int32),
-            jax.ShapeDtypeStruct(coef.shape, coef.dtype),
-            jax.ShapeDtypeStruct((size, ROWS, LANES), BF16),
-        ],
+    return pl.pallas_call(
+        level_kernel,
+        in_specs=[far, far],
+        out_specs=VMEM,
+        out_shape=jax.ShapeDtypeStruct((index.shape[0], LANES), F32),
         scratch_shapes=[
-            pltpu.SemaphoreType.DMA((4,)),
-            pltpu.SMEM(blocks.shape, blocks.dtype),
             pltpu.SMEM(index.shape, index.dtype),
             pltpu.VMEM(levels.shape, levels.dtype),
-            pltpu.VMEM((S, size, TILES * LANES), BF16),
-            pltpu.SemaphoreType.DMA((size // 16,)),
+            pltpu.SemaphoreType.DMA((2,)),
         ],
-        compiler_params=pltpu.CompilerParams(vmem_limit_bytes=8 * 2**20),
-        cost_estimate=pl.CostEstimate(flops=0, bytes_accessed=4 * size * ROWS * LANES, transcendentals=0),
-    )(in_hbm(blocks), counts, in_hbm(index), in_hbm(levels), in_hbm(coef), in_hbm(x))
-
-
-def stages(size):
+        compiler_params=pltpu.CompilerParams(vmem_limit_bytes=2**20),
+        cost_estimate=pl.CostEstimate(flops=0, bytes_accessed=2**20, transcendentals=0),
+    )(in_hbm(index), in_hbm(levels))
+
+
+def stages(size, order):
     bits = []
     while size > 2:
         size //= 2
         bits.append(size)
     steps = [(bits.pop(0),)] if len(bits) % 2 else []
     for high, low in zip(bits[::2], bits[1::2]):
-        steps.append((low, high ^ low, high))
+        both = (low, high, high ^ low)
+        steps.append(tuple(both[k] for k in order))
     return tuple(steps)
 
 
@@ -144,12 +191,9 @@
     rel = lax.bitwise_xor(dev, me)
     place, count = 0, 1
     for step in steps:
-        low = lax.bitwise_and(rel, step[0]) != 0
-        if len(step) == 1:
-            place = place + jnp.where(low, count, 0)
-        else:
-            high = lax.bitwise_and(rel, step[2]) != 0
-            place = place + jnp.where(high, jnp.where(low, 2, 3), jnp.where(low, 1, 0)) * count
+        bits = lax.bitwise_and(rel, functools.reduce(int.__or__, step))
+        for k, mask in enumerate(step):
+            place = place + jnp.where(bits == mask, (k + 1) * count, 0)
         count *= len(step) + 1
     return place
 
@@ -420,9 +464,12 @@
     )(packed)
 
 
-def place_kernel(base, piece, spots, *refs):
+def place_kernel(base, other, piece, spots, *refs):
     out = refs[-1]
     orbs, width = out.shape
+    shift = 0
+    if other:
+        shift = jnp.where(lax.rem(lax.axis_index("aux"), 2) == 0, 1, -1) * (width // BW)
     mid = orbs // 2
     step_tiles = range(width // LANES)
     for first in range(0, orbs, 16):
@@ -436,8 +483,8 @@
             total = [list(row) for row in total]
             for k in range(TERM_TILES):
                 at = (base + d) * SEAT + 2 * k
-                spot = jnp.broadcast_to(spots[pl.ds(at, 1), :], (8, LANES))
-                turn_spot = jnp.broadcast_to(spots[pl.ds(at + 1, 1), :], (8, LANES))
+                spot = jnp.broadcast_to(spots[pl.ds(at, 1), :] - shift, (8, LANES))
+                turn_spot = jnp.broadcast_to(spots[pl.ds(at + 1, 1), :] - shift, (8, LANES))
                 values, turns = [], []
                 for r in parts:
                     half = (k + 1) * LANES > S * BW
@@ -464,10 +511,10 @@
                 out[part, t * LANES : (t + 1) * LANES] = total[r][t]
 
 
-def place_terms(base, piece, spots, total, orbs, rows):
+def place_terms(base, other, piece, spots, total, orbs, rows):
     args = (piece, spots) if total is None else (piece, spots, total)
     return pl.pallas_call(
-        functools.partial(place_kernel, base),
+        functools.partial(place_kernel, base, other),
         in_specs=[VMEM] * len(args),
         out_specs=VMEM,
         out_shape=jax.ShapeDtypeStruct((orbs, rows), F32),
@@ -516,51 +563,60 @@
     integrals, block_list, slot_counts, coefficients, batch_index, occ_energy, vir_energy, owner_map
 ):
     local_rows = coefficients.shape[0]
-    steps = stages(lax.axis_size("aux"))
+    size = lax.axis_size("aux")
+    steps = stages(size, GATHER_COEF)
     x = jnp.transpose(integrals, (1, 0, 2))
     buf = coefficients.T[None]
-    slabs = []
+    slabs, raw = [], None
     for k, step in enumerate(steps):
         far = [swap(buf, mask) for mask in step]
         if k == 0:
-            levels, ids, buf, slab = prepare(
-                block_list, slot_counts.reshape(1, 1), batch_index, occ_energy.reshape(-1, LANES), buf, x
-            )
+            ids, buf, slab, raw = prepare(block_list, slot_counts.reshape(1, 1), buf, x)
             slabs.append(slab)
         if k + 1 == len(steps):
-            slabs.append(retile(x, 1))
+            slab, raw = retile(x, 1, raw)
+            slabs.append(slab)
         buf = jnp.concatenate([buf] + far, axis=0)
         buf, _ = lax.optimization_barrier((buf, slabs[-1]))
-        x, _ = lax.optimization_barrier((x, far[0]))
+        x, raw, _ = lax.optimization_barrier((x, raw, far[0]))
     far = swap(buf, 1)
-    slabs.append(retile(x, 2))
+    slabs += retile(x, 2, raw)
     half, send = half_transform(steps + ((1,),), ids, buf, far, slabs)
     keep = own_squares(half, ids, send) + swap(send, 1)
-    for step in reversed(steps):
-        keep = sum([swap(keep, mask) for mask in step], keep)
+    for k, step in enumerate(reversed(stages(size, SUM_INTS))):
+        far = [swap(keep, mask) for mask in step]
+        if k == 0:
+            levels = level_rows(batch_index, occ_energy.reshape(-1, LANES))
+        keep = sum(far, keep)
+        keep, levels = lax.optimization_barrier((keep, levels))
     other = swap(keep, 1)
     vir = vir_energy.reshape(1, -1)
     own_energy, own = own_weights(keep, levels, vir, half)
+    steps = stages(size, GATHER_TERMS)
     rels = [0]
-    for step in steps + ((1,),):
+    for step in steps:
         rels = rels + [rel ^ mask for mask in step for rel in rels]
     orbs = owner_map.shape[0]
     spots = seats(keep, orbs, local_rows, tuple(rels))
     other, spots = lax.optimization_barrier((other, spots))
     terms, energy = gradient_terms(other, levels, vir, half, own_energy, own, slabs)
-    buf, total, done = terms[None], None, 0
+    buf, done, ours, theirs = terms[None], 0, None, None
     for k, step in enumerate(steps):
         far = [swap(buf, mask) for mask in step]
-        total = place_terms(done, buf[done:], spots, total, orbs, local_rows)
-        if k + 1 == len(steps):
-            pair_energy = pair_slots(owner_map, energy)
-            total, pair_energy = lax.optimization_barrier((total, pair_energy))
+        piece = buf[done:]
+        theirs = place_terms(done, True, piece, spots, theirs, orbs, local_rows)
+        ours = place_terms(done, False, piece, spots, ours, orbs, local_rows)
         done = buf.shape[0]
-        buf = jnp.concatenate([buf] + far, axis=0)
-        buf, total = lax.optimization_barrier((buf, total))
-    far = swap(buf, 1)
-    total = place_terms(done, buf[done:], spots, total, orbs, local_rows)
-    grad_coef = place_terms(buf.shape[0], far, spots, total, orbs, local_rows).T
+        if k + 1 < len(steps):
+            buf = jnp.concatenate([buf] + far, axis=0)
+            buf, ours, theirs = lax.optimization_barrier((buf, ours, theirs))
+    pair_energy = pair_slots(owner_map, energy)
+    ours, theirs, pair_energy = lax.optimization_barrier((ours, theirs, pair_energy))
+    for k, piece in enumerate(far):
+        theirs = place_terms(done + k * piece.shape[0], True, piece, spots, theirs, orbs, local_rows)
+    last = swap(theirs, 1)
+    ours = place_terms(done, False, jnp.concatenate(far, axis=0), spots, ours, orbs, local_rows)
+    grad_coef = (ours + last).T
     return (grad_coef, pair_energy)
 
 

time: 53.7 us -> 52.8 us (0.983)
  waiting for transfers between devices: 13.9 us -> 12.5 us
  other arithmetic: 0.1 us -> 0.74 us
    ppermute x16, waiting for transfers between devices: 13.9 us -> 12.5 us  [swap(): return lax.ppermute(x, 'aux', [(i, i ^ mask) for i in range(size)])]
    pallas_call x2, Pallas kernels: 5.56 us -> 4.9 us  [retile(): pl.pallas_call(functools.partial(retile_kernel, start), in_specs=[pl.Bloc...]
    transpose x0 -> x1, other arithmetic: none -> 0.64 us  [body(): grad_coef = (ours + last).T]
    pallas_call x5 -> x10, Pallas kernels: 3.02 us -> 3.41 us  [the longest x1 1.55 us: prepare(): pl.pallas_call(prepare_kernel, in_specs=[far, VMEM, far, far], out_specs=...]
  transfers between devices with their start and end apart: 16 -> 16, of which waited for: 10 -> 12; matrix products, arithmetic and copies ran while one was open for 0% -> 0% of each run, Pallas kernels for 19% -> 20%
where the time goes in v4:
time: 52.8 us; the launch traced here: 52.5 us
  starting transfers between devices  20.2 us (38%)
  Pallas kernels  17.6 us (33%)
  waiting for transfers between devices  12.5 us (24%)
  between operations  1.49 us (3%)
  other arithmetic  0.74 us (1%)
    ppermute x16, starting transfers between devices, swap(): return lax.ppermute(x, 'aux', [(i, i ^ mask) for i in range(size)])  20.2 us
    ppermute x16, waiting for transfers between devices, swap(): return lax.ppermute(x, 'aux', [(i, i ^ mask) for i in range(size)])  12.5 us
    pallas_call x2, Pallas kernels, retile(): pl.pallas_call(functools.partial(retile_kernel, start), in_specs=[pl.Bloc...  4.9 us
    pallas_call x1, Pallas kernels, gradient_terms(): pl.pallas_call(grad_kernel, in_specs=[VMEM] * (6 + PARTS), out_specs=[VME...  3.94 us
    pallas_call x1, Pallas kernels, half_transform(): pl.pallas_call(functools.partial(half_kernel, steps), in_specs=[SMEM] + [...  2.86 us
    pallas_call x1, Pallas kernels, prepare(): pl.pallas_call(prepare_kernel, in_specs=[far, VMEM, far, far], out_specs=...  1.55 us
    pallas_call x1, Pallas kernels, pair_slots(): pl.pallas_call(pair_kernel, in_specs=[pl.BlockSpec(memory_space=pltpu.HBM...  1.46 us
  transfers between devices with their start and end apart: 16, of which 12 were waited for; matrix products, arithmetic and copies ran while one was open for 0% of the time, Pallas kernels for 20%

profile of v4, /device:TPU:0, one launch (start us, length us, event | category | flops | bytes accessed | tf_op | source)
XLA Modules:
  0.0 52.5 jit_solution(16013603376083826879)
XLA Ops:
  0.6 4.1 %collective-permute-start = (bf16[1,16,1024]{2,1,0:T(8,128)(2,1)}, bf16[1,16,1024]{2,1,0:T(8,128)(2,1)S(1)}, u32[]{:S(2)}, u32[]{:S(2)}) collective-permute-start(bf16[1,16,1024]{2,1,0:T(8,128)(2,1)} %bitcast.20), channel_id=1, source_target_pairs={{0,8},{1,9},{2,10},{3,11},{4,12},{5,13},{6,14},{7,15},{8,0},{9,1},... | collective-permute-start | bytes 98312 | tf_op jit(solution)/shard_map/ppermute | solution.py:559
  5.4 1.5 %shard_map.95 = (s32[1,128]{1,0:T(1,128)S(1)}, bf16[1,16,1024]{2,1,0:T(8,128)(2,1)S(1)}, bf16[16,160,128]{2,1,0:T(8,128)(2,1)S(1)}, bf16[5,32,4096]{2,1,0:T(8,128)(2,1)S(1)}) custom-call(s32[1,5]{1,0:T(1,128)} %blocks.1, s32[1,1]{1,0:T(1,128)} %bitcast.10.counts, bf16[1,16,1024]{2,1,0:T(8,128)(2,1)} %bitcast.21, bf16[5,256,4096]{2,1,0:T(8,128)(2,1)} %bitcast.17), custom_call_target="tpu_custom_call" | custom-call | bytes 1310720 | tf_op jit(solution)/shard_map/pallas_call | solution.py:127
  7.2 1.6 %collective-permute-start.1 = (bf16[2,16,1024]{2,1,0:T(8,128)(2,1)S(1)}, bf16[2,16,1024]{2,1,0:T(8,128)(2,1)S(1)}, u32[]{:S(2)}, u32[]{:S(2)}) collective-permute-start(bf16[2,16,1024]{2,1,0:T(8,128)(2,1)S(1)} %pad_maximum_fusion.2), channel_id=1, source_target_pairs={{0,4},{1,5},{2,6},{3,7},{4,0},{5,1},{6,2},{7,3},{8,12},{9,13},{10,... | collective-permute-start | bytes 196616 | tf_op jit(solution)/shard_map/ppermute | solution.py:559
  8.8 1.6 %collective-permute-start.2 = (bf16[2,16,1024]{2,1,0:T(8,128)(2,1)S(1)}, bf16[2,16,1024]{2,1,0:T(8,128)(2,1)S(1)}, u32[]{:S(2)}, u32[]{:S(2)}) collective-permute-start(bf16[2,16,1024]{2,1,0:T(8,128)(2,1)S(1)} %pad_maximum_fusion.2), channel_id=1, source_target_pairs={{0,6},{1,7},{2,4},{3,5},{4,2},{5,3},{6,0},{7,1},{8,14},{9,15},{10,... | collective-permute-start | bytes 196616 | tf_op jit(solution)/shard_map/ppermute | solution.py:559
  10.4 0.3 collective-permute-start.3
  10.8 3.6 %shard_map.96 = (bf16[208,160,128]{2,1,0:T(8,128)(2,1)S(1)}, bf16[5,16,4096]{2,1,0:T(8,128)(2,1)S(1)}) custom-call(bf16[5,256,4096]{2,1,0:T(8,128)(2,1)} %bitcast.18, bf16[5,32,4096]{2,1,0:T(8,128)(2,1)S(1)} %get-tuple-element.38.raw), custom_call_target="tpu_custom_call" | custom-call | bytes 17039360 | tf_op jit(solution)/shard_map/pallas_call | solution.py:92
  14.4 0.3 collective-permute-done.3
  14.8 1.3 %shard_map.97.refs_2_ = bf16[32,160,128]{2,1,0:T(8,128)(2,1)S(1)} custom-call(bf16[5,256,4096]{2,1,0:T(8,128)(2,1)} %bitcast.19, bf16[5,16,4096]{2,1,0:T(8,128)(2,1)S(1)} %get-tuple-element.43.raw), custom_call_target="tpu_custom_call" | custom-call | bytes 2621440 | tf_op jit(solution)/shard_map/pallas_call | solution.py:92
  16.3 2.9 %shard_map.98 = (bf16[16,128,128]{2,1,0:T(8,128)(2,1)S(1)}, f32[136,128]{1,0:T(8,128)S(1)}) custom-call(s32[1,128]{1,0:T(1,128)S(1)} %get-tuple-element.32.ids.id_row, s32[1,128]{1,0:T(1,128)S(1)} %get-tuple-element.32.ids.id_row, bf16[8,16,1024]{2,1,0:T(8,128)(2,1)S(1)} %pad_maximum_fusion.coef_a, bf16[8,16,1024]{2,1,0:T(8,128)(2,1)S(1)} %collective-permute-done.4.coef_b, ...), custom_call_target="tpu_custom_call" | custom-call | tf_op jit(solution)/shard_map/pallas_call | solution.py:300
  19.2 0.5 collective-permute-start.5
  19.7 0.3 shard_map.99
  20.0 0.6 %collective-permute-done.5 = f32[136,128]{1,0:T(8,128)S(1)} collective-permute-done((f32[136,128]{1,0:T(8,128)S(1)}, f32[136,128]{1,0:T(8,128)S(1)}, u32[]{:S(2)}, u32[]{:S(2)}) %collective-permute-start.5) | collective-permute-done | bytes 69664 | tf_op jit(solution)/shard_map/ppermute | solution.py:559
  20.6 2.2 %collective-permute-start.6 = (f32[136,128]{1,0:T(8,128)S(1)}, f32[136,128]{1,0:T(8,128)S(1)}, u32[]{:S(2)}, u32[]{:S(2)}) collective-permute-start(f32[136,128]{1,0:T(8,128)S(1)} %add.18), channel_id=1, source_target_pairs={{0,6},{1,7},{2,4},{3,5},{4,2},{5,3},{6,0},{7,1},{8,14},{9,15},{10,... | collective-permute-start | bytes 208904 | tf_op jit(solution)/shard_map/ppermute | solution.py:559
  22.8 0.7 %collective-permute-start.7 = (f32[136,128]{1,0:T(8,128)S(1)}, f32[136,128]{1,0:T(8,128)S(1)}, u32[]{:S(2)}, u32[]{:S(2)}) collective-permute-start(f32[136,128]{1,0:T(8,128)S(1)} %add.18), channel_id=1, source_target_pairs={{0,2},{1,3},{2,0},{3,1},{4,6},{5,7},{6,4},{7,5},{8,10},{9,11},{10,... | collective-permute-start | bytes 208904 | tf_op jit(solution)/shard_map/ppermute | solution.py:559
  23.5 0.6 %collective-permute-start.8 = (f32[136,128]{1,0:T(8,128)S(1)}, f32[136,128]{1,0:T(8,128)S(1)}, u32[]{:S(2)}, u32[]{:S(2)}) collective-permute-start(f32[136,128]{1,0:T(8,128)S(1)} %add.18), channel_id=1, source_target_pairs={{0,4},{1,5},{2,6},{3,7},{4,0},{5,1},{6,2},{7,3},{8,12},{9,13},{10,... | collective-permute-start | bytes 208904 | tf_op jit(solution)/shard_map/ppermute | solution.py:559
  24.2 0.9 %shard_map.100.levels = f32[16,128]{1,0:T(8,128)S(1)} custom-call(s32[16]{0:T(128)} %index.1, f32[8,128]{1,0:T(8,128)} %bitcast.22), custom_call_target="tpu_custom_call" | custom-call | bytes 1048576 | tf_op jit(solution)/shard_map/pallas_call | solution.py:163
  25.1 1.0 %collective-permute-done.6 = f32[136,128]{1,0:T(8,128)S(1)} collective-permute-done((f32[136,128]{1,0:T(8,128)S(1)}, f32[136,128]{1,0:T(8,128)S(1)}, u32[]{:S(2)}, u32[]{:S(2)}) %collective-permute-start.6) | collective-permute-done | bytes 69664 | tf_op jit(solution)/shard_map/ppermute | solution.py:559
  26.1 1.4 %collective-permute-done.7 = f32[136,128]{1,0:T(8,128)S(1)} collective-permute-done((f32[136,128]{1,0:T(8,128)S(1)}, f32[136,128]{1,0:T(8,128)S(1)}, u32[]{:S(2)}, u32[]{:S(2)}) %collective-permute-start.7) | collective-permute-done | bytes 69664 | tf_op jit(solution)/shard_map/ppermute | solution.py:559
  27.9 2.9 %collective-permute-start.9 = (f32[136,128]{1,0:T(8,128)S(1)}, f32[136,128]{1,0:T(8,128)S(1)}, u32[]{:S(2)}, u32[]{:S(2)}) collective-permute-start(f32[136,128]{1,0:T(8,128)S(1)} %add_add_fusion), channel_id=1, source_target_pairs={{0,8},{1,9},{2,10},{3,11},{4,12},{5,13},{6,14},{7,15},{8,0},{9,1},... | collective-permute-start | bytes 208904 | tf_op jit(solution)/shard_map/ppermute | solution.py:559
  30.7 3.5 %collective-permute-done.9 = f32[136,128]{1,0:T(8,128)S(1)} collective-permute-done((f32[136,128]{1,0:T(8,128)S(1)}, f32[136,128]{1,0:T(8,128)S(1)}, u32[]{:S(2)}, u32[]{:S(2)}) %collective-permute-start.9) | collective-permute-done | bytes 69664 | tf_op jit(solution)/shard_map/ppermute | solution.py:559
  34.5 0.5 shard_map.102
  35.0 0.5 collective-permute-done.10.packed
  35.5 3.9 %shard_map.103 = (f32[40,128]{1,0:T(8,128)S(1)}, f32[16,128]{1,0:T(8,128)S(1)}) custom-call(f32[136,128]{1,0:T(8,128)S(1)} %collective-permute-done.10.packed, f32[16,128]{1,0:T(8,128)S(1)} %shard_map.100.levels, f32[1,64]{1,0:T(1,128)S(1)} %bitcast.16, bf16[16,128,128]{2,1,0:T(8,128)(2,1)S(1)} %get-tuple-element.44.half, ...), custom_call_target="tpu_custom_call" | custom-call | tf_op jit(solution)/shard_map/pallas_call | solution.py:426
  39.5 1.9 %collective-permute-start.11 = (f32[1,40,128]{2,1,0:T(8,128)S(1)}, f32[1,40,128]{2,1,0:T(8,128)S(1)}, u32[]{:S(2)}, u32[]{:S(2)}) collective-permute-start(f32[1,40,128]{2,1,0:T(8,128)S(1)} %bitcast.11), channel_id=1, source_target_pairs={{0,8},{1,9},{2,10},{3,11},{4,12},{5,13},{6,14},{7,15},{8,0},{9,1},... | collective-permute-start | bytes 61448 | tf_op jit(solution)/shard_map/ppermute | solution.py:559
  41.6 2.6 %collective-permute-done.11 = f32[1,40,128]{2,1,0:T(8,128)S(1)} collective-permute-done((f32[1,40,128]{2,1,0:T(8,128)S(1)}, f32[1,40,128]{2,1,0:T(8,128)S(1)}, u32[]{:S(2)}, u32[]{:S(2)}) %collective-permute-start.11) | collective-permute-done | bytes 20512 | tf_op jit(solution)/shard_map/ppermute | solution.py:559
  44.2 1.2 %collective-permute-start.12 = (f32[2,40,128]{2,1,0:T(8,128)S(1)}, f32[2,40,128]{2,1,0:T(8,128)S(1)}, u32[]{:S(2)}, u32[]{:S(2)}) collective-permute-start(f32[2,40,128]{2,1,0:T(8,128)S(1)} %pad_maximum_fusion.3), channel_id=1, source_target_pairs={{0,2},{1,3},{2,0},{3,1},{4,6},{5,7},{6,4},{7,5},{8,10},{9,11},{10,... | collective-permute-start | bytes 122888 | tf_op jit(solution)/shard_map/ppermute | solution.py:559
  45.4 1.0 %collective-permute-start.13 = (f32[2,40,128]{2,1,0:T(8,128)S(1)}, f32[2,40,128]{2,1,0:T(8,128)S(1)}, u32[]{:S(2)}, u32[]{:S(2)}) collective-permute-start(f32[2,40,128]{2,1,0:T(8,128)S(1)} %pad_maximum_fusion.3), channel_id=1, source_target_pairs={{0,6},{1,7},{2,4},{3,5},{4,2},{5,3},{6,0},{7,1},{8,14},{9,15},{10,... | collective-permute-start | bytes 122888 | tf_op jit(solution)/shard_map/ppermute | solution.py:559
  46.4 1.3 %collective-permute-start.14 = (f32[2,40,128]{2,1,0:T(8,128)S(1)}, f32[2,40,128]{2,1,0:T(8,128)S(1)}, u32[]{:S(2)}, u32[]{:S(2)}) collective-permute-start(f32[2,40,128]{2,1,0:T(8,128)S(1)} %pad_maximum_fusion.3), channel_id=1, source_target_pairs={{0,4},{1,5},{2,6},{3,7},{4,0},{5,1},{6,2},{7,3},{8,12},{9,13},{10,... | collective-permute-start | bytes 122888 | tf_op jit(solution)/shard_map/ppermute | solution.py:559
  47.7 1.5 %shard_map.108 = f32[2]{0:T(128)} custom-call(s32[16]{0:T(128)} %owner.1, f32[16,128]{1,0:T(8,128)S(1)} %get-tuple-element.58.energy), custom_call_target="tpu_custom_call" | custom-call | bytes 1048576 | tf_op jit(solution)/shard_map/pallas_call | solution.py:546
  49.5 0.8 %collective-permute-done.13.piece = f32[2,40,128]{2,1,0:T(8,128)S(1)} collective-permute-done((f32[2,40,128]{2,1,0:T(8,128)S(1)}, f32[2,40,128]{2,1,0:T(8,128)S(1)}, u32[]{:S(2)}, u32[]{:S(2)}) %collective-permute-start.13) | collective-permute-done | bytes 40992 | tf_op jit(solution)/shard_map/ppermute | solution.py:559
  50.9 1.0 %collective-permute-done.15 = f32[16,1024]{1,0:T(8,128)S(1)} collective-permute-done((f32[16,1024]{1,0:T(8,128)S(1)}, f32[16,1024]{1,0:T(8,128)S(1)}, u32[]{:S(2)}, u32[]{:S(2)}) %collective-permute-start.15) | collective-permute-done | bytes 65568 | tf_op jit(solution)/shard_map/ppermute | solution.py:559
  51.9 0.6 %add_bitcast_fusion = f32[1024,16]{0,1:T(8,128)} fusion(f32[16,1024]{1,0:T(8,128)S(1)} %shard_map.109, f32[16,1024]{1,0:T(8,128)S(1)} %collective-permute-done.15), kind=kLoop, calls=%fused_computation.4 | loop fusion | flops 16384 | bytes 196608 | tf_op jit(solution)/shard_map/transpose | solution.py:619
  (29 shorter events, 2.3 us)
Async XLA Ops:
  0.6 6.6 %collective-permute-start = (bf16[1,16,1024]{2,1,0:T(8,128)(2,1)}, bf16[1,16,1024]{2,1,0:T(8,128)(2,1)S(1)}, u32[]{:S(2)}, u32[]{:S(2)}) collective-permute-start(bf16[1,16,1024]{2,1,0:T(8,128)(2,1)} %bitcast.20), channel_id=1, source_target_pairs={{0,8},{1,9},{2,10},{3,11},{4,12},{5,13},{6,14},{7,15},{8,0},{9,1},... | collective-permute-start | bytes 98312 | tf_op jit(solution)/shard_map/ppermute | solution.py:559
  7.2 7.1 %collective-permute-start.1 = (bf16[2,16,1024]{2,1,0:T(8,128)(2,1)S(1)}, bf16[2,16,1024]{2,1,0:T(8,128)(2,1)S(1)}, u32[]{:S(2)}, u32[]{:S(2)}) collective-permute-start(bf16[2,16,1024]{2,1,0:T(8,128)(2,1)S(1)} %pad_maximum_fusion.2), channel_id=1, source_target_pairs={{0,4},{1,5},{2,6},{3,7},{4,0},{5,1},{6,2},{7,3},{8,12},{9,13},{10,... | collective-permute-start | bytes 196616 | tf_op jit(solution)/shard_map/ppermute | solution.py:559
  8.8 5.5 %collective-permute-start.2 = (bf16[2,16,1024]{2,1,0:T(8,128)(2,1)S(1)}, bf16[2,16,1024]{2,1,0:T(8,128)(2,1)S(1)}, u32[]{:S(2)}, u32[]{:S(2)}) collective-permute-start(bf16[2,16,1024]{2,1,0:T(8,128)(2,1)S(1)} %pad_maximum_fusion.2), channel_id=1, source_target_pairs={{0,6},{1,7},{2,4},{3,5},{4,2},{5,3},{6,0},{7,1},{8,14},{9,15},{10,... | collective-permute-start | bytes 196616 | tf_op jit(solution)/shard_map/ppermute | solution.py:559
  10.4 4.3 %collective-permute-start.3 = (bf16[2,16,1024]{2,1,0:T(8,128)(2,1)S(1)}, bf16[2,16,1024]{2,1,0:T(8,128)(2,1)S(1)}, u32[]{:S(2)}, u32[]{:S(2)}) collective-permute-start(bf16[2,16,1024]{2,1,0:T(8,128)(2,1)S(1)} %pad_maximum_fusion.2), channel_id=1, source_target_pairs={{0,2},{1,3},{2,0},{3,1},{4,6},{5,7},{6,4},{7,5},{8,10},{9,11},{10,... | collective-permute-start | bytes 196616 | tf_op jit(solution)/shard_map/ppermute | solution.py:559
  14.7 1.6 %collective-permute-start.4 = (bf16[8,16,1024]{2,1,0:T(8,128)(2,1)S(1)}, bf16[8,16,1024]{2,1,0:T(8,128)(2,1)S(1)}, u32[]{:S(2)}, u32[]{:S(2)}) collective-permute-start(bf16[8,16,1024]{2,1,0:T(8,128)(2,1)S(1)} %pad_maximum_fusion.coef_a), channel_id=1, source_target_pairs={{0,1},{1,0},{2,3},{3,2},{4,5},{5,4},{6,7},{7,6},{8,9},{9,8},{10,11... | collective-permute-start | bytes 786440 | tf_op jit(solution)/shard_map/ppermute | solution.py:559
  16.1 18.4 %copy-start = (f32[64]{0:T(128)S(1)}, f32[64]{0:T(128)}, u32[]{:S(2)}) copy-start(f32[64]{0:T(128)} %param.14) | copy-start | bytes 772
  19.2 1.4 %collective-permute-start.5 = (f32[136,128]{1,0:T(8,128)S(1)}, f32[136,128]{1,0:T(8,128)S(1)}, u32[]{:S(2)}, u32[]{:S(2)}) collective-permute-start(f32[136,128]{1,0:T(8,128)S(1)} %get-tuple-element.45), channel_id=1, source_target_pairs={{0,1},{1,0},{2,3},{3,2},{4,5},{5,4},{6,7},{7,6},{8,9},{9,8},{10,11... | collective-permute-start | bytes 208904 | tf_op jit(solution)/shard_map/ppermute | solution.py:559
  20.6 5.5 %collective-permute-start.6 = (f32[136,128]{1,0:T(8,128)S(1)}, f32[136,128]{1,0:T(8,128)S(1)}, u32[]{:S(2)}, u32[]{:S(2)}) collective-permute-start(f32[136,128]{1,0:T(8,128)S(1)} %add.18), channel_id=1, source_target_pairs={{0,6},{1,7},{2,4},{3,5},{4,2},{5,3},{6,0},{7,1},{8,14},{9,15},{10,... | collective-permute-start | bytes 208904 | tf_op jit(solution)/shard_map/ppermute | solution.py:559
  22.8 4.7 %collective-permute-start.7 = (f32[136,128]{1,0:T(8,128)S(1)}, f32[136,128]{1,0:T(8,128)S(1)}, u32[]{:S(2)}, u32[]{:S(2)}) collective-permute-start(f32[136,128]{1,0:T(8,128)S(1)} %add.18), channel_id=1, source_target_pairs={{0,2},{1,3},{2,0},{3,1},{4,6},{5,7},{6,4},{7,5},{8,10},{9,11},{10,... | collective-permute-start | bytes 208904 | tf_op jit(solution)/shard_map/ppermute | solution.py:559
  23.5 4.3 %collective-permute-start.8 = (f32[136,128]{1,0:T(8,128)S(1)}, f32[136,128]{1,0:T(8,128)S(1)}, u32[]{:S(2)}, u32[]{:S(2)}) collective-permute-start(f32[136,128]{1,0:T(8,128)S(1)} %add.18), channel_id=1, source_target_pairs={{0,4},{1,5},{2,6},{3,7},{4,0},{5,1},{6,2},{7,3},{8,12},{9,13},{10,... | collective-permute-start | bytes 208904 | tf_op jit(solution)/shard_map/ppermute | solution.py:559
  27.9 6.3 %collective-permute-start.9 = (f32[136,128]{1,0:T(8,128)S(1)}, f32[136,128]{1,0:T(8,128)S(1)}, u32[]{:S(2)}, u32[]{:S(2)}) collective-permute-start(f32[136,128]{1,0:T(8,128)S(1)} %add_add_fusion), channel_id=1, source_target_pairs={{0,8},{1,9},{2,10},{3,11},{4,12},{5,13},{6,14},{7,15},{8,0},{9,1},... | collective-permute-start | bytes 208904 | tf_op jit(solution)/shard_map/ppermute | solution.py:559
  34.2 1.3 %collective-permute-start.10 = (f32[136,128]{1,0:T(8,128)S(1)}, f32[136,128]{1,0:T(8,128)S(1)}, u32[]{:S(2)}, u32[]{:S(2)}) collective-permute-start(f32[136,128]{1,0:T(8,128)S(1)} %add.22.packed), channel_id=1, source_target_pairs={{0,1},{1,0},{2,3},{3,2},{4,5},{5,4},{6,7},{7,6},{8,9},{9,8},{10,11... | collective-permute-start | bytes 208904 | tf_op jit(solution)/shard_map/ppermute | solution.py:559
  39.5 4.7 %collective-permute-start.11 = (f32[1,40,128]{2,1,0:T(8,128)S(1)}, f32[1,40,128]{2,1,0:T(8,128)S(1)}, u32[]{:S(2)}, u32[]{:S(2)}) collective-permute-start(f32[1,40,128]{2,1,0:T(8,128)S(1)} %bitcast.11), channel_id=1, source_target_pairs={{0,8},{1,9},{2,10},{3,11},{4,12},{5,13},{6,14},{7,15},{8,0},{9,1},... | collective-permute-start | bytes 61448 | tf_op jit(solution)/shard_map/ppermute | solution.py:559
  44.2 5.2 %collective-permute-start.12 = (f32[2,40,128]{2,1,0:T(8,128)S(1)}, f32[2,40,128]{2,1,0:T(8,128)S(1)}, u32[]{:S(2)}, u32[]{:S(2)}) collective-permute-start(f32[2,40,128]{2,1,0:T(8,128)S(1)} %pad_maximum_fusion.3), channel_id=1, source_target_pairs={{0,2},{1,3},{2,0},{3,1},{4,6},{5,7},{6,4},{7,5},{8,10},{9,11},{10,... | collective-permute-start | bytes 122888 | tf_op jit(solution)/shard_map/ppermute | solution.py:559
  45.4 4.9 %collective-permute-start.13 = (f32[2,40,128]{2,1,0:T(8,128)S(1)}, f32[2,40,128]{2,1,0:T(8,128)S(1)}, u32[]{:S(2)}, u32[]{:S(2)}) collective-permute-start(f32[2,40,128]{2,1,0:T(8,128)S(1)} %pad_maximum_fusion.3), channel_id=1, source_target_pairs={{0,6},{1,7},{2,4},{3,5},{4,2},{5,3},{6,0},{7,1},{8,14},{9,15},{10,... | collective-permute-start | bytes 122888 | tf_op jit(solution)/shard_map/ppermute | solution.py:559
  46.4 4.0 %collective-permute-start.14 = (f32[2,40,128]{2,1,0:T(8,128)S(1)}, f32[2,40,128]{2,1,0:T(8,128)S(1)}, u32[]{:S(2)}, u32[]{:S(2)}) collective-permute-start(f32[2,40,128]{2,1,0:T(8,128)S(1)} %pad_maximum_fusion.3), channel_id=1, source_target_pairs={{0,4},{1,5},{2,6},{3,7},{4,0},{5,1},{6,2},{7,3},{8,12},{9,13},{10,... | collective-permute-start | bytes 122888 | tf_op jit(solution)/shard_map/ppermute | solution.py:559
  50.6 1.3 %collective-permute-start.15 = (f32[16,1024]{1,0:T(8,128)S(1)}, f32[16,1024]{1,0:T(8,128)S(1)}, u32[]{:S(2)}, u32[]{:S(2)}) collective-permute-start(f32[16,1024]{1,0:T(8,128)S(1)} %shard_map.112), channel_id=1, source_target_pairs={{0,1},{1,0},{2,3},{3,2},{4,5},{5,4},{6,7},{7,6},{8,9},{9,8},{10,11... | collective-permute-start | bytes 196616 | tf_op jit(solution)/shard_map/ppermute | solution.py:559

commit v5 on v4

--- a/solution.py
+++ b/solution.py
@@ -198,7 +198,7 @@
     return place
 
 
-def half_kernel(steps, ids, id_row, coef_a, coef_b, *refs):
+def half_kernel(steps, id_row, coef_a, coef_b, *refs):
     slabs, (half, send) = refs[:PARTS], refs[PARTS:]
     me = lax.axis_index("aux")
     orbs, width = coef_a.shape[1], coef_a.shape[2]
@@ -208,9 +208,10 @@
     dst = iota((LANES, LANES), 1)
     wanted = (dst & BW) // BW + (dst & (TILES - 1)) * 2 + (dst & TILES) // TILES * BW
     spread = jnp.where(src == wanted, 1.0, 0.0).astype(BF16)
+    ids = [id_row[0, s] for s in range(S)]
     picked = []
     for s in range(S):
-        block = jnp.maximum(ids[0, s], 0)
+        block = jnp.maximum(ids[s], 0)
         dev = lax.div(block, per_dev)
         inner = lax.rem(block, per_dev)
         place = gather_index(dev, me, steps)
@@ -223,14 +224,14 @@
     group = iota((orbs, LANES), 1) // TILES
     coef = [[jnp.zeros((orbs, LANES), F32) for _ in range(2)] for _ in range(HALVES)]
     for s in range(S):
-        second = lax.rem(ids[0, s], HALVES) == 1
+        second = lax.rem(ids[s], HALVES) == 1
         value = apart[s * orbs : (s + 1) * orbs]
         value = jnp.where(second, pltpu.roll(value, LANES - TILES, 1), value)
         for h in range(HALVES):
             shift = (s * TILES - h * BW) % LANES
             there = pltpu.roll(value, shift, 1) if shift else value
             tile = s * TILES // LANES
-            hit = (group == s % (LANES // TILES)) & (ids[0, s] >= 0)
+            hit = (group == s % (LANES // TILES)) & (ids[s] >= 0)
             coef[h][tile] = jnp.where(hit, there, coef[h][tile])
     coef = jnp.concatenate([jnp.concatenate(coef[h], axis=1)[:, :ROWS] for h in range(HALVES)], axis=0).astype(BF16)
     low = iota((orbs, LANES), 1) < BW
@@ -299,11 +300,11 @@
     packed = jax.ShapeDtypeStruct((rows, LANES), F32)
     return pl.pallas_call(
         functools.partial(half_kernel, steps),
-        in_specs=[SMEM] + [VMEM] * (3 + PARTS),
+        in_specs=[VMEM] * (3 + PARTS),
         out_specs=[VMEM] * 2,
         out_shape=[jax.ShapeDtypeStruct((orbs, pairs, LANES), BF16), packed],
         compiler_params=pltpu.CompilerParams(vmem_limit_bytes=limit(orbs)),
-    )(ids, ids, coef_a, coef_b, *slabs)
+    )(ids, coef_a, coef_b, *slabs)
 
 
 def weight_rows(packed, core, levels, vir, half, energy, weights):
@@ -347,14 +348,15 @@
                     weights[i * pairs : (i + 1) * pairs, :] = w.astype(BF16).astype(F32)
 
 
-def weight_kernel(packed, levels, vir, half, energy, weights):
-    weight_rows(packed, lax.rem(lax.axis_index("aux"), 2), levels, vir, half, energy, weights)
-
-
-def own_weights(packed, levels, vir, half):
+def weight_kernel(other, packed, levels, vir, half, energy, weights):
+    core = lax.rem(lax.axis_index("aux"), 2)
+    weight_rows(packed, 1 - core if other else core, levels, vir, half, energy, weights)
+
+
+def core_weights(other, packed, levels, vir, half):
     orbs, pairs = half.shape[0], half.shape[1]
     return pl.pallas_call(
-        weight_kernel,
+        functools.partial(weight_kernel, other),
         in_specs=[VMEM] * 4,
         out_specs=[VMEM] * 2,
         out_shape=[
@@ -366,12 +368,11 @@
     )(packed, levels, vir, half)
 
 
-def grad_kernel(packed, levels, vir, half, own_energy, own, *refs):
-    slabs, (terms, energy, other_energy, other, mixed) = refs[:PARTS], refs[PARTS:]
+def grad_kernel(own_energy, own, other_energy, other, *refs):
+    slabs, (terms, energy, mixed) = refs[:PARTS], refs[PARTS:]
     core = lax.rem(lax.axis_index("aux"), 2)
-    orbs, pairs = half.shape[0], half.shape[1]
-    mid = orbs // 2
-    weight_rows(packed, 1 - core, levels, vir, half, other_energy, other)
+    mid = own_energy.shape[0]
+    orbs, pairs = 2 * mid, own.shape[0] // mid
 
     def ordered(ours, theirs):
         return jnp.concatenate([jnp.where(core == 0, ours, theirs), jnp.where(core == 0, theirs, ours)], axis=0)
@@ -420,21 +421,17 @@
         terms[t * orbs : t * orbs + out.shape[0], :] = out
 
 
-def gradient_terms(packed, levels, vir, half, own_energy, own, slabs):
-    orbs, pairs = half.shape[0], half.shape[1]
+def gradient_terms(own_energy, own, other_energy, other, slabs):
+    orbs = 2 * own_energy.shape[0]
     width = -(-S * BW // LANES) * LANES
     return pl.pallas_call(
         grad_kernel,
-        in_specs=[VMEM] * (6 + PARTS),
+        in_specs=[VMEM] * (4 + PARTS),
         out_specs=[VMEM] * 2,
         out_shape=[jax.ShapeDtypeStruct((orbs * S * BW // LANES, LANES), F32), jax.ShapeDtypeStruct((orbs, LANES), F32)],
-        scratch_shapes=[
-            pltpu.VMEM(own_energy.shape, F32),
-            pltpu.VMEM(own.shape, F32),
-            pltpu.VMEM((width, LANES), F32),
-        ],
+        scratch_shapes=[pltpu.VMEM((width, LANES), F32)],
         compiler_params=pltpu.CompilerParams(vmem_limit_bytes=limit(orbs)),
-    )(packed, levels, vir, half, own_energy, own, *slabs)
+    )(own_energy, own, other_energy, other, *slabs)
 
 
 def seat_kernel(start, per_dev, rels, packed, out):
@@ -591,7 +588,7 @@
         keep, levels = lax.optimization_barrier((keep, levels))
     other = swap(keep, 1)
     vir = vir_energy.reshape(1, -1)
-    own_energy, own = own_weights(keep, levels, vir, half)
+    own_energy, own = core_weights(False, keep, levels, vir, half)
     steps = stages(size, GATHER_TERMS)
     rels = [0]
     for step in steps:
@@ -599,7 +596,8 @@
     orbs = owner_map.shape[0]
     spots = seats(keep, orbs, local_rows, tuple(rels))
     other, spots = lax.optimization_barrier((other, spots))
-    terms, energy = gradient_terms(other, levels, vir, half, own_energy, own, slabs)
+    other_energy, other = core_weights(True, other, levels, vir, half)
+    terms, energy = gradient_terms(own_energy, own, other_energy, other, slabs)
     buf, done, ours, theirs = terms[None], 0, None, None
     for k, step in enumerate(steps):
         far = [swap(buf, mask) for mask in step]

time: 52.8 us -> 52 us (0.985)
  Pallas kernels: 17.6 us -> 16.8 us
    pallas_call x3 -> x4, Pallas kernels: 7.28 us -> 6.48 us  [the longest x1 3.17 us: gradient_terms(): pl.pallas_call(grad_kernel, in_specs=[VMEM] * (4 + PARTS), out_specs=[VME...]
  transfers between devices with their start and end apart: 16 -> 16, of which waited for: 12 -> 12; matrix products, arithmetic and copies ran while one was open for 0% -> 0% of each run, Pallas kernels for 20% -> 21%
where the time goes in v5:
time: 52 us; the launch traced here: 51.8 us
  starting transfers between devices  20.3 us (39%)
  Pallas kernels  16.8 us (32%)
  waiting for transfers between devices  12.4 us (24%)
  between operations  1.51 us (3%)
  other arithmetic  0.74 us (1%)
    ppermute x16, starting transfers between devices, swap(): return lax.ppermute(x, 'aux', [(i, i ^ mask) for i in range(size)])  20.3 us
    ppermute x16, waiting for transfers between devices, swap(): return lax.ppermute(x, 'aux', [(i, i ^ mask) for i in range(size)])  12.4 us
    pallas_call x2, Pallas kernels, retile(): pl.pallas_call(functools.partial(retile_kernel, start), in_specs=[pl.Bloc...  4.9 us
    pallas_call x1, Pallas kernels, gradient_terms(): pl.pallas_call(grad_kernel, in_specs=[VMEM] * (4 + PARTS), out_specs=[VME...  3.17 us
    pallas_call x1, Pallas kernels, half_transform(): pl.pallas_call(functools.partial(half_kernel, steps), in_specs=[VMEM] * (...  2.38 us
    pallas_call x1, Pallas kernels, prepare(): pl.pallas_call(prepare_kernel, in_specs=[far, VMEM, far, far], out_specs=...  1.55 us
    pallas_call x1, Pallas kernels, pair_slots(): pl.pallas_call(pair_kernel, in_specs=[pl.BlockSpec(memory_space=pltpu.HBM...  1.46 us
  transfers between devices with their start and end apart: 16, of which 12 were waited for; matrix products, arithmetic and copies ran while one was open for 0% of the time, Pallas kernels for 21%

profile of v5, /device:TPU:0, one launch (start us, length us, event | category | flops | bytes accessed | tf_op | source)
XLA Modules:
  0.0 51.8 jit_solution(15981180779581823916)
XLA Ops:
  0.6 4.1 %collective-permute-start = (bf16[1,16,1024]{2,1,0:T(8,128)(2,1)}, bf16[1,16,1024]{2,1,0:T(8,128)(2,1)S(1)}, u32[]{:S(2)}, u32[]{:S(2)}) collective-permute-start(bf16[1,16,1024]{2,1,0:T(8,128)(2,1)} %bitcast.20), channel_id=1, source_target_pairs={{0,8},{1,9},{2,10},{3,11},{4,12},{5,13},{6,14},{7,15},{8,0},{9,1},... | collective-permute-start | bytes 98312 | tf_op jit(solution)/shard_map/ppermute | solution.py:556
  5.4 1.5 %shard_map.95 = (s32[1,128]{1,0:T(1,128)S(1)}, bf16[1,16,1024]{2,1,0:T(8,128)(2,1)S(1)}, bf16[16,160,128]{2,1,0:T(8,128)(2,1)S(1)}, bf16[5,32,4096]{2,1,0:T(8,128)(2,1)S(1)}) custom-call(s32[1,5]{1,0:T(1,128)} %blocks.1, s32[1,1]{1,0:T(1,128)} %bitcast.10.counts, bf16[1,16,1024]{2,1,0:T(8,128)(2,1)} %bitcast.21, bf16[5,256,4096]{2,1,0:T(8,128)(2,1)} %bitcast.17), custom_call_target="tpu_custom_call" | custom-call | bytes 1310720 | tf_op jit(solution)/shard_map/pallas_call | solution.py:127
  7.2 1.8 %collective-permute-start.3 = (bf16[2,16,1024]{2,1,0:T(8,128)(2,1)S(1)}, bf16[2,16,1024]{2,1,0:T(8,128)(2,1)S(1)}, u32[]{:S(2)}, u32[]{:S(2)}) collective-permute-start(bf16[2,16,1024]{2,1,0:T(8,128)(2,1)S(1)} %pad_maximum_fusion.2), channel_id=1, source_target_pairs={{0,2},{1,3},{2,0},{3,1},{4,6},{5,7},{6,4},{7,5},{8,10},{9,11},{10,... | collective-permute-start | bytes 196616 | tf_op jit(solution)/shard_map/ppermute | solution.py:556
  9.0 1.3 %collective-permute-start.2 = (bf16[2,16,1024]{2,1,0:T(8,128)(2,1)S(1)}, bf16[2,16,1024]{2,1,0:T(8,128)(2,1)S(1)}, u32[]{:S(2)}, u32[]{:S(2)}) collective-permute-start(bf16[2,16,1024]{2,1,0:T(8,128)(2,1)S(1)} %pad_maximum_fusion.2), channel_id=1, source_target_pairs={{0,6},{1,7},{2,4},{3,5},{4,2},{5,3},{6,0},{7,1},{8,14},{9,15},{10,... | collective-permute-start | bytes 196616 | tf_op jit(solution)/shard_map/ppermute | solution.py:556
  10.3 0.5 collective-permute-start.1
  10.8 3.6 %shard_map.96 = (bf16[208,160,128]{2,1,0:T(8,128)(2,1)S(1)}, bf16[5,16,4096]{2,1,0:T(8,128)(2,1)S(1)}) custom-call(bf16[5,256,4096]{2,1,0:T(8,128)(2,1)} %bitcast.18, bf16[5,32,4096]{2,1,0:T(8,128)(2,1)S(1)} %get-tuple-element.40.raw), custom_call_target="tpu_custom_call" | custom-call | bytes 17039360 | tf_op jit(solution)/shard_map/pallas_call | solution.py:92
  14.7 1.3 %shard_map.97.refs_2_ = bf16[32,160,128]{2,1,0:T(8,128)(2,1)S(1)} custom-call(bf16[5,256,4096]{2,1,0:T(8,128)(2,1)} %bitcast.19, bf16[5,16,4096]{2,1,0:T(8,128)(2,1)S(1)} %get-tuple-element.45.raw), custom_call_target="tpu_custom_call" | custom-call | bytes 2621440 | tf_op jit(solution)/shard_map/pallas_call | solution.py:92
  16.2 2.4 %shard_map.98 = (bf16[16,128,128]{2,1,0:T(8,128)(2,1)S(1)}, f32[136,128]{1,0:T(8,128)S(1)}) custom-call(s32[1,128]{1,0:T(1,128)S(1)} %get-tuple-element.34.id_row, bf16[8,16,1024]{2,1,0:T(8,128)(2,1)S(1)} %pad_maximum_fusion.coef_a, bf16[8,16,1024]{2,1,0:T(8,128)(2,1)S(1)} %collective-permute-done.4.coef_b, ...), custom_call_target="tpu_custom_call" | custom-call | tf_op jit(solution)/shard_map/pallas_call | solution.py:301
  18.6 0.4 collective-permute-start.5
  18.9 0.3 shard_map.99
  19.3 0.6 %collective-permute-done.5 = f32[136,128]{1,0:T(8,128)S(1)} collective-permute-done((f32[136,128]{1,0:T(8,128)S(1)}, f32[136,128]{1,0:T(8,128)S(1)}, u32[]{:S(2)}, u32[]{:S(2)}) %collective-permute-start.5) | collective-permute-done | bytes 69664 | tf_op jit(solution)/shard_map/ppermute | solution.py:556
  19.9 1.4 %collective-permute-start.8 = (f32[136,128]{1,0:T(8,128)S(1)}, f32[136,128]{1,0:T(8,128)S(1)}, u32[]{:S(2)}, u32[]{:S(2)}) collective-permute-start(f32[136,128]{1,0:T(8,128)S(1)} %add.18), channel_id=1, source_target_pairs={{0,4},{1,5},{2,6},{3,7},{4,0},{5,1},{6,2},{7,3},{8,12},{9,13},{10,... | collective-permute-start | bytes 208904 | tf_op jit(solution)/shard_map/ppermute | solution.py:556
  21.3 1.5 %collective-permute-start.7 = (f32[136,128]{1,0:T(8,128)S(1)}, f32[136,128]{1,0:T(8,128)S(1)}, u32[]{:S(2)}, u32[]{:S(2)}) collective-permute-start(f32[136,128]{1,0:T(8,128)S(1)} %add.18), channel_id=1, source_target_pairs={{0,2},{1,3},{2,0},{3,1},{4,6},{5,7},{6,4},{7,5},{8,10},{9,11},{10,... | collective-permute-start | bytes 208904 | tf_op jit(solution)/shard_map/ppermute | solution.py:556
  22.8 0.6 %collective-permute-start.6 = (f32[136,128]{1,0:T(8,128)S(1)}, f32[136,128]{1,0:T(8,128)S(1)}, u32[]{:S(2)}, u32[]{:S(2)}) collective-permute-start(f32[136,128]{1,0:T(8,128)S(1)} %add.18), channel_id=1, source_target_pairs={{0,6},{1,7},{2,4},{3,5},{4,2},{5,3},{6,0},{7,1},{8,14},{9,15},{10,... | collective-permute-start | bytes 208904 | tf_op jit(solution)/shard_map/ppermute | solution.py:556
  23.5 0.9 %shard_map.100.levels = f32[16,128]{1,0:T(8,128)S(1)} custom-call(s32[16]{0:T(128)} %index.1, f32[8,128]{1,0:T(8,128)} %bitcast.22), custom_call_target="tpu_custom_call" | custom-call | bytes 1048576 | tf_op jit(solution)/shard_map/pallas_call | solution.py:163
  24.4 1.2 %collective-permute-done.7 = f32[136,128]{1,0:T(8,128)S(1)} collective-permute-done((f32[136,128]{1,0:T(8,128)S(1)}, f32[136,128]{1,0:T(8,128)S(1)}, u32[]{:S(2)}, u32[]{:S(2)}) %collective-permute-start.7) | collective-permute-done | bytes 69664 | tf_op jit(solution)/shard_map/ppermute | solution.py:556
  25.7 2.4 %collective-permute-done.6 = f32[136,128]{1,0:T(8,128)S(1)} collective-permute-done((f32[136,128]{1,0:T(8,128)S(1)}, f32[136,128]{1,0:T(8,128)S(1)}, u32[]{:S(2)}, u32[]{:S(2)}) %collective-permute-start.6) | collective-permute-done | bytes 69664 | tf_op jit(solution)/shard_map/ppermute | solution.py:556
  28.1 2.9 %collective-permute-start.9 = (f32[136,128]{1,0:T(8,128)S(1)}, f32[136,128]{1,0:T(8,128)S(1)}, u32[]{:S(2)}, u32[]{:S(2)}) collective-permute-start(f32[136,128]{1,0:T(8,128)S(1)} %add_add_fusion), channel_id=1, source_target_pairs={{0,8},{1,9},{2,10},{3,11},{4,12},{5,13},{6,14},{7,15},{8,0},{9,1},... | collective-permute-start | bytes 208904 | tf_op jit(solution)/shard_map/ppermute | solution.py:556
  31.0 3.1 %collective-permute-done.9 = f32[136,128]{1,0:T(8,128)S(1)} collective-permute-done((f32[136,128]{1,0:T(8,128)S(1)}, f32[136,128]{1,0:T(8,128)S(1)}, u32[]{:S(2)}, u32[]{:S(2)}) %collective-permute-start.9) | collective-permute-done | bytes 69664 | tf_op jit(solution)/shard_map/ppermute | solution.py:556
  34.4 0.5 shard_map.101
  34.9 0.5 %collective-permute-done.10.packed = f32[136,128]{1,0:T(8,128)S(1)} collective-permute-done((f32[136,128]{1,0:T(8,128)S(1)}, f32[136,128]{1,0:T(8,128)S(1)}, u32[]{:S(2)}, u32[]{:S(2)}) %collective-permute-start.10) | collective-permute-done | bytes 69664 | tf_op jit(solution)/shard_map/ppermute | solution.py:556
  35.4 0.5 shard_map.103
  35.9 3.2 %shard_map.104 = (f32[40,128]{1,0:T(8,128)S(1)}, f32[16,128]{1,0:T(8,128)S(1)}) custom-call(f32[8,128]{1,0:T(8,128)S(1)} %get-tuple-element.52.own_energy, f32[1024,128]{1,0:T(8,128)S(1)} %get-tuple-element.53.own, f32[8,128]{1,0:T(8,128)S(1)} %get-tuple-element.55.other_energy, f32[1024,128]{1,0:T(8,128)S(1)} %get-tuple-element.56.other, ...), custom_call_target="tpu_custom_call" | custom-call | tf_op jit(solution)/shard_map/pallas_call | solution.py:427
  39.1 2.1 %collective-permute-start.11 = (f32[1,40,128]{2,1,0:T(8,128)S(1)}, f32[1,40,128]{2,1,0:T(8,128)S(1)}, u32[]{:S(2)}, u32[]{:S(2)}) collective-permute-start(f32[1,40,128]{2,1,0:T(8,128)S(1)} %bitcast.11), channel_id=1, source_target_pairs={{0,8},{1,9},{2,10},{3,11},{4,12},{5,13},{6,14},{7,15},{8,0},{9,1},... | collective-permute-start | bytes 61448 | tf_op jit(solution)/shard_map/ppermute | solution.py:556
  41.4 2.4 %collective-permute-done.11 = f32[1,40,128]{2,1,0:T(8,128)S(1)} collective-permute-done((f32[1,40,128]{2,1,0:T(8,128)S(1)}, f32[1,40,128]{2,1,0:T(8,128)S(1)}, u32[]{:S(2)}, u32[]{:S(2)}) %collective-permute-start.11) | collective-permute-done | bytes 20512 | tf_op jit(solution)/shard_map/ppermute | solution.py:556
  43.8 0.6 %collective-permute-start.12 = (f32[2,40,128]{2,1,0:T(8,128)S(1)}, f32[2,40,128]{2,1,0:T(8,128)S(1)}, u32[]{:S(2)}, u32[]{:S(2)}) collective-permute-start(f32[2,40,128]{2,1,0:T(8,128)S(1)} %pad_maximum_fusion.3), channel_id=1, source_target_pairs={{0,2},{1,3},{2,0},{3,1},{4,6},{5,7},{6,4},{7,5},{8,10},{9,11},{10,... | collective-permute-start | bytes 122888 | tf_op jit(solution)/shard_map/ppermute | solution.py:556
  44.4 1.0 %collective-permute-start.13 = (f32[2,40,128]{2,1,0:T(8,128)S(1)}, f32[2,40,128]{2,1,0:T(8,128)S(1)}, u32[]{:S(2)}, u32[]{:S(2)}) collective-permute-start(f32[2,40,128]{2,1,0:T(8,128)S(1)} %pad_maximum_fusion.3), channel_id=1, source_target_pairs={{0,6},{1,7},{2,4},{3,5},{4,2},{5,3},{6,0},{7,1},{8,14},{9,15},{10,... | collective-permute-start | bytes 122888 | tf_op jit(solution)/shard_map/ppermute | solution.py:556
  45.3 1.9 %collective-permute-start.14 = (f32[2,40,128]{2,1,0:T(8,128)S(1)}, f32[2,40,128]{2,1,0:T(8,128)S(1)}, u32[]{:S(2)}, u32[]{:S(2)}) collective-permute-start(f32[2,40,128]{2,1,0:T(8,128)S(1)} %pad_maximum_fusion.3), channel_id=1, source_target_pairs={{0,4},{1,5},{2,6},{3,7},{4,0},{5,1},{6,2},{7,3},{8,12},{9,13},{10,... | collective-permute-start | bytes 122888 | tf_op jit(solution)/shard_map/ppermute | solution.py:556
  47.3 1.5 %shard_map.109 = f32[2]{0:T(128)} custom-call(s32[16]{0:T(128)} %owner.1, f32[16,128]{1,0:T(8,128)S(1)} %get-tuple-element.62.energy), custom_call_target="tpu_custom_call" | custom-call | bytes 1048576 | tf_op jit(solution)/shard_map/pallas_call | solution.py:543
  49.4 0.3 collective-permute-done.14.piece
  50.2 1.0 %collective-permute-done.15 = f32[16,1024]{1,0:T(8,128)S(1)} collective-permute-done((f32[16,1024]{1,0:T(8,128)S(1)}, f32[16,1024]{1,0:T(8,128)S(1)}, u32[]{:S(2)}, u32[]{:S(2)}) %collective-permute-start.15) | collective-permute-done | bytes 65568 | tf_op jit(solution)/shard_map/ppermute | solution.py:556
  51.1 0.6 %add_bitcast_fusion = f32[1024,16]{0,1:T(8,128)} fusion(f32[16,1024]{1,0:T(8,128)S(1)} %shard_map.110, f32[16,1024]{1,0:T(8,128)S(1)} %collective-permute-done.15), kind=kLoop, calls=%fused_computation.4 | loop fusion | flops 16384 | bytes 196608 | tf_op jit(solution)/shard_map/transpose | solution.py:617
  (30 shorter events, 2.3 us)
Async XLA Ops:
  0.6 6.6 %collective-permute-start = (bf16[1,16,1024]{2,1,0:T(8,128)(2,1)}, bf16[1,16,1024]{2,1,0:T(8,128)(2,1)S(1)}, u32[]{:S(2)}, u32[]{:S(2)}) collective-permute-start(bf16[1,16,1024]{2,1,0:T(8,128)(2,1)} %bitcast.20), channel_id=1, source_target_pairs={{0,8},{1,9},{2,10},{3,11},{4,12},{5,13},{6,14},{7,15},{8,0},{9,1},... | collective-permute-start | bytes 98312 | tf_op jit(solution)/shard_map/ppermute | solution.py:556
  7.2 7.1 %collective-permute-start.3 = (bf16[2,16,1024]{2,1,0:T(8,128)(2,1)S(1)}, bf16[2,16,1024]{2,1,0:T(8,128)(2,1)S(1)}, u32[]{:S(2)}, u32[]{:S(2)}) collective-permute-start(bf16[2,16,1024]{2,1,0:T(8,128)(2,1)S(1)} %pad_maximum_fusion.2), channel_id=1, source_target_pairs={{0,2},{1,3},{2,0},{3,1},{4,6},{5,7},{6,4},{7,5},{8,10},{9,11},{10,... | collective-permute-start | bytes 196616 | tf_op jit(solution)/shard_map/ppermute | solution.py:556
  9.0 5.4 %collective-permute-start.2 = (bf16[2,16,1024]{2,1,0:T(8,128)(2,1)S(1)}, bf16[2,16,1024]{2,1,0:T(8,128)(2,1)S(1)}, u32[]{:S(2)}, u32[]{:S(2)}) collective-permute-start(bf16[2,16,1024]{2,1,0:T(8,128)(2,1)S(1)} %pad_maximum_fusion.2), channel_id=1, source_target_pairs={{0,6},{1,7},{2,4},{3,5},{4,2},{5,3},{6,0},{7,1},{8,14},{9,15},{10,... | collective-permute-start | bytes 196616 | tf_op jit(solution)/shard_map/ppermute | solution.py:556
  10.3 4.3 %collective-permute-start.1 = (bf16[2,16,1024]{2,1,0:T(8,128)(2,1)S(1)}, bf16[2,16,1024]{2,1,0:T(8,128)(2,1)S(1)}, u32[]{:S(2)}, u32[]{:S(2)}) collective-permute-start(bf16[2,16,1024]{2,1,0:T(8,128)(2,1)S(1)} %pad_maximum_fusion.2), channel_id=1, source_target_pairs={{0,4},{1,5},{2,6},{3,7},{4,0},{5,1},{6,2},{7,3},{8,12},{9,13},{10,... | collective-permute-start | bytes 196616 | tf_op jit(solution)/shard_map/ppermute | solution.py:556
  14.6 1.6 %collective-permute-start.4 = (bf16[8,16,1024]{2,1,0:T(8,128)(2,1)S(1)}, bf16[8,16,1024]{2,1,0:T(8,128)(2,1)S(1)}, u32[]{:S(2)}, u32[]{:S(2)}) collective-permute-start(bf16[8,16,1024]{2,1,0:T(8,128)(2,1)S(1)} %pad_maximum_fusion.coef_a), channel_id=1, source_target_pairs={{0,1},{1,0},{2,3},{3,2},{4,5},{5,4},{6,7},{7,6},{8,9},{9,8},{10,11... | collective-permute-start | bytes 786440 | tf_op jit(solution)/shard_map/ppermute | solution.py:556
  16.0 18.4 %copy-start = (f32[64]{0:T(128)S(1)}, f32[64]{0:T(128)}, u32[]{:S(2)}) copy-start(f32[64]{0:T(128)} %param.14) | copy-start | bytes 772
  18.6 1.3 %collective-permute-start.5 = (f32[136,128]{1,0:T(8,128)S(1)}, f32[136,128]{1,0:T(8,128)S(1)}, u32[]{:S(2)}, u32[]{:S(2)}) collective-permute-start(f32[136,128]{1,0:T(8,128)S(1)} %get-tuple-element.47), channel_id=1, source_target_pairs={{0,1},{1,0},{2,3},{3,2},{4,5},{5,4},{6,7},{7,6},{8,9},{9,8},{10,11... | collective-permute-start | bytes 208904 | tf_op jit(solution)/shard_map/ppermute | solution.py:556
  19.9 4.5 %collective-permute-start.8 = (f32[136,128]{1,0:T(8,128)S(1)}, f32[136,128]{1,0:T(8,128)S(1)}, u32[]{:S(2)}, u32[]{:S(2)}) collective-permute-start(f32[136,128]{1,0:T(8,128)S(1)} %add.18), channel_id=1, source_target_pairs={{0,4},{1,5},{2,6},{3,7},{4,0},{5,1},{6,2},{7,3},{8,12},{9,13},{10,... | collective-permute-start | bytes 208904 | tf_op jit(solution)/shard_map/ppermute | solution.py:556
  21.3 4.3 %collective-permute-start.7 = (f32[136,128]{1,0:T(8,128)S(1)}, f32[136,128]{1,0:T(8,128)S(1)}, u32[]{:S(2)}, u32[]{:S(2)}) collective-permute-start(f32[136,128]{1,0:T(8,128)S(1)} %add.18), channel_id=1, source_target_pairs={{0,2},{1,3},{2,0},{3,1},{4,6},{5,7},{6,4},{7,5},{8,10},{9,11},{10,... | collective-permute-start | bytes 208904 | tf_op jit(solution)/shard_map/ppermute | solution.py:556
  22.8 5.2 %collective-permute-start.6 = (f32[136,128]{1,0:T(8,128)S(1)}, f32[136,128]{1,0:T(8,128)S(1)}, u32[]{:S(2)}, u32[]{:S(2)}) collective-permute-start(f32[136,128]{1,0:T(8,128)S(1)} %add.18), channel_id=1, source_target_pairs={{0,6},{1,7},{2,4},{3,5},{4,2},{5,3},{6,0},{7,1},{8,14},{9,15},{10,... | collective-permute-start | bytes 208904 | tf_op jit(solution)/shard_map/ppermute | solution.py:556
  28.1 6.0 %collective-permute-start.9 = (f32[136,128]{1,0:T(8,128)S(1)}, f32[136,128]{1,0:T(8,128)S(1)}, u32[]{:S(2)}, u32[]{:S(2)}) collective-permute-start(f32[136,128]{1,0:T(8,128)S(1)} %add_add_fusion), channel_id=1, source_target_pairs={{0,8},{1,9},{2,10},{3,11},{4,12},{5,13},{6,14},{7,15},{8,0},{9,1},... | collective-permute-start | bytes 208904 | tf_op jit(solution)/shard_map/ppermute | solution.py:556
  34.1 1.3 %collective-permute-start.10 = (f32[136,128]{1,0:T(8,128)S(1)}, f32[136,128]{1,0:T(8,128)S(1)}, u32[]{:S(2)}, u32[]{:S(2)}) collective-permute-start(f32[136,128]{1,0:T(8,128)S(1)} %add.22.packed), channel_id=1, source_target_pairs={{0,1},{1,0},{2,3},{3,2},{4,5},{5,4},{6,7},{7,6},{8,9},{9,8},{10,11... | collective-permute-start | bytes 208904 | tf_op jit(solution)/shard_map/ppermute | solution.py:556
  39.1 4.7 %collective-permute-start.11 = (f32[1,40,128]{2,1,0:T(8,128)S(1)}, f32[1,40,128]{2,1,0:T(8,128)S(1)}, u32[]{:S(2)}, u32[]{:S(2)}) collective-permute-start(f32[1,40,128]{2,1,0:T(8,128)S(1)} %bitcast.11), channel_id=1, source_target_pairs={{0,8},{1,9},{2,10},{3,11},{4,12},{5,13},{6,14},{7,15},{8,0},{9,1},... | collective-permute-start | bytes 61448 | tf_op jit(solution)/shard_map/ppermute | solution.py:556
  43.8 5.2 %collective-permute-start.12 = (f32[2,40,128]{2,1,0:T(8,128)S(1)}, f32[2,40,128]{2,1,0:T(8,128)S(1)}, u32[]{:S(2)}, u32[]{:S(2)}) collective-permute-start(f32[2,40,128]{2,1,0:T(8,128)S(1)} %pad_maximum_fusion.3), channel_id=1, source_target_pairs={{0,2},{1,3},{2,0},{3,1},{4,6},{5,7},{6,4},{7,5},{8,10},{9,11},{10,... | collective-permute-start | bytes 122888 | tf_op jit(solution)/shard_map/ppermute | solution.py:556
  44.4 4.9 %collective-permute-start.13 = (f32[2,40,128]{2,1,0:T(8,128)S(1)}, f32[2,40,128]{2,1,0:T(8,128)S(1)}, u32[]{:S(2)}, u32[]{:S(2)}) collective-permute-start(f32[2,40,128]{2,1,0:T(8,128)S(1)} %pad_maximum_fusion.3), channel_id=1, source_target_pairs={{0,6},{1,7},{2,4},{3,5},{4,2},{5,3},{6,0},{7,1},{8,14},{9,15},{10,... | collective-permute-start | bytes 122888 | tf_op jit(solution)/shard_map/ppermute | solution.py:556
  45.3 4.4 %collective-permute-start.14 = (f32[2,40,128]{2,1,0:T(8,128)S(1)}, f32[2,40,128]{2,1,0:T(8,128)S(1)}, u32[]{:S(2)}, u32[]{:S(2)}) collective-permute-start(f32[2,40,128]{2,1,0:T(8,128)S(1)} %pad_maximum_fusion.3), channel_id=1, source_target_pairs={{0,4},{1,5},{2,6},{3,7},{4,0},{5,1},{6,2},{7,3},{8,12},{9,13},{10,... | collective-permute-start | bytes 122888 | tf_op jit(solution)/shard_map/ppermute | solution.py:556
  49.8 1.3 %collective-permute-start.15 = (f32[16,1024]{1,0:T(8,128)S(1)}, f32[16,1024]{1,0:T(8,128)S(1)}, u32[]{:S(2)}, u32[]{:S(2)}) collective-permute-start(f32[16,1024]{1,0:T(8,128)S(1)} %shard_map.113), channel_id=1, source_target_pairs={{0,1},{1,0},{2,3},{3,2},{4,5},{5,4},{6,7},{7,6},{8,9},{9,8},{10,11... | collective-permute-start | bytes 196616 | tf_op jit(solution)/shard_map/ppermute | solution.py:556

commit v6 on v5

--- a/solution.py
+++ b/solution.py
@@ -17,7 +17,7 @@
 PARTS = 3
 GATHER_COEF = (1, 2, 0)
 SUM_INTS = (2, 0, 1)
-GATHER_TERMS = (0, 2, 1)
+GATHER_TERMS = (2, 0, 1)
 SEAT = 8
 SEATS = LANES // SEAT
 TERM_TILES = -(-S * BW // LANES)

time: 52 us -> 51.7 us (level)
  transfers between devices with their start and end apart: 16 -> 16, of which waited for: 12 -> 11; matrix products, arithmetic and copies ran while one was open for 0% -> 0% of each run, Pallas kernels for 21% -> 21%
where the time goes in v6:
time: 51.7 us; the launch traced here: 51.4 us
  starting transfers between devices  20.3 us (39%)
  Pallas kernels  16.8 us (32%)
  waiting for transfers between devices  12 us (23%)
  between operations  1.52 us (3%)
  other arithmetic  0.74 us (1%)
    ppermute x16, starting transfers between devices, swap(): return lax.ppermute(x, 'aux', [(i, i ^ mask) for i in range(size)])  20.3 us
    ppermute x16, waiting for transfers between devices, swap(): return lax.ppermute(x, 'aux', [(i, i ^ mask) for i in range(size)])  12 us
    pallas_call x2, Pallas kernels, retile(): pl.pallas_call(functools.partial(retile_kernel, start), in_specs=[pl.Bloc...  4.9 us
    pallas_call x1, Pallas kernels, gradient_terms(): pl.pallas_call(grad_kernel, in_specs=[VMEM] * (4 + PARTS), out_specs=[VME...  3.17 us
    pallas_call x1, Pallas kernels, half_transform(): pl.pallas_call(functools.partial(half_kernel, steps), in_specs=[VMEM] * (...  2.38 us
    pallas_call x1, Pallas kernels, prepare(): pl.pallas_call(prepare_kernel, in_specs=[far, VMEM, far, far], out_specs=...  1.55 us
    pallas_call x1, Pallas kernels, pair_slots(): pl.pallas_call(pair_kernel, in_specs=[pl.BlockSpec(memory_space=pltpu.HBM...  1.46 us
  transfers between devices with their start and end apart: 16, of which 11 were waited for; matrix products, arithmetic and copies ran while one was open for 0% of the time, Pallas kernels for 21%

profile of v6, /device:TPU:0, one launch (start us, length us, event | category | flops | bytes accessed | tf_op | source)
XLA Modules:
  0.0 51.4 jit_solution(7086216296845184357)
XLA Ops:
  0.6 4.1 %collective-permute-start = (bf16[1,16,1024]{2,1,0:T(8,128)(2,1)}, bf16[1,16,1024]{2,1,0:T(8,128)(2,1)S(1)}, u32[]{:S(2)}, u32[]{:S(2)}) collective-permute-start(bf16[1,16,1024]{2,1,0:T(8,128)(2,1)} %bitcast.20), channel_id=1, source_target_pairs={{0,8},{1,9},{2,10},{3,11},{4,12},{5,13},{6,14},{7,15},{8,0},{9,1},... | collective-permute-start | bytes 98312 | tf_op jit(solution)/shard_map/ppermute | solution.py:556
  5.4 1.5 %shard_map.95 = (s32[1,128]{1,0:T(1,128)S(1)}, bf16[1,16,1024]{2,1,0:T(8,128)(2,1)S(1)}, bf16[16,160,128]{2,1,0:T(8,128)(2,1)S(1)}, bf16[5,32,4096]{2,1,0:T(8,128)(2,1)S(1)}) custom-call(s32[1,5]{1,0:T(1,128)} %blocks.1, s32[1,1]{1,0:T(1,128)} %bitcast.10.counts, bf16[1,16,1024]{2,1,0:T(8,128)(2,1)} %bitcast.21, bf16[5,256,4096]{2,1,0:T(8,128)(2,1)} %bitcast.17), custom_call_target="tpu_custom_call" | custom-call | bytes 1310720 | tf_op jit(solution)/shard_map/pallas_call | solution.py:127
  6.9 0.2 collective-permute-done
  7.2 1.8 %collective-permute-start.3 = (bf16[2,16,1024]{2,1,0:T(8,128)(2,1)S(1)}, bf16[2,16,1024]{2,1,0:T(8,128)(2,1)S(1)}, u32[]{:S(2)}, u32[]{:S(2)}) collective-permute-start(bf16[2,16,1024]{2,1,0:T(8,128)(2,1)S(1)} %pad_maximum_fusion.2), channel_id=1, source_target_pairs={{0,2},{1,3},{2,0},{3,1},{4,6},{5,7},{6,4},{7,5},{8,10},{9,11},{10,... | collective-permute-start | bytes 196616 | tf_op jit(solution)/shard_map/ppermute | solution.py:556
  9.0 1.3 %collective-permute-start.2 = (bf16[2,16,1024]{2,1,0:T(8,128)(2,1)S(1)}, bf16[2,16,1024]{2,1,0:T(8,128)(2,1)S(1)}, u32[]{:S(2)}, u32[]{:S(2)}) collective-permute-start(bf16[2,16,1024]{2,1,0:T(8,128)(2,1)S(1)} %pad_maximum_fusion.2), channel_id=1, source_target_pairs={{0,6},{1,7},{2,4},{3,5},{4,2},{5,3},{6,0},{7,1},{8,14},{9,15},{10,... | collective-permute-start | bytes 196616 | tf_op jit(solution)/shard_map/ppermute | solution.py:556
  10.3 0.5 collective-permute-start.1
  10.8 3.6 %shard_map.96 = (bf16[208,160,128]{2,1,0:T(8,128)(2,1)S(1)}, bf16[5,16,4096]{2,1,0:T(8,128)(2,1)S(1)}) custom-call(bf16[5,256,4096]{2,1,0:T(8,128)(2,1)} %bitcast.18, bf16[5,32,4096]{2,1,0:T(8,128)(2,1)S(1)} %get-tuple-element.40.raw), custom_call_target="tpu_custom_call" | custom-call | bytes 17039360 | tf_op jit(solution)/shard_map/pallas_call | solution.py:92
  14.7 1.3 %shard_map.97.refs_2_ = bf16[32,160,128]{2,1,0:T(8,128)(2,1)S(1)} custom-call(bf16[5,256,4096]{2,1,0:T(8,128)(2,1)} %bitcast.19, bf16[5,16,4096]{2,1,0:T(8,128)(2,1)S(1)} %get-tuple-element.45.raw), custom_call_target="tpu_custom_call" | custom-call | bytes 2621440 | tf_op jit(solution)/shard_map/pallas_call | solution.py:92
  16.2 2.4 %shard_map.98 = (bf16[16,128,128]{2,1,0:T(8,128)(2,1)S(1)}, f32[136,128]{1,0:T(8,128)S(1)}) custom-call(s32[1,128]{1,0:T(1,128)S(1)} %get-tuple-element.34.id_row, bf16[8,16,1024]{2,1,0:T(8,128)(2,1)S(1)} %pad_maximum_fusion.coef_a, bf16[8,16,1024]{2,1,0:T(8,128)(2,1)S(1)} %collective-permute-done.4.coef_b, ...), custom_call_target="tpu_custom_call" | custom-call | tf_op jit(solution)/shard_map/pallas_call | solution.py:301
  18.6 0.4 collective-permute-start.5
  18.9 0.3 shard_map.99
  19.3 0.6 %collective-permute-done.5 = f32[136,128]{1,0:T(8,128)S(1)} collective-permute-done((f32[136,128]{1,0:T(8,128)S(1)}, f32[136,128]{1,0:T(8,128)S(1)}, u32[]{:S(2)}, u32[]{:S(2)}) %collective-permute-start.5) | collective-permute-done | bytes 69664 | tf_op jit(solution)/shard_map/ppermute | solution.py:556
  19.9 1.4 %collective-permute-start.8 = (f32[136,128]{1,0:T(8,128)S(1)}, f32[136,128]{1,0:T(8,128)S(1)}, u32[]{:S(2)}, u32[]{:S(2)}) collective-permute-start(f32[136,128]{1,0:T(8,128)S(1)} %add.18), channel_id=1, source_target_pairs={{0,4},{1,5},{2,6},{3,7},{4,0},{5,1},{6,2},{7,3},{8,12},{9,13},{10,... | collective-permute-start | bytes 208904 | tf_op jit(solution)/shard_map/ppermute | solution.py:556
  21.3 1.5 %collective-permute-start.7 = (f32[136,128]{1,0:T(8,128)S(1)}, f32[136,128]{1,0:T(8,128)S(1)}, u32[]{:S(2)}, u32[]{:S(2)}) collective-permute-start(f32[136,128]{1,0:T(8,128)S(1)} %add.18), channel_id=1, source_target_pairs={{0,2},{1,3},{2,0},{3,1},{4,6},{5,7},{6,4},{7,5},{8,10},{9,11},{10,... | collective-permute-start | bytes 208904 | tf_op jit(solution)/shard_map/ppermute | solution.py:556
  22.8 0.6 %collective-permute-start.6 = (f32[136,128]{1,0:T(8,128)S(1)}, f32[136,128]{1,0:T(8,128)S(1)}, u32[]{:S(2)}, u32[]{:S(2)}) collective-permute-start(f32[136,128]{1,0:T(8,128)S(1)} %add.18), channel_id=1, source_target_pairs={{0,6},{1,7},{2,4},{3,5},{4,2},{5,3},{6,0},{7,1},{8,14},{9,15},{10,... | collective-permute-start | bytes 208904 | tf_op jit(solution)/shard_map/ppermute | solution.py:556
  23.5 0.9 %shard_map.100.levels = f32[16,128]{1,0:T(8,128)S(1)} custom-call(s32[16]{0:T(128)} %index.1, f32[8,128]{1,0:T(8,128)} %bitcast.22), custom_call_target="tpu_custom_call" | custom-call | bytes 1048576 | tf_op jit(solution)/shard_map/pallas_call | solution.py:163
  24.4 1.2 %collective-permute-done.7 = f32[136,128]{1,0:T(8,128)S(1)} collective-permute-done((f32[136,128]{1,0:T(8,128)S(1)}, f32[136,128]{1,0:T(8,128)S(1)}, u32[]{:S(2)}, u32[]{:S(2)}) %collective-permute-start.7) | collective-permute-done | bytes 69664 | tf_op jit(solution)/shard_map/ppermute | solution.py:556
  25.7 2.4 %collective-permute-done.6 = f32[136,128]{1,0:T(8,128)S(1)} collective-permute-done((f32[136,128]{1,0:T(8,128)S(1)}, f32[136,128]{1,0:T(8,128)S(1)}, u32[]{:S(2)}, u32[]{:S(2)}) %collective-permute-start.6) | collective-permute-done | bytes 69664 | tf_op jit(solution)/shard_map/ppermute | solution.py:556
  28.1 2.9 %collective-permute-start.9 = (f32[136,128]{1,0:T(8,128)S(1)}, f32[136,128]{1,0:T(8,128)S(1)}, u32[]{:S(2)}, u32[]{:S(2)}) collective-permute-start(f32[136,128]{1,0:T(8,128)S(1)} %add_add_fusion), channel_id=1, source_target_pairs={{0,8},{1,9},{2,10},{3,11},{4,12},{5,13},{6,14},{7,15},{8,0},{9,1},... | collective-permute-start | bytes 208904 | tf_op jit(solution)/shard_map/ppermute | solution.py:556
  31.0 3.1 %collective-permute-done.9 = f32[136,128]{1,0:T(8,128)S(1)} collective-permute-done((f32[136,128]{1,0:T(8,128)S(1)}, f32[136,128]{1,0:T(8,128)S(1)}, u32[]{:S(2)}, u32[]{:S(2)}) %collective-permute-start.9) | collective-permute-done | bytes 69664 | tf_op jit(solution)/shard_map/ppermute | solution.py:556
  34.2 0.2 shard_map.102.spots
  34.4 0.5 shard_map.101
  34.9 0.5 %collective-permute-done.10.packed = f32[136,128]{1,0:T(8,128)S(1)} collective-permute-done((f32[136,128]{1,0:T(8,128)S(1)}, f32[136,128]{1,0:T(8,128)S(1)}, u32[]{:S(2)}, u32[]{:S(2)}) %collective-permute-start.10) | collective-permute-done | bytes 69664 | tf_op jit(solution)/shard_map/ppermute | solution.py:556
  35.4 0.5 shard_map.103
  35.9 3.2 %shard_map.104 = (f32[40,128]{1,0:T(8,128)S(1)}, f32[16,128]{1,0:T(8,128)S(1)}) custom-call(f32[8,128]{1,0:T(8,128)S(1)} %get-tuple-element.52.own_energy, f32[1024,128]{1,0:T(8,128)S(1)} %get-tuple-element.53.own, f32[8,128]{1,0:T(8,128)S(1)} %get-tuple-element.55.other_energy, f32[1024,128]{1,0:T(8,128)S(1)} %get-tuple-element.56.other, ...), custom_call_target="tpu_custom_call" | custom-call | tf_op jit(solution)/shard_map/pallas_call | solution.py:427
  39.1 2.1 %collective-permute-start.11 = (f32[1,40,128]{2,1,0:T(8,128)S(1)}, f32[1,40,128]{2,1,0:T(8,128)S(1)}, u32[]{:S(2)}, u32[]{:S(2)}) collective-permute-start(f32[1,40,128]{2,1,0:T(8,128)S(1)} %bitcast.11), channel_id=1, source_target_pairs={{0,8},{1,9},{2,10},{3,11},{4,12},{5,13},{6,14},{7,15},{8,0},{9,1},... | collective-permute-start | bytes 61448 | tf_op jit(solution)/shard_map/ppermute | solution.py:556
  41.4 2.4 %collective-permute-done.11 = f32[1,40,128]{2,1,0:T(8,128)S(1)} collective-permute-done((f32[1,40,128]{2,1,0:T(8,128)S(1)}, f32[1,40,128]{2,1,0:T(8,128)S(1)}, u32[]{:S(2)}, u32[]{:S(2)}) %collective-permute-start.11) | collective-permute-done | bytes 20512 | tf_op jit(solution)/shard_map/ppermute | solution.py:556
  43.9 1.4 %collective-permute-start.13 = (f32[2,40,128]{2,1,0:T(8,128)S(1)}, f32[2,40,128]{2,1,0:T(8,128)S(1)}, u32[]{:S(2)}, u32[]{:S(2)}) collective-permute-start(f32[2,40,128]{2,1,0:T(8,128)S(1)} %pad_maximum_fusion.3), channel_id=1, source_target_pairs={{0,2},{1,3},{2,0},{3,1},{4,6},{5,7},{6,4},{7,5},{8,10},{9,11},{10,... | collective-permute-start | bytes 122888 | tf_op jit(solution)/shard_map/ppermute | solution.py:556
  45.3 1.9 %collective-permute-start.14 = (f32[2,40,128]{2,1,0:T(8,128)S(1)}, f32[2,40,128]{2,1,0:T(8,128)S(1)}, u32[]{:S(2)}, u32[]{:S(2)}) collective-permute-start(f32[2,40,128]{2,1,0:T(8,128)S(1)} %pad_maximum_fusion.3), channel_id=1, source_target_pairs={{0,4},{1,5},{2,6},{3,7},{4,0},{5,1},{6,2},{7,3},{8,12},{9,13},{10,... | collective-permute-start | bytes 122888 | tf_op jit(solution)/shard_map/ppermute | solution.py:556
  47.3 1.5 %shard_map.109 = f32[2]{0:T(128)} custom-call(s32[16]{0:T(128)} %owner.1, f32[16,128]{1,0:T(8,128)S(1)} %get-tuple-element.62.energy), custom_call_target="tpu_custom_call" | custom-call | bytes 1048576 | tf_op jit(solution)/shard_map/pallas_call | solution.py:543
  49.8 1.0 %collective-permute-done.15 = f32[16,1024]{1,0:T(8,128)S(1)} collective-permute-done((f32[16,1024]{1,0:T(8,128)S(1)}, f32[16,1024]{1,0:T(8,128)S(1)}, u32[]{:S(2)}, u32[]{:S(2)}) %collective-permute-start.15) | collective-permute-done | bytes 65568 | tf_op jit(solution)/shard_map/ppermute | solution.py:556
  50.8 0.6 %add_bitcast_fusion = f32[1024,16]{0,1:T(8,128)} fusion(f32[16,1024]{1,0:T(8,128)S(1)} %shard_map.110, f32[16,1024]{1,0:T(8,128)S(1)} %collective-permute-done.15), kind=kLoop, calls=%fused_computation.4 | loop fusion | flops 16384 | bytes 196608 | tf_op jit(solution)/shard_map/transpose | solution.py:617
  (30 shorter events, 1.9 us)
Async XLA Ops:
  0.6 6.6 %collective-permute-start = (bf16[1,16,1024]{2,1,0:T(8,128)(2,1)}, bf16[1,16,1024]{2,1,0:T(8,128)(2,1)S(1)}, u32[]{:S(2)}, u32[]{:S(2)}) collective-permute-start(bf16[1,16,1024]{2,1,0:T(8,128)(2,1)} %bitcast.20), channel_id=1, source_target_pairs={{0,8},{1,9},{2,10},{3,11},{4,12},{5,13},{6,14},{7,15},{8,0},{9,1},... | collective-permute-start | bytes 98312 | tf_op jit(solution)/shard_map/ppermute | solution.py:556
  7.2 7.1 %collective-permute-start.3 = (bf16[2,16,1024]{2,1,0:T(8,128)(2,1)S(1)}, bf16[2,16,1024]{2,1,0:T(8,128)(2,1)S(1)}, u32[]{:S(2)}, u32[]{:S(2)}) collective-permute-start(bf16[2,16,1024]{2,1,0:T(8,128)(2,1)S(1)} %pad_maximum_fusion.2), channel_id=1, source_target_pairs={{0,2},{1,3},{2,0},{3,1},{4,6},{5,7},{6,4},{7,5},{8,10},{9,11},{10,... | collective-permute-start | bytes 196616 | tf_op jit(solution)/shard_map/ppermute | solution.py:556
  9.0 5.4 %collective-permute-start.2 = (bf16[2,16,1024]{2,1,0:T(8,128)(2,1)S(1)}, bf16[2,16,1024]{2,1,0:T(8,128)(2,1)S(1)}, u32[]{:S(2)}, u32[]{:S(2)}) collective-permute-start(bf16[2,16,1024]{2,1,0:T(8,128)(2,1)S(1)} %pad_maximum_fusion.2), channel_id=1, source_target_pairs={{0,6},{1,7},{2,4},{3,5},{4,2},{5,3},{6,0},{7,1},{8,14},{9,15},{10,... | collective-permute-start | bytes 196616 | tf_op jit(solution)/shard_map/ppermute | solution.py:556
  10.3 4.3 %collective-permute-start.1 = (bf16[2,16,1024]{2,1,0:T(8,128)(2,1)S(1)}, bf16[2,16,1024]{2,1,0:T(8,128)(2,1)S(1)}, u32[]{:S(2)}, u32[]{:S(2)}) collective-permute-start(bf16[2,16,1024]{2,1,0:T(8,128)(2,1)S(1)} %pad_maximum_fusion.2), channel_id=1, source_target_pairs={{0,4},{1,5},{2,6},{3,7},{4,0},{5,1},{6,2},{7,3},{8,12},{9,13},{10,... | collective-permute-start | bytes 196616 | tf_op jit(solution)/shard_map/ppermute | solution.py:556
  14.6 1.6 %collective-permute-start.4 = (bf16[8,16,1024]{2,1,0:T(8,128)(2,1)S(1)}, bf16[8,16,1024]{2,1,0:T(8,128)(2,1)S(1)}, u32[]{:S(2)}, u32[]{:S(2)}) collective-permute-start(bf16[8,16,1024]{2,1,0:T(8,128)(2,1)S(1)} %pad_maximum_fusion.coef_a), channel_id=1, source_target_pairs={{0,1},{1,0},{2,3},{3,2},{4,5},{5,4},{6,7},{7,6},{8,9},{9,8},{10,11... | collective-permute-start | bytes 786440 | tf_op jit(solution)/shard_map/ppermute | solution.py:556
  16.0 18.4 %copy-start = (f32[64]{0:T(128)S(1)}, f32[64]{0:T(128)}, u32[]{:S(2)}) copy-start(f32[64]{0:T(128)} %param.14) | copy-start | bytes 772
  18.6 1.3 %collective-permute-start.5 = (f32[136,128]{1,0:T(8,128)S(1)}, f32[136,128]{1,0:T(8,128)S(1)}, u32[]{:S(2)}, u32[]{:S(2)}) collective-permute-start(f32[136,128]{1,0:T(8,128)S(1)} %get-tuple-element.47), channel_id=1, source_target_pairs={{0,1},{1,0},{2,3},{3,2},{4,5},{5,4},{6,7},{7,6},{8,9},{9,8},{10,11... | collective-permute-start | bytes 208904 | tf_op jit(solution)/shard_map/ppermute | solution.py:556
  19.9 4.5 %collective-permute-start.8 = (f32[136,128]{1,0:T(8,128)S(1)}, f32[136,128]{1,0:T(8,128)S(1)}, u32[]{:S(2)}, u32[]{:S(2)}) collective-permute-start(f32[136,128]{1,0:T(8,128)S(1)} %add.18), channel_id=1, source_target_pairs={{0,4},{1,5},{2,6},{3,7},{4,0},{5,1},{6,2},{7,3},{8,12},{9,13},{10,... | collective-permute-start | bytes 208904 | tf_op jit(solution)/shard_map/ppermute | solution.py:556
  21.3 4.3 %collective-permute-start.7 = (f32[136,128]{1,0:T(8,128)S(1)}, f32[136,128]{1,0:T(8,128)S(1)}, u32[]{:S(2)}, u32[]{:S(2)}) collective-permute-start(f32[136,128]{1,0:T(8,128)S(1)} %add.18), channel_id=1, source_target_pairs={{0,2},{1,3},{2,0},{3,1},{4,6},{5,7},{6,4},{7,5},{8,10},{9,11},{10,... | collective-permute-start | bytes 208904 | tf_op jit(solution)/shard_map/ppermute | solution.py:556
  22.8 5.2 %collective-permute-start.6 = (f32[136,128]{1,0:T(8,128)S(1)}, f32[136,128]{1,0:T(8,128)S(1)}, u32[]{:S(2)}, u32[]{:S(2)}) collective-permute-start(f32[136,128]{1,0:T(8,128)S(1)} %add.18), channel_id=1, source_target_pairs={{0,6},{1,7},{2,4},{3,5},{4,2},{5,3},{6,0},{7,1},{8,14},{9,15},{10,... | collective-permute-start | bytes 208904 | tf_op jit(solution)/shard_map/ppermute | solution.py:556
  28.1 6.0 %collective-permute-start.9 = (f32[136,128]{1,0:T(8,128)S(1)}, f32[136,128]{1,0:T(8,128)S(1)}, u32[]{:S(2)}, u32[]{:S(2)}) collective-permute-start(f32[136,128]{1,0:T(8,128)S(1)} %add_add_fusion), channel_id=1, source_target_pairs={{0,8},{1,9},{2,10},{3,11},{4,12},{5,13},{6,14},{7,15},{8,0},{9,1},... | collective-permute-start | bytes 208904 | tf_op jit(solution)/shard_map/ppermute | solution.py:556
  34.1 1.3 %collective-permute-start.10 = (f32[136,128]{1,0:T(8,128)S(1)}, f32[136,128]{1,0:T(8,128)S(1)}, u32[]{:S(2)}, u32[]{:S(2)}) collective-permute-start(f32[136,128]{1,0:T(8,128)S(1)} %add.22.packed), channel_id=1, source_target_pairs={{0,1},{1,0},{2,3},{3,2},{4,5},{5,4},{6,7},{7,6},{8,9},{9,8},{10,11... | collective-permute-start | bytes 208904 | tf_op jit(solution)/shard_map/ppermute | solution.py:556
  39.1 4.7 %collective-permute-start.11 = (f32[1,40,128]{2,1,0:T(8,128)S(1)}, f32[1,40,128]{2,1,0:T(8,128)S(1)}, u32[]{:S(2)}, u32[]{:S(2)}) collective-permute-start(f32[1,40,128]{2,1,0:T(8,128)S(1)} %bitcast.11), channel_id=1, source_target_pairs={{0,8},{1,9},{2,10},{3,11},{4,12},{5,13},{6,14},{7,15},{8,0},{9,1},... | collective-permute-start | bytes 61448 | tf_op jit(solution)/shard_map/ppermute | solution.py:556
  43.8 5.2 %collective-permute-start.12 = (f32[2,40,128]{2,1,0:T(8,128)S(1)}, f32[2,40,128]{2,1,0:T(8,128)S(1)}, u32[]{:S(2)}, u32[]{:S(2)}) collective-permute-start(f32[2,40,128]{2,1,0:T(8,128)S(1)} %pad_maximum_fusion.3), channel_id=1, source_target_pairs={{0,6},{1,7},{2,4},{3,5},{4,2},{5,3},{6,0},{7,1},{8,14},{9,15},{10,... | collective-permute-start | bytes 122888 | tf_op jit(solution)/shard_map/ppermute | solution.py:556
  43.9 5.2 %collective-permute-start.13 = (f32[2,40,128]{2,1,0:T(8,128)S(1)}, f32[2,40,128]{2,1,0:T(8,128)S(1)}, u32[]{:S(2)}, u32[]{:S(2)}) collective-permute-start(f32[2,40,128]{2,1,0:T(8,128)S(1)} %pad_maximum_fusion.3), channel_id=1, source_target_pairs={{0,2},{1,3},{2,0},{3,1},{4,6},{5,7},{6,4},{7,5},{8,10},{9,11},{10,... | collective-permute-start | bytes 122888 | tf_op jit(solution)/shard_map/ppermute | solution.py:556
  45.3 4.0 %collective-permute-start.14 = (f32[2,40,128]{2,1,0:T(8,128)S(1)}, f32[2,40,128]{2,1,0:T(8,128)S(1)}, u32[]{:S(2)}, u32[]{:S(2)}) collective-permute-start(f32[2,40,128]{2,1,0:T(8,128)S(1)} %pad_maximum_fusion.3), channel_id=1, source_target_pairs={{0,4},{1,5},{2,6},{3,7},{4,0},{5,1},{6,2},{7,3},{8,12},{9,13},{10,... | collective-permute-start | bytes 122888 | tf_op jit(solution)/shard_map/ppermute | solution.py:556
  49.5 1.3 %collective-permute-start.15 = (f32[16,1024]{1,0:T(8,128)S(1)}, f32[16,1024]{1,0:T(8,128)S(1)}, u32[]{:S(2)}, u32[]{:S(2)}) collective-permute-start(f32[16,1024]{1,0:T(8,128)S(1)} %shard_map.113), channel_id=1, source_target_pairs={{0,1},{1,0},{2,3},{3,2},{4,5},{5,4},{6,7},{7,6},{8,9},{9,8},{10,11... | collective-permute-start | bytes 196616 | tf_op jit(solution)/shard_map/ppermute | solution.py:556

commit v7 on v6

--- a/solution.py
+++ b/solution.py
@@ -139,40 +139,45 @@
     )(in_hbm(blocks), counts, in_hbm(coef), in_hbm(x))
 
 
-def level_kernel(index, levels, rows, own_index, own_levels, sems):
-    pairs = (index, own_index), (levels, own_levels)
+def level_kernel(index, levels, owner, rows, slots, own_index, own_levels, held, sems):
+    pairs = (index, own_index), (levels, own_levels), (owner, held)
     copies = [pltpu.make_async_copy(src, dst, sems.at[k]) for k, (src, dst) in enumerate(pairs)]
     for copy in copies:
         copy.start()
     for copy in copies:
         copy.wait()
+    me = lax.axis_index("aux")
     lane = iota((1, LANES), 1)
 
-    def step(i, carry):
+    def step(i, rank):
         at = own_index[i]
         row = own_levels[pl.ds(lax.div(at, LANES), 1), :]
         rows[pl.ds(i, 1), :] = jnp.where(lane == lax.rem(at, LANES), 2.0 * row, 0.0)
-        return carry
-
-    lax.fori_loop(0, rows.shape[0], step, 0)
+        mine = held[i] == me
+        slots[pl.ds(i, 1), :] = jnp.broadcast_to(jnp.where(mine, rank, -1), (1, LANES))
+        return rank + jnp.where(mine, 1, 0)
+
+    lax.fori_loop(0, rows.shape[0], step, jnp.int32(0))
     rows[...] = jnp.broadcast_to(jnp.sum(rows[...], axis=1, keepdims=True), rows.shape)
 
 
-def level_rows(index, levels):
+def level_rows(index, levels, owner):
     far = pl.BlockSpec(memory_space=pltpu.HBM)
+    shape = (index.shape[0], LANES)
     return pl.pallas_call(
         level_kernel,
-        in_specs=[far, far],
-        out_specs=VMEM,
-        out_shape=jax.ShapeDtypeStruct((index.shape[0], LANES), F32),
+        in_specs=[far] * 3,
+        out_specs=[VMEM] * 2,
+        out_shape=[jax.ShapeDtypeStruct(shape, F32), jax.ShapeDtypeStruct(shape, jnp.int32)],
         scratch_shapes=[
             pltpu.SMEM(index.shape, index.dtype),
             pltpu.VMEM(levels.shape, levels.dtype),
-            pltpu.SemaphoreType.DMA((2,)),
+            pltpu.SMEM(owner.shape, owner.dtype),
+            pltpu.SemaphoreType.DMA((3,)),
         ],
         compiler_params=pltpu.CompilerParams(vmem_limit_bytes=2**20),
         cost_estimate=pl.CostEstimate(flops=0, bytes_accessed=2**20, transcendentals=0),
-    )(in_hbm(index), in_hbm(levels))
+    )(in_hbm(index), in_hbm(levels), in_hbm(owner))
 
 
 def stages(size, order):
@@ -520,35 +525,20 @@
     )(*args)
 
 
-def pair_kernel(owner, energy, out, held, sem):
-    copy = pltpu.make_async_copy(owner, held, sem)
-    copy.start()
-    copy.wait()
-    me = lax.axis_index("aux")
-
-    def step(i, carry):
-        rank, rows = carry
-        mine = held[i] == me
-        row = energy[pl.ds(i, 1), :]
-        rows = [jnp.where(mine & (rank == k), row, rows[k]) for k in range(CAP)]
-        return rank + jnp.where(mine, 1, 0), rows
-
-    blank = jnp.zeros((1, LANES), F32)
-    _, rows = lax.fori_loop(0, energy.shape[0], step, (jnp.int32(0), [blank] * CAP))
+def pair_kernel(slots, energy, out):
     for k in range(CAP):
-        out[k] = jnp.sum(rows[k])
-
-
-def pair_slots(owner_map, energy):
+        out[k] = jnp.sum(jnp.where(slots[...] == k, energy[...], 0.0))
+
+
+def pair_slots(slots, energy):
     return pl.pallas_call(
         pair_kernel,
-        in_specs=[pl.BlockSpec(memory_space=pltpu.HBM), VMEM],
+        in_specs=[VMEM] * 2,
         out_specs=SMEM,
         out_shape=jax.ShapeDtypeStruct((CAP,), F32),
-        scratch_shapes=[pltpu.SMEM(owner_map.shape, owner_map.dtype), pltpu.SemaphoreType.DMA],
         compiler_params=pltpu.CompilerParams(vmem_limit_bytes=2**20),
         cost_estimate=pl.CostEstimate(flops=0, bytes_accessed=2**20, transcendentals=0),
-    )(in_hbm(owner_map), energy)
+    )(slots, energy)
 
 
 def swap(x, mask):
@@ -583,9 +573,9 @@
     for k, step in enumerate(reversed(stages(size, SUM_INTS))):
         far = [swap(keep, mask) for mask in step]
         if k == 0:
-            levels = level_rows(batch_index, occ_energy.reshape(-1, LANES))
+            levels, slots = level_rows(batch_index, occ_energy.reshape(-1, LANES), owner_map)
         keep = sum(far, keep)
-        keep, levels = lax.optimization_barrier((keep, levels))
+        keep, levels, slots = lax.optimization_barrier((keep, levels, slots))
     other = swap(keep, 1)
     vir = vir_energy.reshape(1, -1)
     own_energy, own = core_weights(False, keep, levels, vir, half)
@@ -604,12 +594,13 @@
         piece = buf[done:]
         theirs = place_terms(done, True, piece, spots, theirs, orbs, local_rows)
         ours = place_terms(done, False, piece, spots, ours, orbs, local_rows)
+        if k == 0:
+            pair_energy = pair_slots(slots, energy)
+            ours, pair_energy = lax.optimization_barrier((ours, pair_energy))
         done = buf.shape[0]
         if k + 1 < len(steps):
             buf = jnp.concatenate([buf] + far, axis=0)
             buf, ours, theirs = lax.optimization_barrier((buf, ours, theirs))
-    pair_energy = pair_slots(owner_map, energy)
-    ours, theirs, pair_energy = lax.optimization_barrier((ours, theirs, pair_energy))
     for k, piece in enumerate(far):
         theirs = place_terms(done + k * piece.shape[0], True, piece, spots, theirs, orbs, local_rows)
     last = swap(theirs, 1)

time: 51.7 us -> 51.7 us (level)
  Pallas kernels: 16.8 us -> 16.1 us
  waiting for transfers between devices: 12 us -> 12.7 us
    ppermute x16, waiting for transfers between devices: 12 us -> 12.7 us  [swap(): return lax.ppermute(x, 'aux', [(i, i ^ mask) for i in range(size)])]
    pallas_call x2, Pallas kernels: 2.37 us -> 1.71 us  [the longest x1 1.07 us: level_rows(): pl.pallas_call(level_kernel, in_specs=[far] * 3, out_specs=[VMEM] * 2, ou...]
  transfers between devices with their start and end apart: 16 -> 16, of which waited for: 11 -> 12; matrix products, arithmetic and copies ran while one was open for 0% -> 0% of each run, Pallas kernels for 21% -> 19%
where the time goes in v7:
time: 51.7 us; the launch traced here: 51.4 us
  starting transfers between devices  20.3 us (39%)
  Pallas kernels  16.1 us (31%)
  waiting for transfers between devices  12.7 us (25%)
  between operations  1.51 us (3%)
  other arithmetic  0.74 us (1%)
    ppermute x16, starting transfers between devices, swap(): return lax.ppermute(x, 'aux', [(i, i ^ mask) for i in range(size)])  20.3 us
    ppermute x16, waiting for transfers between devices, swap(): return lax.ppermute(x, 'aux', [(i, i ^ mask) for i in range(size)])  12.7 us
    pallas_call x2, Pallas kernels, retile(): pl.pallas_call(functools.partial(retile_kernel, start), in_specs=[pl.Bloc...  4.9 us
    pallas_call x1, Pallas kernels, gradient_terms(): pl.pallas_call(grad_kernel, in_specs=[VMEM] * (4 + PARTS), out_specs=[VME...  3.16 us
    pallas_call x1, Pallas kernels, half_transform(): pl.pallas_call(functools.partial(half_kernel, steps), in_specs=[VMEM] * (...  2.38 us
    pallas_call x1, Pallas kernels, prepare(): pl.pallas_call(prepare_kernel, in_specs=[far, VMEM, far, far], out_specs=...  1.55 us
    pallas_call x1, Pallas kernels, level_rows(): pl.pallas_call(level_kernel, in_specs=[far] * 3, out_specs=[VMEM] * 2, ou...  1.07 us
  transfers between devices with their start and end apart: 16, of which 12 were waited for; matrix products, arithmetic and copies ran while one was open for 0% of the time, Pallas kernels for 19%

profile of v7, /device:TPU:0, one launch (start us, length us, event | category | flops | bytes accessed | tf_op | source)
XLA Modules:
  0.0 51.4 jit_solution(2905362351395027439)
XLA Ops:
  0.6 4.1 %collective-permute-start = (bf16[1,16,1024]{2,1,0:T(8,128)(2,1)}, bf16[1,16,1024]{2,1,0:T(8,128)(2,1)S(1)}, u32[]{:S(2)}, u32[]{:S(2)}) collective-permute-start(bf16[1,16,1024]{2,1,0:T(8,128)(2,1)} %bitcast.20), channel_id=1, source_target_pairs={{0,8},{1,9},{2,10},{3,11},{4,12},{5,13},{6,14},{7,15},{8,0},{9,1},... | collective-permute-start | bytes 98312 | tf_op jit(solution)/shard_map/ppermute | solution.py:546
  5.4 1.5 %shard_map.95 = (s32[1,128]{1,0:T(1,128)S(1)}, bf16[1,16,1024]{2,1,0:T(8,128)(2,1)S(1)}, bf16[16,160,128]{2,1,0:T(8,128)(2,1)S(1)}, bf16[5,32,4096]{2,1,0:T(8,128)(2,1)S(1)}) custom-call(s32[1,5]{1,0:T(1,128)} %blocks.1, s32[1,1]{1,0:T(1,128)} %bitcast.10.counts, bf16[1,16,1024]{2,1,0:T(8,128)(2,1)} %bitcast.21, bf16[5,256,4096]{2,1,0:T(8,128)(2,1)} %bitcast.17), custom_call_target="tpu_custom_call" | custom-call | bytes 1310720 | tf_op jit(solution)/shard_map/pallas_call | solution.py:127
  7.2 1.8 %collective-permute-start.3 = (bf16[2,16,1024]{2,1,0:T(8,128)(2,1)S(1)}, bf16[2,16,1024]{2,1,0:T(8,128)(2,1)S(1)}, u32[]{:S(2)}, u32[]{:S(2)}) collective-permute-start(bf16[2,16,1024]{2,1,0:T(8,128)(2,1)S(1)} %pad_maximum_fusion.2), channel_id=1, source_target_pairs={{0,2},{1,3},{2,0},{3,1},{4,6},{5,7},{6,4},{7,5},{8,10},{9,11},{10,... | collective-permute-start | bytes 196616 | tf_op jit(solution)/shard_map/ppermute | solution.py:546
  9.0 1.3 %collective-permute-start.2 = (bf16[2,16,1024]{2,1,0:T(8,128)(2,1)S(1)}, bf16[2,16,1024]{2,1,0:T(8,128)(2,1)S(1)}, u32[]{:S(2)}, u32[]{:S(2)}) collective-permute-start(bf16[2,16,1024]{2,1,0:T(8,128)(2,1)S(1)} %pad_maximum_fusion.2), channel_id=1, source_target_pairs={{0,6},{1,7},{2,4},{3,5},{4,2},{5,3},{6,0},{7,1},{8,14},{9,15},{10,... | collective-permute-start | bytes 196616 | tf_op jit(solution)/shard_map/ppermute | solution.py:546
  10.3 0.5 collective-permute-start.1
  10.8 3.6 %shard_map.96 = (bf16[208,160,128]{2,1,0:T(8,128)(2,1)S(1)}, bf16[5,16,4096]{2,1,0:T(8,128)(2,1)S(1)}) custom-call(bf16[5,256,4096]{2,1,0:T(8,128)(2,1)} %bitcast.18, bf16[5,32,4096]{2,1,0:T(8,128)(2,1)S(1)} %get-tuple-element.43.raw), custom_call_target="tpu_custom_call" | custom-call | bytes 17039360 | tf_op jit(solution)/shard_map/pallas_call | solution.py:92
  14.7 1.3 %shard_map.97.refs_2_ = bf16[32,160,128]{2,1,0:T(8,128)(2,1)S(1)} custom-call(bf16[5,256,4096]{2,1,0:T(8,128)(2,1)} %bitcast.19, bf16[5,16,4096]{2,1,0:T(8,128)(2,1)S(1)} %get-tuple-element.48.raw), custom_call_target="tpu_custom_call" | custom-call | bytes 2621440 | tf_op jit(solution)/shard_map/pallas_call | solution.py:92
  16.2 2.4 %shard_map.98 = (bf16[16,128,128]{2,1,0:T(8,128)(2,1)S(1)}, f32[136,128]{1,0:T(8,128)S(1)}) custom-call(s32[1,128]{1,0:T(1,128)S(1)} %get-tuple-element.37.id_row, bf16[8,16,1024]{2,1,0:T(8,128)(2,1)S(1)} %pad_maximum_fusion.coef_a, bf16[8,16,1024]{2,1,0:T(8,128)(2,1)S(1)} %collective-permute-done.4.coef_b, ...), custom_call_target="tpu_custom_call" | custom-call | tf_op jit(solution)/shard_map/pallas_call | solution.py:306
  18.6 0.4 collective-permute-start.5
  18.9 0.3 shard_map.99
  19.3 0.6 %collective-permute-done.5 = f32[136,128]{1,0:T(8,128)S(1)} collective-permute-done((f32[136,128]{1,0:T(8,128)S(1)}, f32[136,128]{1,0:T(8,128)S(1)}, u32[]{:S(2)}, u32[]{:S(2)}) %collective-permute-start.5) | collective-permute-done | bytes 69664 | tf_op jit(solution)/shard_map/ppermute | solution.py:546
  19.9 1.4 %collective-permute-start.8 = (f32[136,128]{1,0:T(8,128)S(1)}, f32[136,128]{1,0:T(8,128)S(1)}, u32[]{:S(2)}, u32[]{:S(2)}) collective-permute-start(f32[136,128]{1,0:T(8,128)S(1)} %add.18), channel_id=1, source_target_pairs={{0,4},{1,5},{2,6},{3,7},{4,0},{5,1},{6,2},{7,3},{8,12},{9,13},{10,... | collective-permute-start | bytes 208904 | tf_op jit(solution)/shard_map/ppermute | solution.py:546
  21.3 1.5 %collective-permute-start.7 = (f32[136,128]{1,0:T(8,128)S(1)}, f32[136,128]{1,0:T(8,128)S(1)}, u32[]{:S(2)}, u32[]{:S(2)}) collective-permute-start(f32[136,128]{1,0:T(8,128)S(1)} %add.18), channel_id=1, source_target_pairs={{0,2},{1,3},{2,0},{3,1},{4,6},{5,7},{6,4},{7,5},{8,10},{9,11},{10,... | collective-permute-start | bytes 208904 | tf_op jit(solution)/shard_map/ppermute | solution.py:546
  22.8 0.6 %collective-permute-start.6 = (f32[136,128]{1,0:T(8,128)S(1)}, f32[136,128]{1,0:T(8,128)S(1)}, u32[]{:S(2)}, u32[]{:S(2)}) collective-permute-start(f32[136,128]{1,0:T(8,128)S(1)} %add.18), channel_id=1, source_target_pairs={{0,6},{1,7},{2,4},{3,5},{4,2},{5,3},{6,0},{7,1},{8,14},{9,15},{10,... | collective-permute-start | bytes 208904 | tf_op jit(solution)/shard_map/ppermute | solution.py:546
  23.5 1.1 %shard_map.100 = (f32[16,128]{1,0:T(8,128)S(1)}, s32[16,128]{1,0:T(8,128)S(1)}) custom-call(s32[16]{0:T(128)} %index.1, f32[8,128]{1,0:T(8,128)} %bitcast.22, s32[16]{0:T(128)} %owner.1), custom_call_target="tpu_custom_call" | custom-call | bytes 1048576 | tf_op jit(solution)/shard_map/pallas_call | solution.py:167
  24.6 1.1 %collective-permute-done.7 = f32[136,128]{1,0:T(8,128)S(1)} collective-permute-done((f32[136,128]{1,0:T(8,128)S(1)}, f32[136,128]{1,0:T(8,128)S(1)}, u32[]{:S(2)}, u32[]{:S(2)}) %collective-permute-start.7) | collective-permute-done | bytes 69664 | tf_op jit(solution)/shard_map/ppermute | solution.py:546
  25.7 2.4 %collective-permute-done.6 = f32[136,128]{1,0:T(8,128)S(1)} collective-permute-done((f32[136,128]{1,0:T(8,128)S(1)}, f32[136,128]{1,0:T(8,128)S(1)}, u32[]{:S(2)}, u32[]{:S(2)}) %collective-permute-start.6) | collective-permute-done | bytes 69664 | tf_op jit(solution)/shard_map/ppermute | solution.py:546
  28.1 2.9 %collective-permute-start.9 = (f32[136,128]{1,0:T(8,128)S(1)}, f32[136,128]{1,0:T(8,128)S(1)}, u32[]{:S(2)}, u32[]{:S(2)}) collective-permute-start(f32[136,128]{1,0:T(8,128)S(1)} %add_add_fusion), channel_id=1, source_target_pairs={{0,8},{1,9},{2,10},{3,11},{4,12},{5,13},{6,14},{7,15},{8,0},{9,1},... | collective-permute-start | bytes 208904 | tf_op jit(solution)/shard_map/ppermute | solution.py:546
  31.0 3.1 %collective-permute-done.9 = f32[136,128]{1,0:T(8,128)S(1)} collective-permute-done((f32[136,128]{1,0:T(8,128)S(1)}, f32[136,128]{1,0:T(8,128)S(1)}, u32[]{:S(2)}, u32[]{:S(2)}) %collective-permute-start.9) | collective-permute-done | bytes 69664 | tf_op jit(solution)/shard_map/ppermute | solution.py:546
  34.4 0.5 shard_map.101
  34.9 0.5 %collective-permute-done.10.packed = f32[136,128]{1,0:T(8,128)S(1)} collective-permute-done((f32[136,128]{1,0:T(8,128)S(1)}, f32[136,128]{1,0:T(8,128)S(1)}, u32[]{:S(2)}, u32[]{:S(2)}) %collective-permute-start.10) | collective-permute-done | bytes 69664 | tf_op jit(solution)/shard_map/ppermute | solution.py:546
  35.4 0.5 shard_map.103
  35.9 3.2 %shard_map.104 = (f32[40,128]{1,0:T(8,128)S(1)}, f32[16,128]{1,0:T(8,128)S(1)}) custom-call(f32[8,128]{1,0:T(8,128)S(1)} %get-tuple-element.58.own_energy, f32[1024,128]{1,0:T(8,128)S(1)} %get-tuple-element.59.own, f32[8,128]{1,0:T(8,128)S(1)} %get-tuple-element.61.other_energy, f32[1024,128]{1,0:T(8,128)S(1)} %get-tuple-element.62.other, ...), custom_call_target="tpu_custom_call" | custom-call | tf_op jit(solution)/shard_map/pallas_call | solution.py:432
  39.1 2.1 %collective-permute-start.11 = (f32[1,40,128]{2,1,0:T(8,128)S(1)}, f32[1,40,128]{2,1,0:T(8,128)S(1)}, u32[]{:S(2)}, u32[]{:S(2)}) collective-permute-start(f32[1,40,128]{2,1,0:T(8,128)S(1)} %bitcast.11), channel_id=1, source_target_pairs={{0,8},{1,9},{2,10},{3,11},{4,12},{5,13},{6,14},{7,15},{8,0},{9,1},... | collective-permute-start | bytes 61448 | tf_op jit(solution)/shard_map/ppermute | solution.py:546
  41.4 0.6 %shard_map.106 = f32[2]{0:T(128)} custom-call(s32[16,128]{1,0:T(8,128)S(1)} %get-tuple-element.65.slots, f32[16,128]{1,0:T(8,128)S(1)} %get-tuple-element.66.energy), custom_call_target="tpu_custom_call" | custom-call | bytes 1048576 | tf_op jit(solution)/shard_map/pallas_call | solution.py:534
  42.0 1.7 %collective-permute-done.11 = f32[1,40,128]{2,1,0:T(8,128)S(1)} collective-permute-done((f32[1,40,128]{2,1,0:T(8,128)S(1)}, f32[1,40,128]{2,1,0:T(8,128)S(1)}, u32[]{:S(2)}, u32[]{:S(2)}) %collective-permute-start.11) | collective-permute-done | bytes 20512 | tf_op jit(solution)/shard_map/ppermute | solution.py:546
  43.9 1.4 %collective-permute-start.13 = (f32[2,40,128]{2,1,0:T(8,128)S(1)}, f32[2,40,128]{2,1,0:T(8,128)S(1)}, u32[]{:S(2)}, u32[]{:S(2)}) collective-permute-start(f32[2,40,128]{2,1,0:T(8,128)S(1)} %pad_maximum_fusion.3), channel_id=1, source_target_pairs={{0,2},{1,3},{2,0},{3,1},{4,6},{5,7},{6,4},{7,5},{8,10},{9,11},{10,... | collective-permute-start | bytes 122888 | tf_op jit(solution)/shard_map/ppermute | solution.py:546
  45.3 1.9 %collective-permute-start.14 = (f32[2,40,128]{2,1,0:T(8,128)S(1)}, f32[2,40,128]{2,1,0:T(8,128)S(1)}, u32[]{:S(2)}, u32[]{:S(2)}) collective-permute-start(f32[2,40,128]{2,1,0:T(8,128)S(1)} %pad_maximum_fusion.3), channel_id=1, source_target_pairs={{0,4},{1,5},{2,6},{3,7},{4,0},{5,1},{6,2},{7,3},{8,12},{9,13},{10,... | collective-permute-start | bytes 122888 | tf_op jit(solution)/shard_map/ppermute | solution.py:546
  47.5 1.2 %collective-permute-done.12.piece = f32[2,40,128]{2,1,0:T(8,128)S(1)} collective-permute-done((f32[2,40,128]{2,1,0:T(8,128)S(1)}, f32[2,40,128]{2,1,0:T(8,128)S(1)}, u32[]{:S(2)}, u32[]{:S(2)}) %collective-permute-start.12) | collective-permute-done | bytes 40992 | tf_op jit(solution)/shard_map/ppermute | solution.py:546
  48.9 0.4 collective-permute-done.14.piece
  49.8 1.0 %collective-permute-done.15 = f32[16,1024]{1,0:T(8,128)S(1)} collective-permute-done((f32[16,1024]{1,0:T(8,128)S(1)}, f32[16,1024]{1,0:T(8,128)S(1)}, u32[]{:S(2)}, u32[]{:S(2)}) %collective-permute-start.15) | collective-permute-done | bytes 65568 | tf_op jit(solution)/shard_map/ppermute | solution.py:546
  50.8 0.6 %add_bitcast_fusion = f32[1024,16]{0,1:T(8,128)} fusion(f32[16,1024]{1,0:T(8,128)S(1)} %shard_map.109, f32[16,1024]{1,0:T(8,128)S(1)} %collective-permute-done.15), kind=kLoop, calls=%fused_computation.4 | loop fusion | flops 16384 | bytes 196608 | tf_op jit(solution)/shard_map/transpose | solution.py:608
  (30 shorter events, 2.2 us)
Async XLA Ops:
  0.6 6.6 %collective-permute-start = (bf16[1,16,1024]{2,1,0:T(8,128)(2,1)}, bf16[1,16,1024]{2,1,0:T(8,128)(2,1)S(1)}, u32[]{:S(2)}, u32[]{:S(2)}) collective-permute-start(bf16[1,16,1024]{2,1,0:T(8,128)(2,1)} %bitcast.20), channel_id=1, source_target_pairs={{0,8},{1,9},{2,10},{3,11},{4,12},{5,13},{6,14},{7,15},{8,0},{9,1},... | collective-permute-start | bytes 98312 | tf_op jit(solution)/shard_map/ppermute | solution.py:546
  7.2 7.1 %collective-permute-start.3 = (bf16[2,16,1024]{2,1,0:T(8,128)(2,1)S(1)}, bf16[2,16,1024]{2,1,0:T(8,128)(2,1)S(1)}, u32[]{:S(2)}, u32[]{:S(2)}) collective-permute-start(bf16[2,16,1024]{2,1,0:T(8,128)(2,1)S(1)} %pad_maximum_fusion.2), channel_id=1, source_target_pairs={{0,2},{1,3},{2,0},{3,1},{4,6},{5,7},{6,4},{7,5},{8,10},{9,11},{10,... | collective-permute-start | bytes 196616 | tf_op jit(solution)/shard_map/ppermute | solution.py:546
  9.0 5.4 %collective-permute-start.2 = (bf16[2,16,1024]{2,1,0:T(8,128)(2,1)S(1)}, bf16[2,16,1024]{2,1,0:T(8,128)(2,1)S(1)}, u32[]{:S(2)}, u32[]{:S(2)}) collective-permute-start(bf16[2,16,1024]{2,1,0:T(8,128)(2,1)S(1)} %pad_maximum_fusion.2), channel_id=1, source_target_pairs={{0,6},{1,7},{2,4},{3,5},{4,2},{5,3},{6,0},{7,1},{8,14},{9,15},{10,... | collective-permute-start | bytes 196616 | tf_op jit(solution)/shard_map/ppermute | solution.py:546
  10.3 4.3 %collective-permute-start.1 = (bf16[2,16,1024]{2,1,0:T(8,128)(2,1)S(1)}, bf16[2,16,1024]{2,1,0:T(8,128)(2,1)S(1)}, u32[]{:S(2)}, u32[]{:S(2)}) collective-permute-start(bf16[2,16,1024]{2,1,0:T(8,128)(2,1)S(1)} %pad_maximum_fusion.2), channel_id=1, source_target_pairs={{0,4},{1,5},{2,6},{3,7},{4,0},{5,1},{6,2},{7,3},{8,12},{9,13},{10,... | collective-permute-start | bytes 196616 | tf_op jit(solution)/shard_map/ppermute | solution.py:546
  14.6 1.6 %collective-permute-start.4 = (bf16[8,16,1024]{2,1,0:T(8,128)(2,1)S(1)}, bf16[8,16,1024]{2,1,0:T(8,128)(2,1)S(1)}, u32[]{:S(2)}, u32[]{:S(2)}) collective-permute-start(bf16[8,16,1024]{2,1,0:T(8,128)(2,1)S(1)} %pad_maximum_fusion.coef_a), channel_id=1, source_target_pairs={{0,1},{1,0},{2,3},{3,2},{4,5},{5,4},{6,7},{7,6},{8,9},{9,8},{10,11... | collective-permute-start | bytes 786440 | tf_op jit(solution)/shard_map/ppermute | solution.py:546
  16.0 18.4 %copy-start = (f32[64]{0:T(128)S(1)}, f32[64]{0:T(128)}, u32[]{:S(2)}) copy-start(f32[64]{0:T(128)} %param.14) | copy-start | bytes 772
  18.6 1.3 %collective-permute-start.5 = (f32[136,128]{1,0:T(8,128)S(1)}, f32[136,128]{1,0:T(8,128)S(1)}, u32[]{:S(2)}, u32[]{:S(2)}) collective-permute-start(f32[136,128]{1,0:T(8,128)S(1)} %get-tuple-element.50), channel_id=1, source_target_pairs={{0,1},{1,0},{2,3},{3,2},{4,5},{5,4},{6,7},{7,6},{8,9},{9,8},{10,11... | collective-permute-start | bytes 208904 | tf_op jit(solution)/shard_map/ppermute | solution.py:546
  19.9 4.6 %collective-permute-start.8 = (f32[136,128]{1,0:T(8,128)S(1)}, f32[136,128]{1,0:T(8,128)S(1)}, u32[]{:S(2)}, u32[]{:S(2)}) collective-permute-start(f32[136,128]{1,0:T(8,128)S(1)} %add.18), channel_id=1, source_target_pairs={{0,4},{1,5},{2,6},{3,7},{4,0},{5,1},{6,2},{7,3},{8,12},{9,13},{10,... | collective-permute-start | bytes 208904 | tf_op jit(solution)/shard_map/ppermute | solution.py:546
  21.3 4.3 %collective-permute-start.7 = (f32[136,128]{1,0:T(8,128)S(1)}, f32[136,128]{1,0:T(8,128)S(1)}, u32[]{:S(2)}, u32[]{:S(2)}) collective-permute-start(f32[136,128]{1,0:T(8,128)S(1)} %add.18), channel_id=1, source_target_pairs={{0,2},{1,3},{2,0},{3,1},{4,6},{5,7},{6,4},{7,5},{8,10},{9,11},{10,... | collective-permute-start | bytes 208904 | tf_op jit(solution)/shard_map/ppermute | solution.py:546
  22.8 5.2 %collective-permute-start.6 = (f32[136,128]{1,0:T(8,128)S(1)}, f32[136,128]{1,0:T(8,128)S(1)}, u32[]{:S(2)}, u32[]{:S(2)}) collective-permute-start(f32[136,128]{1,0:T(8,128)S(1)} %add.18), channel_id=1, source_target_pairs={{0,6},{1,7},{2,4},{3,5},{4,2},{5,3},{6,0},{7,1},{8,14},{9,15},{10,... | collective-permute-start | bytes 208904 | tf_op jit(solution)/shard_map/ppermute | solution.py:546
  28.1 6.0 %collective-permute-start.9 = (f32[136,128]{1,0:T(8,128)S(1)}, f32[136,128]{1,0:T(8,128)S(1)}, u32[]{:S(2)}, u32[]{:S(2)}) collective-permute-start(f32[136,128]{1,0:T(8,128)S(1)} %add_add_fusion), channel_id=1, source_target_pairs={{0,8},{1,9},{2,10},{3,11},{4,12},{5,13},{6,14},{7,15},{8,0},{9,1},... | collective-permute-start | bytes 208904 | tf_op jit(solution)/shard_map/ppermute | solution.py:546
  34.1 1.3 %collective-permute-start.10 = (f32[136,128]{1,0:T(8,128)S(1)}, f32[136,128]{1,0:T(8,128)S(1)}, u32[]{:S(2)}, u32[]{:S(2)}) collective-permute-start(f32[136,128]{1,0:T(8,128)S(1)} %add.22.packed), channel_id=1, source_target_pairs={{0,1},{1,0},{2,3},{3,2},{4,5},{5,4},{6,7},{7,6},{8,9},{9,8},{10,11... | collective-permute-start | bytes 208904 | tf_op jit(solution)/shard_map/ppermute | solution.py:546
  39.1 4.7 %collective-permute-start.11 = (f32[1,40,128]{2,1,0:T(8,128)S(1)}, f32[1,40,128]{2,1,0:T(8,128)S(1)}, u32[]{:S(2)}, u32[]{:S(2)}) collective-permute-start(f32[1,40,128]{2,1,0:T(8,128)S(1)} %bitcast.11), channel_id=1, source_target_pairs={{0,8},{1,9},{2,10},{3,11},{4,12},{5,13},{6,14},{7,15},{8,0},{9,1},... | collective-permute-start | bytes 61448 | tf_op jit(solution)/shard_map/ppermute | solution.py:546
  43.8 4.9 %collective-permute-start.12 = (f32[2,40,128]{2,1,0:T(8,128)S(1)}, f32[2,40,128]{2,1,0:T(8,128)S(1)}, u32[]{:S(2)}, u32[]{:S(2)}) collective-permute-start(f32[2,40,128]{2,1,0:T(8,128)S(1)} %pad_maximum_fusion.3), channel_id=1, source_target_pairs={{0,6},{1,7},{2,4},{3,5},{4,2},{5,3},{6,0},{7,1},{8,14},{9,15},{10,... | collective-permute-start | bytes 122888 | tf_op jit(solution)/shard_map/ppermute | solution.py:546
  43.9 4.9 %collective-permute-start.13 = (f32[2,40,128]{2,1,0:T(8,128)S(1)}, f32[2,40,128]{2,1,0:T(8,128)S(1)}, u32[]{:S(2)}, u32[]{:S(2)}) collective-permute-start(f32[2,40,128]{2,1,0:T(8,128)S(1)} %pad_maximum_fusion.3), channel_id=1, source_target_pairs={{0,2},{1,3},{2,0},{3,1},{4,6},{5,7},{6,4},{7,5},{8,10},{9,11},{10,... | collective-permute-start | bytes 122888 | tf_op jit(solution)/shard_map/ppermute | solution.py:546
  45.3 4.0 %collective-permute-start.14 = (f32[2,40,128]{2,1,0:T(8,128)S(1)}, f32[2,40,128]{2,1,0:T(8,128)S(1)}, u32[]{:S(2)}, u32[]{:S(2)}) collective-permute-start(f32[2,40,128]{2,1,0:T(8,128)S(1)} %pad_maximum_fusion.3), channel_id=1, source_target_pairs={{0,4},{1,5},{2,6},{3,7},{4,0},{5,1},{6,2},{7,3},{8,12},{9,13},{10,... | collective-permute-start | bytes 122888 | tf_op jit(solution)/shard_map/ppermute | solution.py:546
  49.5 1.3 %collective-permute-start.15 = (f32[16,1024]{1,0:T(8,128)S(1)}, f32[16,1024]{1,0:T(8,128)S(1)}, u32[]{:S(2)}, u32[]{:S(2)}) collective-permute-start(f32[16,1024]{1,0:T(8,128)S(1)} %shard_map.113), channel_id=1, source_target_pairs={{0,1},{1,0},{2,3},{3,2},{4,5},{5,4},{6,7},{7,6},{8,9},{9,8},{10,11... | collective-permute-start | bytes 196616 | tf_op jit(solution)/shard_map/ppermute | solution.py:546

commit v8 on v7

--- a/solution.py
+++ b/solution.py
@@ -16,7 +16,7 @@
 ROWS = S * TILES
 PARTS = 3
 GATHER_COEF = (1, 2, 0)
-SUM_INTS = (2, 0, 1)
+SUM_INTS = (1, 0, 2)
 GATHER_TERMS = (2, 0, 1)
 SEAT = 8
 SEATS = LANES // SEAT

time: 51.7 us -> 51.8 us (level)
  waiting for transfers between devices: 12.7 us -> 13.3 us
    ppermute x16, waiting for transfers between devices: 12.7 us -> 13.3 us  [swap(): return lax.ppermute(x, 'aux', [(i, i ^ mask) for i in range(size)])]
  transfers between devices with their start and end apart: 16 -> 16, of which waited for: 12 -> 14; matrix products, arithmetic and copies ran while one was open for 0% -> 0% of each run, Pallas kernels for 19% -> 19%
where the time goes in v8:
time: 51.8 us; the launch traced here: 51.6 us
  starting transfers between devices  20 us (39%)
  Pallas kernels  16.1 us (31%)
  waiting for transfers between devices  13.3 us (26%)
  between operations  1.5 us (3%)
  other arithmetic  0.74 us (1%)
    ppermute x16, starting transfers between devices, swap(): return lax.ppermute(x, 'aux', [(i, i ^ mask) for i in range(size)])  20 us
    ppermute x16, waiting for transfers between devices, swap(): return lax.ppermute(x, 'aux', [(i, i ^ mask) for i in range(size)])  13.3 us
    pallas_call x2, Pallas kernels, retile(): pl.pallas_call(functools.partial(retile_kernel, start), in_specs=[pl.Bloc...  4.9 us
    pallas_call x1, Pallas kernels, gradient_terms(): pl.pallas_call(grad_kernel, in_specs=[VMEM] * (4 + PARTS), out_specs=[VME...  3.17 us
    pallas_call x1, Pallas kernels, half_transform(): pl.pallas_call(functools.partial(half_kernel, steps), in_specs=[VMEM] * (...  2.38 us
    pallas_call x1, Pallas kernels, prepare(): pl.pallas_call(prepare_kernel, in_specs=[far, VMEM, far, far], out_specs=...  1.55 us
    pallas_call x1, Pallas kernels, level_rows(): pl.pallas_call(level_kernel, in_specs=[far] * 3, out_specs=[VMEM] * 2, ou...  1.07 us
  transfers between devices with their start and end apart: 16, of which 14 were waited for; matrix products, arithmetic and copies ran while one was open for 0% of the time, Pallas kernels for 19%

profile of v8, /device:TPU:0, one launch (start us, length us, event | category | flops | bytes accessed | tf_op | source)
XLA Modules:
  0.0 51.6 jit_solution(16161173240544695649)
XLA Ops:
  0.6 4.1 %collective-permute-start = (bf16[1,16,1024]{2,1,0:T(8,128)(2,1)}, bf16[1,16,1024]{2,1,0:T(8,128)(2,1)S(1)}, u32[]{:S(2)}, u32[]{:S(2)}) collective-permute-start(bf16[1,16,1024]{2,1,0:T(8,128)(2,1)} %bitcast.20), channel_id=1, source_target_pairs={{0,8},{1,9},{2,10},{3,11},{4,12},{5,13},{6,14},{7,15},{8,0},{9,1},... | collective-permute-start | bytes 98312 | tf_op jit(solution)/shard_map/ppermute | solution.py:546
  5.4 1.5 %shard_map.95 = (s32[1,128]{1,0:T(1,128)S(1)}, bf16[1,16,1024]{2,1,0:T(8,128)(2,1)S(1)}, bf16[16,160,128]{2,1,0:T(8,128)(2,1)S(1)}, bf16[5,32,4096]{2,1,0:T(8,128)(2,1)S(1)}) custom-call(s32[1,5]{1,0:T(1,128)} %blocks.1, s32[1,1]{1,0:T(1,128)} %bitcast.10.counts, bf16[1,16,1024]{2,1,0:T(8,128)(2,1)} %bitcast.21, bf16[5,256,4096]{2,1,0:T(8,128)(2,1)} %bitcast.17), custom_call_target="tpu_custom_call" | custom-call | bytes 1310720 | tf_op jit(solution)/shard_map/pallas_call | solution.py:127
  7.2 1.8 %collective-permute-start.3 = (bf16[2,16,1024]{2,1,0:T(8,128)(2,1)S(1)}, bf16[2,16,1024]{2,1,0:T(8,128)(2,1)S(1)}, u32[]{:S(2)}, u32[]{:S(2)}) collective-permute-start(bf16[2,16,1024]{2,1,0:T(8,128)(2,1)S(1)} %pad_maximum_fusion.2), channel_id=1, source_target_pairs={{0,2},{1,3},{2,0},{3,1},{4,6},{5,7},{6,4},{7,5},{8,10},{9,11},{10,... | collective-permute-start | bytes 196616 | tf_op jit(solution)/shard_map/ppermute | solution.py:546
  9.0 1.3 %collective-permute-start.2 = (bf16[2,16,1024]{2,1,0:T(8,128)(2,1)S(1)}, bf16[2,16,1024]{2,1,0:T(8,128)(2,1)S(1)}, u32[]{:S(2)}, u32[]{:S(2)}) collective-permute-start(bf16[2,16,1024]{2,1,0:T(8,128)(2,1)S(1)} %pad_maximum_fusion.2), channel_id=1, source_target_pairs={{0,6},{1,7},{2,4},{3,5},{4,2},{5,3},{6,0},{7,1},{8,14},{9,15},{10,... | collective-permute-start | bytes 196616 | tf_op jit(solution)/shard_map/ppermute | solution.py:546
  10.3 0.5 collective-permute-start.1
  10.8 3.6 %shard_map.96 = (bf16[208,160,128]{2,1,0:T(8,128)(2,1)S(1)}, bf16[5,16,4096]{2,1,0:T(8,128)(2,1)S(1)}) custom-call(bf16[5,256,4096]{2,1,0:T(8,128)(2,1)} %bitcast.18, bf16[5,32,4096]{2,1,0:T(8,128)(2,1)S(1)} %get-tuple-element.43.raw), custom_call_target="tpu_custom_call" | custom-call | bytes 17039360 | tf_op jit(solution)/shard_map/pallas_call | solution.py:92
  14.7 1.3 %shard_map.97.refs_2_ = bf16[32,160,128]{2,1,0:T(8,128)(2,1)S(1)} custom-call(bf16[5,256,4096]{2,1,0:T(8,128)(2,1)} %bitcast.19, bf16[5,16,4096]{2,1,0:T(8,128)(2,1)S(1)} %get-tuple-element.48.raw), custom_call_target="tpu_custom_call" | custom-call | bytes 2621440 | tf_op jit(solution)/shard_map/pallas_call | solution.py:92
  16.2 2.4 %shard_map.98 = (bf16[16,128,128]{2,1,0:T(8,128)(2,1)S(1)}, f32[136,128]{1,0:T(8,128)S(1)}) custom-call(s32[1,128]{1,0:T(1,128)S(1)} %get-tuple-element.37.id_row, bf16[8,16,1024]{2,1,0:T(8,128)(2,1)S(1)} %pad_maximum_fusion.coef_a, bf16[8,16,1024]{2,1,0:T(8,128)(2,1)S(1)} %collective-permute-done.4.coef_b, ...), custom_call_target="tpu_custom_call" | custom-call | tf_op jit(solution)/shard_map/pallas_call | solution.py:306
  19.3 0.6 %collective-permute-done.5 = f32[136,128]{1,0:T(8,128)S(1)} collective-permute-done((f32[136,128]{1,0:T(8,128)S(1)}, f32[136,128]{1,0:T(8,128)S(1)}, u32[]{:S(2)}, u32[]{:S(2)}) %collective-permute-start.5) | collective-permute-done | bytes 69664 | tf_op jit(solution)/shard_map/ppermute | solution.py:546
  19.9 2.4 %collective-permute-start.8 = (f32[136,128]{1,0:T(8,128)S(1)}, f32[136,128]{1,0:T(8,128)S(1)}, u32[]{:S(2)}, u32[]{:S(2)}) collective-permute-start(f32[136,128]{1,0:T(8,128)S(1)} %add.18), channel_id=1, source_target_pairs={{0,6},{1,7},{2,4},{3,5},{4,2},{5,3},{6,0},{7,1},{8,14},{9,15},{10,... | collective-permute-start | bytes 208904 | tf_op jit(solution)/shard_map/ppermute | solution.py:546
  22.3 0.5 %collective-permute-start.7 = (f32[136,128]{1,0:T(8,128)S(1)}, f32[136,128]{1,0:T(8,128)S(1)}, u32[]{:S(2)}, u32[]{:S(2)}) collective-permute-start(f32[136,128]{1,0:T(8,128)S(1)} %add.18), channel_id=1, source_target_pairs={{0,2},{1,3},{2,0},{3,1},{4,6},{5,7},{6,4},{7,5},{8,10},{9,11},{10,... | collective-permute-start | bytes 208904 | tf_op jit(solution)/shard_map/ppermute | solution.py:546
  22.8 0.7 %collective-permute-start.6 = (f32[136,128]{1,0:T(8,128)S(1)}, f32[136,128]{1,0:T(8,128)S(1)}, u32[]{:S(2)}, u32[]{:S(2)}) collective-permute-start(f32[136,128]{1,0:T(8,128)S(1)} %add.18), channel_id=1, source_target_pairs={{0,4},{1,5},{2,6},{3,7},{4,0},{5,1},{6,2},{7,3},{8,12},{9,13},{10,... | collective-permute-start | bytes 208904 | tf_op jit(solution)/shard_map/ppermute | solution.py:546
  23.5 1.1 %shard_map.100 = (f32[16,128]{1,0:T(8,128)S(1)}, s32[16,128]{1,0:T(8,128)S(1)}) custom-call(s32[16]{0:T(128)} %index.1, f32[8,128]{1,0:T(8,128)} %bitcast.22, s32[16]{0:T(128)} %owner.1), custom_call_target="tpu_custom_call" | custom-call | bytes 1048576 | tf_op jit(solution)/shard_map/pallas_call | solution.py:167
  24.5 0.7 %collective-permute-done.8 = f32[136,128]{1,0:T(8,128)S(1)} collective-permute-done((f32[136,128]{1,0:T(8,128)S(1)}, f32[136,128]{1,0:T(8,128)S(1)}, u32[]{:S(2)}, u32[]{:S(2)}) %collective-permute-start.8) | collective-permute-done | bytes 69664 | tf_op jit(solution)/shard_map/ppermute | solution.py:546
  25.3 1.5 %collective-permute-done.7 = f32[136,128]{1,0:T(8,128)S(1)} collective-permute-done((f32[136,128]{1,0:T(8,128)S(1)}, f32[136,128]{1,0:T(8,128)S(1)}, u32[]{:S(2)}, u32[]{:S(2)}) %collective-permute-start.7) | collective-permute-done | bytes 69664 | tf_op jit(solution)/shard_map/ppermute | solution.py:546
  26.7 0.4 collective-permute-done.6
  27.1 2.9 %collective-permute-start.9 = (f32[136,128]{1,0:T(8,128)S(1)}, f32[136,128]{1,0:T(8,128)S(1)}, u32[]{:S(2)}, u32[]{:S(2)}) collective-permute-start(f32[136,128]{1,0:T(8,128)S(1)} %add_add_fusion), channel_id=1, source_target_pairs={{0,8},{1,9},{2,10},{3,11},{4,12},{5,13},{6,14},{7,15},{8,0},{9,1},... | collective-permute-start | bytes 208904 | tf_op jit(solution)/shard_map/ppermute | solution.py:546
  30.1 3.6 %collective-permute-done.9 = f32[136,128]{1,0:T(8,128)S(1)} collective-permute-done((f32[136,128]{1,0:T(8,128)S(1)}, f32[136,128]{1,0:T(8,128)S(1)}, u32[]{:S(2)}, u32[]{:S(2)}) %collective-permute-start.9) | collective-permute-done | bytes 69664 | tf_op jit(solution)/shard_map/ppermute | solution.py:546
  33.9 0.5 shard_map.101
  34.4 0.5 %collective-permute-done.10.packed = f32[136,128]{1,0:T(8,128)S(1)} collective-permute-done((f32[136,128]{1,0:T(8,128)S(1)}, f32[136,128]{1,0:T(8,128)S(1)}, u32[]{:S(2)}, u32[]{:S(2)}) %collective-permute-start.10) | collective-permute-done | bytes 69664 | tf_op jit(solution)/shard_map/ppermute | solution.py:546
  34.9 0.5 shard_map.103
  35.4 3.2 %shard_map.104 = (f32[40,128]{1,0:T(8,128)S(1)}, f32[16,128]{1,0:T(8,128)S(1)}) custom-call(f32[8,128]{1,0:T(8,128)S(1)} %get-tuple-element.58.own_energy, f32[1024,128]{1,0:T(8,128)S(1)} %get-tuple-element.59.own, f32[8,128]{1,0:T(8,128)S(1)} %get-tuple-element.61.other_energy, f32[1024,128]{1,0:T(8,128)S(1)} %get-tuple-element.62.other, ...), custom_call_target="tpu_custom_call" | custom-call | tf_op jit(solution)/shard_map/pallas_call | solution.py:432
  38.6 1.8 %collective-permute-start.11 = (f32[1,40,128]{2,1,0:T(8,128)S(1)}, f32[1,40,128]{2,1,0:T(8,128)S(1)}, u32[]{:S(2)}, u32[]{:S(2)}) collective-permute-start(f32[1,40,128]{2,1,0:T(8,128)S(1)} %bitcast.11), channel_id=1, source_target_pairs={{0,8},{1,9},{2,10},{3,11},{4,12},{5,13},{6,14},{7,15},{8,0},{9,1},... | collective-permute-start | bytes 61448 | tf_op jit(solution)/shard_map/ppermute | solution.py:546
  40.6 0.6 %shard_map.106 = f32[2]{0:T(128)} custom-call(s32[16,128]{1,0:T(8,128)S(1)} %get-tuple-element.65.slots, f32[16,128]{1,0:T(8,128)S(1)} %get-tuple-element.66.energy), custom_call_target="tpu_custom_call" | custom-call | bytes 1048576 | tf_op jit(solution)/shard_map/pallas_call | solution.py:534
  41.2 2.3 %collective-permute-done.11 = f32[1,40,128]{2,1,0:T(8,128)S(1)} collective-permute-done((f32[1,40,128]{2,1,0:T(8,128)S(1)}, f32[1,40,128]{2,1,0:T(8,128)S(1)}, u32[]{:S(2)}, u32[]{:S(2)}) %collective-permute-start.11) | collective-permute-done | bytes 20512 | tf_op jit(solution)/shard_map/ppermute | solution.py:546
  43.5 1.1 %collective-permute-start.12 = (f32[2,40,128]{2,1,0:T(8,128)S(1)}, f32[2,40,128]{2,1,0:T(8,128)S(1)}, u32[]{:S(2)}, u32[]{:S(2)}) collective-permute-start(f32[2,40,128]{2,1,0:T(8,128)S(1)} %pad_maximum_fusion.3), channel_id=1, source_target_pairs={{0,6},{1,7},{2,4},{3,5},{4,2},{5,3},{6,0},{7,1},{8,14},{9,15},{10,... | collective-permute-start | bytes 122888 | tf_op jit(solution)/shard_map/ppermute | solution.py:546
  44.6 0.9 %collective-permute-start.13 = (f32[2,40,128]{2,1,0:T(8,128)S(1)}, f32[2,40,128]{2,1,0:T(8,128)S(1)}, u32[]{:S(2)}, u32[]{:S(2)}) collective-permute-start(f32[2,40,128]{2,1,0:T(8,128)S(1)} %pad_maximum_fusion.3), channel_id=1, source_target_pairs={{0,2},{1,3},{2,0},{3,1},{4,6},{5,7},{6,4},{7,5},{8,10},{9,11},{10,... | collective-permute-start | bytes 122888 | tf_op jit(solution)/shard_map/ppermute | solution.py:546
  45.5 1.5 %collective-permute-start.14 = (f32[2,40,128]{2,1,0:T(8,128)S(1)}, f32[2,40,128]{2,1,0:T(8,128)S(1)}, u32[]{:S(2)}, u32[]{:S(2)}) collective-permute-start(f32[2,40,128]{2,1,0:T(8,128)S(1)} %pad_maximum_fusion.3), channel_id=1, source_target_pairs={{0,4},{1,5},{2,6},{3,7},{4,0},{5,1},{6,2},{7,3},{8,12},{9,13},{10,... | collective-permute-start | bytes 122888 | tf_op jit(solution)/shard_map/ppermute | solution.py:546
  47.2 1.2 %collective-permute-done.12.piece = f32[2,40,128]{2,1,0:T(8,128)S(1)} collective-permute-done((f32[2,40,128]{2,1,0:T(8,128)S(1)}, f32[2,40,128]{2,1,0:T(8,128)S(1)}, u32[]{:S(2)}, u32[]{:S(2)}) %collective-permute-start.12) | collective-permute-done | bytes 40992 | tf_op jit(solution)/shard_map/ppermute | solution.py:546
  49.0 0.5 %collective-permute-done.14.piece = f32[2,40,128]{2,1,0:T(8,128)S(1)} collective-permute-done((f32[2,40,128]{2,1,0:T(8,128)S(1)}, f32[2,40,128]{2,1,0:T(8,128)S(1)}, u32[]{:S(2)}, u32[]{:S(2)}) %collective-permute-start.14) | collective-permute-done | bytes 40992 | tf_op jit(solution)/shard_map/ppermute | solution.py:546
  50.0 1.0 %collective-permute-done.15 = f32[16,1024]{1,0:T(8,128)S(1)} collective-permute-done((f32[16,1024]{1,0:T(8,128)S(1)}, f32[16,1024]{1,0:T(8,128)S(1)}, u32[]{:S(2)}, u32[]{:S(2)}) %collective-permute-start.15) | collective-permute-done | bytes 65568 | tf_op jit(solution)/shard_map/ppermute | solution.py:546
  51.0 0.6 %add_bitcast_fusion = f32[1024,16]{0,1:T(8,128)} fusion(f32[16,1024]{1,0:T(8,128)S(1)} %shard_map.109, f32[16,1024]{1,0:T(8,128)S(1)} %collective-permute-done.15), kind=kLoop, calls=%fused_computation.4 | loop fusion | flops 16384 | bytes 196608 | tf_op jit(solution)/shard_map/transpose | solution.py:608
  (30 shorter events, 3.1 us)
Async XLA Ops:
  0.6 6.6 %collective-permute-start = (bf16[1,16,1024]{2,1,0:T(8,128)(2,1)}, bf16[1,16,1024]{2,1,0:T(8,128)(2,1)S(1)}, u32[]{:S(2)}, u32[]{:S(2)}) collective-permute-start(bf16[1,16,1024]{2,1,0:T(8,128)(2,1)} %bitcast.20), channel_id=1, source_target_pairs={{0,8},{1,9},{2,10},{3,11},{4,12},{5,13},{6,14},{7,15},{8,0},{9,1},... | collective-permute-start | bytes 98312 | tf_op jit(solution)/shard_map/ppermute | solution.py:546
  7.2 7.1 %collective-permute-start.3 = (bf16[2,16,1024]{2,1,0:T(8,128)(2,1)S(1)}, bf16[2,16,1024]{2,1,0:T(8,128)(2,1)S(1)}, u32[]{:S(2)}, u32[]{:S(2)}) collective-permute-start(bf16[2,16,1024]{2,1,0:T(8,128)(2,1)S(1)} %pad_maximum_fusion.2), channel_id=1, source_target_pairs={{0,2},{1,3},{2,0},{3,1},{4,6},{5,7},{6,4},{7,5},{8,10},{9,11},{10,... | collective-permute-start | bytes 196616 | tf_op jit(solution)/shard_map/ppermute | solution.py:546
  9.0 5.4 %collective-permute-start.2 = (bf16[2,16,1024]{2,1,0:T(8,128)(2,1)S(1)}, bf16[2,16,1024]{2,1,0:T(8,128)(2,1)S(1)}, u32[]{:S(2)}, u32[]{:S(2)}) collective-permute-start(bf16[2,16,1024]{2,1,0:T(8,128)(2,1)S(1)} %pad_maximum_fusion.2), channel_id=1, source_target_pairs={{0,6},{1,7},{2,4},{3,5},{4,2},{5,3},{6,0},{7,1},{8,14},{9,15},{10,... | collective-permute-start | bytes 196616 | tf_op jit(solution)/shard_map/ppermute | solution.py:546
  10.3 4.3 %collective-permute-start.1 = (bf16[2,16,1024]{2,1,0:T(8,128)(2,1)S(1)}, bf16[2,16,1024]{2,1,0:T(8,128)(2,1)S(1)}, u32[]{:S(2)}, u32[]{:S(2)}) collective-permute-start(bf16[2,16,1024]{2,1,0:T(8,128)(2,1)S(1)} %pad_maximum_fusion.2), channel_id=1, source_target_pairs={{0,4},{1,5},{2,6},{3,7},{4,0},{5,1},{6,2},{7,3},{8,12},{9,13},{10,... | collective-permute-start | bytes 196616 | tf_op jit(solution)/shard_map/ppermute | solution.py:546
  14.6 1.6 %collective-permute-start.4 = (bf16[8,16,1024]{2,1,0:T(8,128)(2,1)S(1)}, bf16[8,16,1024]{2,1,0:T(8,128)(2,1)S(1)}, u32[]{:S(2)}, u32[]{:S(2)}) collective-permute-start(bf16[8,16,1024]{2,1,0:T(8,128)(2,1)S(1)} %pad_maximum_fusion.coef_a), channel_id=1, source_target_pairs={{0,1},{1,0},{2,3},{3,2},{4,5},{5,4},{6,7},{7,6},{8,9},{9,8},{10,11... | collective-permute-start | bytes 786440 | tf_op jit(solution)/shard_map/ppermute | solution.py:546
  16.0 17.9 %copy-start = (f32[64]{0:T(128)S(1)}, f32[64]{0:T(128)}, u32[]{:S(2)}) copy-start(f32[64]{0:T(128)} %param.14) | copy-start | bytes 772
  18.6 1.3 %collective-permute-start.5 = (f32[136,128]{1,0:T(8,128)S(1)}, f32[136,128]{1,0:T(8,128)S(1)}, u32[]{:S(2)}, u32[]{:S(2)}) collective-permute-start(f32[136,128]{1,0:T(8,128)S(1)} %get-tuple-element.50), channel_id=1, source_target_pairs={{0,1},{1,0},{2,3},{3,2},{4,5},{5,4},{6,7},{7,6},{8,9},{9,8},{10,11... | collective-permute-start | bytes 208904 | tf_op jit(solution)/shard_map/ppermute | solution.py:546
  19.9 5.4 %collective-permute-start.8 = (f32[136,128]{1,0:T(8,128)S(1)}, f32[136,128]{1,0:T(8,128)S(1)}, u32[]{:S(2)}, u32[]{:S(2)}) collective-permute-start(f32[136,128]{1,0:T(8,128)S(1)} %add.18), channel_id=1, source_target_pairs={{0,6},{1,7},{2,4},{3,5},{4,2},{5,3},{6,0},{7,1},{8,14},{9,15},{10,... | collective-permute-start | bytes 208904 | tf_op jit(solution)/shard_map/ppermute | solution.py:546
  22.3 4.5 %collective-permute-start.7 = (f32[136,128]{1,0:T(8,128)S(1)}, f32[136,128]{1,0:T(8,128)S(1)}, u32[]{:S(2)}, u32[]{:S(2)}) collective-permute-start(f32[136,128]{1,0:T(8,128)S(1)} %add.18), channel_id=1, source_target_pairs={{0,2},{1,3},{2,0},{3,1},{4,6},{5,7},{6,4},{7,5},{8,10},{9,11},{10,... | collective-permute-start | bytes 208904 | tf_op jit(solution)/shard_map/ppermute | solution.py:546
  22.8 4.3 %collective-permute-start.6 = (f32[136,128]{1,0:T(8,128)S(1)}, f32[136,128]{1,0:T(8,128)S(1)}, u32[]{:S(2)}, u32[]{:S(2)}) collective-permute-start(f32[136,128]{1,0:T(8,128)S(1)} %add.18), channel_id=1, source_target_pairs={{0,4},{1,5},{2,6},{3,7},{4,0},{5,1},{6,2},{7,3},{8,12},{9,13},{10,... | collective-permute-start | bytes 208904 | tf_op jit(solution)/shard_map/ppermute | solution.py:546
  27.1 6.5 %collective-permute-start.9 = (f32[136,128]{1,0:T(8,128)S(1)}, f32[136,128]{1,0:T(8,128)S(1)}, u32[]{:S(2)}, u32[]{:S(2)}) collective-permute-start(f32[136,128]{1,0:T(8,128)S(1)} %add_add_fusion), channel_id=1, source_target_pairs={{0,8},{1,9},{2,10},{3,11},{4,12},{5,13},{6,14},{7,15},{8,0},{9,1},... | collective-permute-start | bytes 208904 | tf_op jit(solution)/shard_map/ppermute | solution.py:546
  33.6 1.3 %collective-permute-start.10 = (f32[136,128]{1,0:T(8,128)S(1)}, f32[136,128]{1,0:T(8,128)S(1)}, u32[]{:S(2)}, u32[]{:S(2)}) collective-permute-start(f32[136,128]{1,0:T(8,128)S(1)} %add.22.packed), channel_id=1, source_target_pairs={{0,1},{1,0},{2,3},{3,2},{4,5},{5,4},{6,7},{7,6},{8,9},{9,8},{10,11... | collective-permute-start | bytes 208904 | tf_op jit(solution)/shard_map/ppermute | solution.py:546
  38.6 4.9 %collective-permute-start.11 = (f32[1,40,128]{2,1,0:T(8,128)S(1)}, f32[1,40,128]{2,1,0:T(8,128)S(1)}, u32[]{:S(2)}, u32[]{:S(2)}) collective-permute-start(f32[1,40,128]{2,1,0:T(8,128)S(1)} %bitcast.11), channel_id=1, source_target_pairs={{0,8},{1,9},{2,10},{3,11},{4,12},{5,13},{6,14},{7,15},{8,0},{9,1},... | collective-permute-start | bytes 61448 | tf_op jit(solution)/shard_map/ppermute | solution.py:546
  43.5 4.9 %collective-permute-start.12 = (f32[2,40,128]{2,1,0:T(8,128)S(1)}, f32[2,40,128]{2,1,0:T(8,128)S(1)}, u32[]{:S(2)}, u32[]{:S(2)}) collective-permute-start(f32[2,40,128]{2,1,0:T(8,128)S(1)} %pad_maximum_fusion.3), channel_id=1, source_target_pairs={{0,6},{1,7},{2,4},{3,5},{4,2},{5,3},{6,0},{7,1},{8,14},{9,15},{10,... | collective-permute-start | bytes 122888 | tf_op jit(solution)/shard_map/ppermute | solution.py:546
  44.6 4.3 %collective-permute-start.13 = (f32[2,40,128]{2,1,0:T(8,128)S(1)}, f32[2,40,128]{2,1,0:T(8,128)S(1)}, u32[]{:S(2)}, u32[]{:S(2)}) collective-permute-start(f32[2,40,128]{2,1,0:T(8,128)S(1)} %pad_maximum_fusion.3), channel_id=1, source_target_pairs={{0,2},{1,3},{2,0},{3,1},{4,6},{5,7},{6,4},{7,5},{8,10},{9,11},{10,... | collective-permute-start | bytes 122888 | tf_op jit(solution)/shard_map/ppermute | solution.py:546
  45.5 4.0 %collective-permute-start.14 = (f32[2,40,128]{2,1,0:T(8,128)S(1)}, f32[2,40,128]{2,1,0:T(8,128)S(1)}, u32[]{:S(2)}, u32[]{:S(2)}) collective-permute-start(f32[2,40,128]{2,1,0:T(8,128)S(1)} %pad_maximum_fusion.3), channel_id=1, source_target_pairs={{0,4},{1,5},{2,6},{3,7},{4,0},{5,1},{6,2},{7,3},{8,12},{9,13},{10,... | collective-permute-start | bytes 122888 | tf_op jit(solution)/shard_map/ppermute | solution.py:546
  49.6 1.3 %collective-permute-start.15 = (f32[16,1024]{1,0:T(8,128)S(1)}, f32[16,1024]{1,0:T(8,128)S(1)}, u32[]{:S(2)}, u32[]{:S(2)}) collective-permute-start(f32[16,1024]{1,0:T(8,128)S(1)} %shard_map.113), channel_id=1, source_target_pairs={{0,1},{1,0},{2,3},{3,2},{4,5},{5,4},{6,7},{7,6},{8,9},{9,8},{10,11... | collective-permute-start | bytes 196616 | tf_op jit(solution)/shard_map/ppermute | solution.py:546
